TPU v7x, 1024 devices: a whole 4x4x32 slice. The times are simulated.
1024 devices in a mesh: expert: 32 (over y, z_lo), replica: 32 (over z_hi, x, core).
Axes of the slice: x: 4, y: 4, z: 32 (z_hi: 4, z_lo: 8; z = z_hi * 8 + z_lo), core: 2. Of those that a mesh axis runs over, the one named last changes fastest.
Arguments:
- grad_out: bfloat16 [8192, 4096], P('expert', 'replica'), may hold values from -6 to 6
- gate_prob: bfloat16 [8192], P('expert'), may hold values from 0.19921875 to 1
- routes: int32 [8192, 1], P('expert'), may hold values from 0 to 31; in each aligned block of 256 rows (0 to 255, 256 to 511, ...) at most 16 rows name the same one
- hidden_saved: bfloat16 [32, 32, 16, 6144], P('expert', None, None, 'replica'), may hold values from -0.75 to 0.75
- w_out: bfloat16 [32, 6144, 4096], P('expert', 'replica'), may hold values from -0.078125 to 0.078125
Outputs:
- grad_hidden: bfloat16 [32, 32, 16, 6144], P('expert', None, None, 'replica')
- grad_weight: bfloat16 [32, 6144, 4096], P('expert', 'replica')
- grad_gate: float32 [8192], P('expert')
Inputs may be any that keep to these rules, and one draw needn't show every extreme that they name: `routes`: among the 256 tokens of one device no expert is chosen more than 16 times, and in every draw some device chooses some expert exactly 16 times.
All inputs are finite; a program needn't handle non-finite values.
Results may differ from a plain program's by a relative error of at most 0.0049.
Values may be sent and summed in bfloat16 or wider, within the bound.
No kernel may reach another device: no remote copies, remote signals or barrier semaphores. Data moves between devices by JAX's collectives and lax.ppermute only.
A program may use at most 32 MiB of HBM per device.

v0:
```python
import jax
import jax.numpy as jnp
from jax import lax
from jax.sharding import PartitionSpec as P


def placing_table(routes, experts, slot_count):
    chosen = routes[:, 0]
    onehot = (chosen[:, None] == jnp.arange(experts, dtype=jnp.int32)[None, :]).astype(jnp.int32)
    position = jnp.sum((jnp.cumsum(onehot, axis=0) - 1) * onehot, axis=1)
    target = chosen * slot_count + position
    return jnp.arange(experts * slot_count, dtype=jnp.int32)[:, None] == target[None, :]


def per_device(grad_out, gate_prob, routes, hidden_saved, w_out):
    experts = lax.axis_size("expert")
    token_count = routes.shape[0]
    slot_count = 2 * token_count // experts
    slot_total = experts * slot_count
    placing = placing_table(routes, experts, slot_count)
    place_bf = placing.astype(jnp.bfloat16)
    place_f = placing.astype(jnp.float32)
    gate_slots = jnp.sum(place_f * gate_prob.astype(jnp.float32)[None, :], axis=1).astype(
        jnp.bfloat16
    )
    weight = w_out[0]
    hidden_width = weight.shape[0]
    saved = hidden_saved.reshape(slot_total, hidden_width)
    outgoing = jnp.dot(place_bf, grad_out, preferred_element_type=jnp.float32).astype(jnp.bfloat16)
    arrived, arrived_gate = (
        lax.all_to_all(
            outgoing.reshape(experts, slot_count, -1),
            "expert",
            split_axis=0,
            concat_axis=0,
            tiled=True,
        ),
        lax.all_to_all(
            gate_slots.reshape(experts, slot_count),
            "expert",
            split_axis=0,
            concat_axis=0,
            tiled=True,
        ),
    )
    feature_rows = arrived.reshape(slot_total, -1)
    gate_col = arrived_gate.reshape(slot_total, 1).astype(jnp.float32)
    piece = lax.all_gather(feature_rows, "replica", axis=1, tiled=True)
    running = lax.dot_general(
        piece, weight, (((1,), (1,)), ((), ())), preferred_element_type=jnp.float32
    )
    scaled_piece = (gate_col * piece.astype(jnp.float32)).astype(jnp.bfloat16)
    block = lax.dot_general(
        saved, scaled_piece, (((0,), (0,)), ((), ())), preferred_element_type=jnp.float32
    ).astype(jnp.bfloat16)
    grad_hidden = (gate_col * running).astype(jnp.bfloat16).reshape(hidden_saved.shape)
    partial_value = jnp.sum(running * saved.astype(jnp.float32), axis=1).reshape(
        experts, slot_count
    )
    summed = lax.psum(partial_value, "replica")
    returned = lax.all_to_all(summed, "expert", split_axis=0, concat_axis=0, tiled=True)
    grad_gate = jnp.sum(place_f * returned.reshape(slot_total, 1), axis=0)
    return (grad_hidden, block[None], grad_gate)


def solution(mesh):
    placed = (
        P("expert", "replica"),
        P("expert"),
        P("expert", None),
        P("expert", None, None, "replica"),
        P("expert", "replica", None),
    )
    return jax.shard_map(
        per_device,
        mesh=mesh,
        in_specs=placed,
        out_specs=(P("expert", None, None, "replica"), P("expert", "replica", None), P("expert")),
        check_vma=False,
    )
```

profile of v0, /device:TPU:8, one launch (start us, length us, event | category | flops | bytes accessed | tf_op | source)
XLA Modules:
  0.0 527.3 jit_solution(10749680428825963083)
XLA Ops:
  7.2 0.0 copy-start
  7.2 0.0 copy-start.2
  7.2 0.0 all-gather.2.cloned.1.call-start
  7.2 0.8 fusion.7
  8.0 0.6 reduce-window.6
  8.6 0.2 slice_reduce_fusion
  8.8 0.8 fusion.6
  9.6 0.7 multiply_add_fusion
  10.3 1.1 convolution_convert_fusion.1
  11.4 28.3 %all_to_all.20 = bf16[32,16,128]{2,1,0:T(8,128)(2,1)} all-to-all(bf16[32,16,128]{2,1,0:T(8,128)(2,1)S(1)} %bitcast.38), channel_id=1, replica_groups=mesh['expert'=32,'replica'=32] {'expert'}, dimensions={0} | all-to-all | bytes 262144 | tf_op jit(solution)/shard_map/all_to_all | solution.py:31
  39.7 0.0 all-gather.2.cloned.1.call-update
  39.7 1.1 copy.21
  40.8 0.0 copy-start.1
  40.8 178.8 %all-gather.2.cloned.1.call-done = bf16[512,4096]{1,0:T(8,128)(2,1)} async-done(((bf16[512,128]{1,0:T(8,128)(2,1)}), bf16[512,4096]{1,0:T(8,128)(2,1)}) %all-gather.2.cloned.1.call-update) | async-done | bytes 4194320 | tf_op jit(solution)/shard_map/all_gather | solution.py:48
  219.6 0.0 copy-done
  219.6 3.7 multiply_reduce_fusion
  223.3 0.1 all_to_all.15
  223.4 247.9 %psum.7 = f32[32,1,16]{2,0,1:T(8,128)} all-reduce(f32[32,1,16]{2,0,1:T(8,128)S(1)} %all_to_all.15), channel_id=1, replica_groups=mesh['expert'=32,'replica'=32] {'replica'}, use_global_device_ids=true, to_apply=%region_5.6 | all-reduce | flops 512 | bytes 4096 | tf_op jit(solution)/shard_map/psum | solution.py:60
  471.3 14.8 %all-to-all-start.2 = ((f32[32,1,16]{2,1,0:T(1,128)}), f32[32,1,16]{2,1,0:T(1,128)S(1)}, u32[]{:S(2)}, u32[]{:S(2)}) async-start(f32[32,1,16]{2,1,0:T(1,128)} %bitcast.10), calls=%async_computation.2 | async-start | bytes 32768 | tf_op jit(solution)/shard_map/all_to_all | solution.py:61
  486.2 0.0 copy-done.2
  486.2 11.2 %all-to-all-done.2 = f32[32,1,16]{2,1,0:T(1,128)S(1)} async-done(((f32[32,1,16]{2,1,0:T(1,128)}), f32[32,1,16]{2,1,0:T(1,128)S(1)}, u32[]{:S(2)}, u32[]{:S(2)}) %all-to-all-start.2) | async-done | bytes 2080 | tf_op jit(solution)/shard_map/all_to_all | solution.py:61
  497.4 0.5 broadcast.46
  497.9 0.7 reduce.9
  498.6 0.1 mul.60
  498.7 0.7 select_reduce_fusion
  499.4 0.1 convert_element_type.70
  499.5 15.4 %all_to_all.21 = bf16[32,1,16]{2,1,0:T(2,128)(2,1)S(1)} all-to-all(bf16[32,1,16]{2,1,0:T(2,128)(2,1)S(1)} %convert_element_type.70), channel_id=1, replica_groups=mesh['expert'=32,'replica'=32] {'expert'}, dimensions={0} | all-to-all | bytes 2048 | tf_op jit(solution)/shard_map/all_to_all | solution.py:38
  514.9 0.1 convert_reduce_fusion
  515.0 0.1 reshape.86
  515.1 0.8 copy.20
  516.0 0.0 copy-done.1
  516.0 4.5 fusion
  (4 shorter events, 0.1 us)
Async XLA Ops:
  7.2 212.4 %copy-start = (bf16[1,192,4096]{2,1,0:T(8,128)(2,1)S(1)}, bf16[1,192,4096]{2,1,0:T(8,128)(2,1)}, u32[]{:S(2)}) copy-start(bf16[1,192,4096]{2,1,0:T(8,128)(2,1)} %param.9) | copy-start | bytes 4718596
  7.2 479.0 %copy-start.2 = (bf16[256]{0:T(256)(128)(2,1)S(1)}, bf16[256]{0:T(256)(128)(2,1)}, u32[]{:S(2)}) copy-start(bf16[256]{0:T(256)(128)(2,1)} %param.6) | copy-start | bytes 1540
  7.2 212.4 %all-gather.2.cloned.1.call-start = ((), (), s32[]{:S(2)}) async-start(), calls=%async_computation.3 | async-start | bytes 4325376 | tf_op jit(solution)/shard_map/all_gather | solution.py:48
  40.8 475.2 %copy-start.1 = (bf16[1,32,16,192]{3,2,1,0:T(8,128)(2,1)S(1)}, bf16[1,32,16,192]{3,2,1,0:T(8,128)(2,1)}, u32[]{:S(2)}) copy-start(bf16[1,32,16,192]{3,2,1,0:T(8,128)(2,1)} %param.8) | copy-start | bytes 589828
  471.3 26.1 %all-to-all-start.2 = ((f32[32,1,16]{2,1,0:T(1,128)}), f32[32,1,16]{2,1,0:T(1,128)S(1)}, u32[]{:S(2)}, u32[]{:S(2)}) async-start(f32[32,1,16]{2,1,0:T(1,128)} %bitcast.10), calls=%async_computation.2 | async-start | bytes 32768 | tf_op jit(solution)/shard_map/all_to_all | solution.py:61
Sparse Core Ops, SparseCore 0:
  39.8 179.7 all-gather.1
where the time goes:
time: 528 us; the launch traced here: 527 us
  blocking collectives  292 us (55%)
  waiting for transfers between devices  190 us (36%)
  starting transfers between devices  14.9 us (3%)
  between operations  14.1 us (3%)
  matrix products  9.32 us (2%)
    psum x1, blocking collectives, per_device(): summed = lax.psum(partial_value, 'replica')  248 us
    all_gather x1, waiting for transfers between devices, per_device(): piece = lax.all_gather(feature_rows, 'replica', axis=1, tiled=True)  179 us
    all_to_all x1, blocking collectives, per_device(): lax.all_to_all(outgoing.reshape(experts, slot_count, -1), 'expert', split...  28.3 us
    all_to_all x1, blocking collectives, per_device(): lax.all_to_all(gate_slots.reshape(experts, slot_count), 'expert', split_a...  15.4 us
    all_to_all x1, starting transfers between devices, per_device(): lax.all_to_all(summed, 'expert', split_axis=0, concat_axis=0, tiled=True)  14.8 us
    all_to_all x1, waiting for transfers between devices, per_device(): lax.all_to_all(summed, 'expert', split_axis=0, concat_axis=0, tiled=True)  11.2 us
  transfers between devices with their start and end apart: 2, of which 2 were waited for; matrix products, arithmetic and copies ran while one was open for 0% of the time, Pallas kernels for 0%

commit v1 on v0

v1 whole, which is shorter than its diff:
```python
import itertools

import jax
import jax.numpy as jnp
from jax import lax
from jax.experimental import pallas as pl
from jax.experimental.pallas import tpu as pltpu
from jax.sharding import PartitionSpec as P

SIZES = dict(y=4, lo=8, hi=4, x=4, core=2)
BOTH = ("expert", "replica")


def groups(*free):
    fixed = [name for name in SIZES if name not in free]
    out = []
    for held in itertools.product(*[range(SIZES[name]) for name in fixed]):
        at = dict(zip(fixed, held))
        group = []
        for moved in itertools.product(*[range(SIZES[name]) for name in free]):
            at.update(zip(free, moved))
            expert = at["y"] * SIZES["lo"] + at["lo"]
            replica = (at["hi"] * SIZES["x"] + at["x"]) * SIZES["core"] + at["core"]
            group.append(expert * 32 + replica)
        out.append(group)
    return out


def slot_of_token(routes, experts, slot_count):
    chosen = routes[:, 0]
    onehot = (chosen[:, None] == jnp.arange(experts, dtype=jnp.int32)[None, :]).astype(jnp.int32)
    position = jnp.sum((jnp.cumsum(onehot, axis=0) - 1) * onehot, axis=1)
    return chosen * slot_count + position


def columns(block, core):
    return pl.ds(pl.multiple_of(block * 256 + core * 128, 128), 128)


def project_kernel(core_ref, own_ref, other_ref, w_ref, saved_ref, hidden_ref, partial_ref):
    core = core_ref[0]
    total = None
    for rows, side in ((own_ref, core), (other_ref, 1 - core)):
        for first in range(0, 16, 8):
            left = jnp.concatenate([rows[first + i] for i in range(8)], axis=1)
            right = jnp.concatenate(
                [w_ref[:, columns((i % 4) * 4 + i // 4, side)] for i in range(first, first + 8)],
                axis=1,
            )
            term = lax.dot_general(
                left, right, (((1,), (1,)), ((), ())), preferred_element_type=jnp.float32
            )
            total = term if total is None else total + term
    hidden_ref[...] = total.astype(jnp.bfloat16)
    partial_ref[...] = jnp.sum(total * saved_ref[...].astype(jnp.float32), axis=1, keepdims=True)


def weight_kernel(core_ref, own_ref, other_ref, saved_ref, out_ref):
    core = core_ref[0]
    left = saved_ref[...].T
    for rows, side in ((own_ref, core), (other_ref, 1 - core)):
        for i in range(16):
            out_ref[:, columns((i % 4) * 4 + i // 4, side)] = jnp.dot(
                left, rows[i], preferred_element_type=jnp.float32
            ).astype(jnp.bfloat16)


def per_device(grad_out, gate_prob, routes, hidden_saved, w_out):
    experts, slot_count = 32, 16
    slot_total = experts * slot_count
    target = slot_of_token(routes, experts, slot_count)
    placing = jnp.arange(slot_total, dtype=jnp.int32)[:, None] == target[None, :]
    gate = gate_prob.astype(jnp.float32)
    scaled = (gate[:, None] * grad_out.astype(jnp.float32)).astype(jnp.bfloat16)
    outgoing = jnp.dot(
        placing.astype(jnp.bfloat16), scaled, preferred_element_type=jnp.float32
    ).astype(jnp.bfloat16)
    weight = w_out[0]
    saved = hidden_saved.reshape(slot_total, -1)
    core = lax.rem(lax.axis_index("replica"), 2).astype(jnp.int32).reshape(1)

    arrived = lax.all_to_all(
        outgoing.reshape(experts, slot_count, -1), "expert", 0, 0, tiled=True
    ).reshape(slot_total, -1)
    over_hi = lax.all_gather(
        arrived, BOTH, axis=0, tiled=False, axis_index_groups=groups("hi")
    )
    own = lax.all_to_all(
        jnp.broadcast_to(over_hi[None], (4, *over_hi.shape)),
        BOTH, 0, 0, tiled=True, axis_index_groups=groups("x"),
    ).reshape(16, slot_total, -1)
    other = lax.ppermute(own, "replica", [(i, i ^ 1) for i in range(32)])

    smem = pl.BlockSpec(memory_space=pltpu.SMEM)
    vmem = pl.BlockSpec(memory_space=pltpu.VMEM)
    hidden_out, partial_value = pl.pallas_call(
        project_kernel,
        out_shape=(
            jax.ShapeDtypeStruct(saved.shape, jnp.bfloat16),
            jax.ShapeDtypeStruct((slot_total, 1), jnp.float32),
        ),
        in_specs=[smem, vmem, vmem, vmem, vmem],
        out_specs=(vmem, vmem),
        compiler_params=pltpu.CompilerParams(vmem_limit_bytes=40 * 1024 * 1024),
        cost_estimate=pl.CostEstimate(
            flops=2 * 512 * 4096 * 192, bytes_accessed=6 * 1024 * 1024, transcendentals=0
        ),
        name="project",
    )(core, own, other, weight, saved)
    weight_out = pl.pallas_call(
        weight_kernel,
        out_shape=jax.ShapeDtypeStruct(weight.shape, jnp.bfloat16),
        in_specs=[smem, vmem, vmem, vmem],
        out_specs=vmem,
        compiler_params=pltpu.CompilerParams(vmem_limit_bytes=40 * 1024 * 1024),
        cost_estimate=pl.CostEstimate(
            flops=2 * 512 * 4096 * 192, bytes_accessed=6 * 1024 * 1024, transcendentals=0
        ),
        name="weight",
    )(core, own, other, saved)

    to_z = partial_value.reshape(4, 8, 16).transpose(1, 0, 2).reshape(8, 64)
    from_z = lax.all_to_all(
        jnp.broadcast_to(to_z[None], (4, 8, 64)).reshape(32, 64),
        BOTH, 0, 0, tiled=True, axis_index_groups=groups("hi", "lo"),
    )
    to_plane = (
        jnp.sum(from_z.reshape(4, 8, 4, 16), axis=0).transpose(1, 0, 2).reshape(4, 1, 128)
    )
    from_plane = lax.all_to_all(
        jnp.broadcast_to(to_plane, (4, 8, 128)).reshape(32, 128),
        BOTH, 0, 0, tiled=True, axis_index_groups=groups("y", "x", "core"),
    )
    returned = jnp.sum(from_plane.reshape(4, 8, 128), axis=1).reshape(slot_total, 1)
    grad_gate = jnp.sum(jnp.where(placing, returned, 0.0), axis=0) / gate
    return (hidden_out.reshape(hidden_saved.shape), weight_out[None], grad_gate)


def solution(mesh):
    placed = (
        P("expert", "replica"),
        P("expert"),
        P("expert", None),
        P("expert", None, None, "replica"),
        P("expert", "replica", None),
    )
    return jax.shard_map(
        per_device,
        mesh=mesh,
        in_specs=placed,
        out_specs=(P("expert", None, None, "replica"), P("expert", "replica", None), P("expert")),
        check_vma=False,
    )
```

time: 528 us -> 183 us (0.35)
  the two profiles are of different devices: /device:TPU:8 before, /device:TPU:1 now
where the time goes in v1:
time: 183 us
  blocking collectives  147 us (80%)
  starting transfers between devices  11 us (6%)
  Pallas kernels  8.17 us (4%)
  waiting for transfers between devices  6.34 us (3%)
  other arithmetic  5.01 us (3%)
  local copies, waits for them, and re-layouts  3.48 us (2%)
    all_gather x1, blocking collectives, per_device(): lax.all_gather(arrived, BOTH, axis=0, tiled=False, axis_index_groups=grou...  56.1 us
    all_to_all x1, blocking collectives, per_device(): lax.all_to_all(jnp.broadcast_to(to_z[None], (4, 8, 64)).reshape(32, 64),...  35.6 us
    all_to_all x1, blocking collectives, per_device(): lax.all_to_all(outgoing.reshape(experts, slot_count, -1), 'expert', 0, 0,...  27.7 us
    all_to_all x1, blocking collectives, per_device(): lax.all_to_all(jnp.broadcast_to(over_hi[None], (4, *over_hi.shape)), BOTH...  27.3 us
    ppermute x1, starting transfers between devices, per_device(): other = lax.ppermute(own, 'replica', [(i, i ^ 1) for i in range(32)])  5.81 us
    all_to_all x1, starting transfers between devices, per_device(): lax.all_to_all(jnp.broadcast_to(to_plane, (4, 8, 128)).reshape(32, 128),...  5.23 us
    pallas_call x1, Pallas kernels, per_device(): pl.pallas_call(weight_kernel, out_shape=jax.ShapeDtypeStruct(weight.shape...  4.58 us
    ppermute x1, waiting for transfers between devices, per_device(): other = lax.ppermute(own, 'replica', [(i, i ^ 1) for i in range(32)])  3.89 us
  transfers between devices with their start and end apart: 2, of which 2 were waited for; matrix products, arithmetic and copies ran while one was open for 0% of the time, Pallas kernels for 3%

profile of v1, /device:TPU:1, one launch (start us, length us, event | category | flops | bytes accessed | tf_op | source)
XLA Modules:
  0.0 182.6 jit_solution(847635062315254434)
XLA Ops:
  0.6 0.7 fusion.4
  1.3 0.6 reduce-window.6
  1.9 0.2 slice_reduce_fusion
  2.1 0.8 fusion.3
  2.9 0.7 multiply_add_fusion
  3.6 0.7 convert_element_type.19
  4.2 1.1 convolution_convert_fusion
  5.4 27.7 %all_to_all.28 = bf16[32,16,128]{2,1,0:T(8,128)(2,1)S(1)} all-to-all(bf16[32,16,128]{2,1,0:T(8,128)(2,1)S(1)} %bitcast.41), channel_id=1, replica_groups=mesh['expert'=32,'replica'=32] {'expert'}, dimensions={0} | all-to-all | bytes 262144 | tf_op jit(solution)/shard_map/all_to_all | solution.py:82
  33.1 56.1 %all_gather.3 = bf16[4,512,128]{2,1,0:T(8,128)(2,1)S(1)} all-gather(bf16[1,512,128]{2,1,0:T(8,128)(2,1)S(1)} %bitcast.40), channel_id=1, replica_groups={{0,8,16,24},{1,9,17,25},{2,10,18,26},{3,11,19,27},{4,12,20,28},{5,13,21..., dimensions={0}, use_global_device_ids=true | all-gather | bytes 655360 | tf_op jit(solution)/shard_map/all_gather | solution.py:85
  89.1 0.4 broadcast_in_dim.41
  89.6 0.0 copy-start.1
  89.6 27.3 %all_to_all.29 = bf16[4,4,512,128]{3,2,1,0:T(8,128)(2,1)S(1)} all-to-all(bf16[4,4,512,128]{3,2,1,0:T(8,128)(2,1)S(1)} %broadcast_in_dim.41), channel_id=1, replica_groups={{0,2,4,6},{1,3,5,7},{8,10,12,14},{9,11,13,15},{16,18,20,22},{17,19,21,2..., dimensions={0} | all-to-all | bytes 4194304 | tf_op jit(solution)/shard_map/all_to_all | solution.py:88
  116.9 5.8 %collective-permute-start = (bf16[16,512,128]{2,1,0:T(8,128)(2,1)S(1)}, bf16[16,512,128]{2,1,0:T(8,128)(2,1)}, u32[]{:S(2)}, u32[]{:S(2)}) collective-permute-start(bf16[16,512,128]{2,1,0:T(8,128)(2,1)S(1)} %bitcast.33), channel_id=1, source_target_pairs={{0,1},{1,0},{2,3},{3,2},{4,5},{5,4},{6,7},{7,6},{8,9},{9,8},{10,11... | collective-permute-start | bytes 6291464 | tf_op jit(solution)/shard_map/ppermute | solution.py:92
  122.7 3.9 %collective-permute-done.other_ref = bf16[16,512,128]{2,1,0:T(8,128)(2,1)} collective-permute-done((bf16[16,512,128]{2,1,0:T(8,128)(2,1)S(1)}, bf16[16,512,128]{2,1,0:T(8,128)(2,1)}, u32[]{:S(2)}, u32[]{:S(2)}) %collective-permute-start) | collective-permute-done | bytes 2097184 | tf_op jit(solution)/shard_map/ppermute | solution.py:92
  126.6 0.0 copy-done.1
  126.6 0.0 copy-start
  126.6 1.4 copy-done
  128.0 3.6 %project.1 = (bf16[512,192]{1,0:T(8,128)(2,1)}, f32[512,1]{1,0:T(8,128)S(1)}) custom-call(s32[1]{0:T(128)} %bitcast.core_ref, bf16[16,512,128]{2,1,0:T(8,128)(2,1)S(1)} %bitcast.34, bf16[16,512,128]{2,1,0:T(8,128)(2,1)} %collective-permute-done.other_ref, bf16[192,4096]{1,0:T(8,128)(2,1)S(1)} %bitcast.36, bf16[512,192]{1,0:T(8,128)(2,1)S(1)} %bitcast.37), custom_call_target="tpu_custom_call" | custom-call | flops 805306368 | bytes 6291456 | tf_op jit(solution)/shard_map/project/pallas_call | solution.py:96
  131.6 0.1 reduce.1
  131.8 0.1 reshape.79
  131.9 0.1 broadcast_in_dim.43
  131.9 35.6 %all_to_all.30 = f32[32,1,64]{2,1,0:T(1,128)S(1)} all-to-all(f32[32,1,64]{2,1,0:T(1,128)S(1)} %bitcast.43), channel_id=1, replica_groups={{0,32,64,96,128,160,192,224,8,40,72,104,136,168,200,232,16,48,80,112,14..., dimensions={0} | all-to-all | bytes 16384 | tf_op jit(solution)/shard_map/all_to_all | solution.py:123
  167.5 0.5 broadcast.39
  168.0 0.7 reduce.6
  168.7 0.1 reshape.80
  168.9 0.1 broadcast_in_dim.45
  168.9 0.6 broadcast_in_dim.46
  169.5 5.2 %all-to-all-start.3 = ((f32[32,1,128]{2,1,0:T(1,128)}), f32[32,1,128]{2,1,0:T(1,128)S(1)}, u32[]{:S(2)}, u32[]{:S(2)}) async-start(f32[32,1,128]{2,1,0:T(1,128)} %bitcast.14), calls=%async_computation.3 | async-start | bytes 32768 | tf_op jit(solution)/shard_map/all_to_all | solution.py:130
  174.8 0.0 copy-start.2
  174.8 4.6 %weight.1 = bf16[192,4096]{1,0:T(8,128)(2,1)} custom-call(s32[1]{0:T(128)} %bitcast.core_ref, bf16[16,512,128]{2,1,0:T(8,128)(2,1)S(1)} %bitcast.35, bf16[16,512,128]{2,1,0:T(8,128)(2,1)} %collective-permute-done.other_ref, bf16[512,192]{1,0:T(8,128)(2,1)S(1)} %bitcast.38), custom_call_target="tpu_custom_call" | custom-call | flops 805306368 | bytes 6291456 | tf_op jit(solution)/shard_map/weight/pallas_call | solution.py:110
  179.4 2.5 %all-to-all-done.3 = f32[32,1,128]{2,1,0:T(1,128)S(1)} async-done(((f32[32,1,128]{2,1,0:T(1,128)}), f32[32,1,128]{2,1,0:T(1,128)S(1)}, u32[]{:S(2)}, u32[]{:S(2)}) %all-to-all-start.3) | async-done | bytes 16416 | tf_op jit(solution)/shard_map/all_to_all | solution.py:130
  181.8 0.2 select_reduce_fusion
  182.0 0.0 copy-done.2
  182.0 0.6 convert_divide_fusion
  (7 shorter events, 0.1 us)
Async XLA Ops:
  89.6 37.1 %copy-start.1 = (bf16[1,32,16,192]{3,2,1,0:T(8,128)(2,1)S(1)}, bf16[1,32,16,192]{3,2,1,0:T(8,128)(2,1)}, u32[]{:S(2)}) copy-start(bf16[1,32,16,192]{3,2,1,0:T(8,128)(2,1)} %param.8) | copy-start | bytes 589828
  116.9 9.7 %collective-permute-start = (bf16[16,512,128]{2,1,0:T(8,128)(2,1)S(1)}, bf16[16,512,128]{2,1,0:T(8,128)(2,1)}, u32[]{:S(2)}, u32[]{:S(2)}) collective-permute-start(bf16[16,512,128]{2,1,0:T(8,128)(2,1)S(1)} %bitcast.33), channel_id=1, source_target_pairs={{0,1},{1,0},{2,3},{3,2},{4,5},{5,4},{6,7},{7,6},{8,9},{9,8},{10,11... | collective-permute-start | bytes 6291464 | tf_op jit(solution)/shard_map/ppermute | solution.py:92
  126.6 1.4 copy-start
  169.5 12.3 %all-to-all-start.3 = ((f32[32,1,128]{2,1,0:T(1,128)}), f32[32,1,128]{2,1,0:T(1,128)S(1)}, u32[]{:S(2)}, u32[]{:S(2)}) async-start(f32[32,1,128]{2,1,0:T(1,128)} %bitcast.14), calls=%async_computation.3 | async-start | bytes 32768 | tf_op jit(solution)/shard_map/all_to_all | solution.py:130
  174.8 7.2 %copy-start.2 = (bf16[256]{0:T(256)(128)(2,1)S(1)}, bf16[256]{0:T(256)(128)(2,1)}, u32[]{:S(2)}) copy-start(bf16[256]{0:T(256)(128)(2,1)} %param.6) | copy-start | bytes 1540

commit v2 on v1

v2 whole, which is shorter than its diff:
```python
import itertools

import jax
import jax.numpy as jnp
from jax import lax
from jax.experimental import pallas as pl
from jax.experimental.pallas import tpu as pltpu
from jax.sharding import PartitionSpec as P

SIZES = dict(y=4, lo=8, hi=4, x=4, core=2)
BOTH = ("expert", "replica")


def groups(*free):
    fixed = [name for name in SIZES if name not in free]
    out = []
    for held in itertools.product(*[range(SIZES[name]) for name in fixed]):
        at = dict(zip(fixed, held))
        group = []
        for moved in itertools.product(*[range(SIZES[name]) for name in free]):
            at.update(zip(free, moved))
            expert = at["y"] * SIZES["lo"] + at["lo"]
            replica = (at["hi"] * SIZES["x"] + at["x"]) * SIZES["core"] + at["core"]
            group.append(expert * 32 + replica)
        out.append(group)
    return out


def slot_of_token(routes, experts, slot_count):
    chosen = routes[:, 0]
    onehot = (chosen[:, None] == jnp.arange(experts, dtype=jnp.int32)[None, :]).astype(jnp.int32)
    position = jnp.sum((jnp.cumsum(onehot, axis=0) - 1) * onehot, axis=1)
    return chosen * slot_count + position


def both_cores(at_ref, own_ref, other_ref):
    for rows, side in ((own_ref, at_ref[1]), (other_ref, 1 - at_ref[1])):
        for hi in range(4):
            yield rows[hi], pl.multiple_of(hi * 256 + side * 128, 128)


def project_kernel(at_ref, own_ref, other_ref, swap_ref, sums_ref, slots_ref):
    blocks = list(both_cores(at_ref, own_ref, other_ref))
    total = lax.dot_general(
        jnp.concatenate([swap_ref[:, pl.ds(first, 128)] for _, first in blocks], axis=1),
        jnp.concatenate([rows for rows, _ in blocks], axis=1),
        (((1,), (1,)), ((), ())),
        preferred_element_type=jnp.float32,
    )
    sums_ref[...] = total.astype(jnp.bfloat16)
    slots_ref[...] = jnp.sum(
        total * swap_ref[:, 1024:].astype(jnp.float32), axis=0, keepdims=True
    )


def weight_kernel(at_ref, own_ref, other_ref, swap_ref, sums_ref, *out_refs):
    for k in range(4):
        first_row = pl.multiple_of(lax.rem(at_ref[0] + k, 4) * 192, 64)
        left = swap_ref[pl.ds(first_row, 192), 1024:]
        out_refs[k][:, 1024:] = sums_ref[pl.ds(first_row, 192), :]
        for rows, first in both_cores(at_ref, own_ref, other_ref):
            out_refs[k][:, pl.ds(first, 128)] = jnp.dot(
                left, rows, preferred_element_type=jnp.float32
            ).astype(jnp.bfloat16)


def finish_kernel(at_ref, *refs):
    *in_refs, hidden_ref, weight_ref = refs
    total = None
    for k in range(4):
        source = lax.rem(at_ref[0] + 4 - k, 4)
        for hi in range(4):
            column = pl.multiple_of((hi * 4 + source) * 256, 256)
            weight_ref[:, pl.ds(column, 256)] = in_refs[k][:, hi * 256 : hi * 256 + 256]
        term = in_refs[k][:, 1024:].astype(jnp.float32)
        total = term if total is None else total + term
    hidden_ref[...] = total.T.astype(jnp.bfloat16)


def per_device(grad_out, gate_prob, routes, hidden_saved, w_out):
    experts, slot_count = 32, 16
    slot_total = experts * slot_count
    target = slot_of_token(routes, experts, slot_count)
    placing = jnp.arange(slot_total, dtype=jnp.int32)[:, None] == target[None, :]
    gate = gate_prob.astype(jnp.float32)
    scaled = (gate[:, None] * grad_out.astype(jnp.float32)).astype(jnp.bfloat16)
    outgoing = jnp.dot(
        placing.astype(jnp.bfloat16), scaled, preferred_element_type=jnp.float32
    ).astype(jnp.bfloat16)
    weight = w_out[0]
    saved = hidden_saved.reshape(slot_total, -1)
    replica = lax.axis_index("replica").astype(jnp.int32)
    at = jnp.stack([lax.rem(replica // 2, 4), lax.rem(replica, 2)])

    swap = jnp.concatenate(
        [
            weight.reshape(192, 4, 4, 256).transpose(2, 0, 1, 3).reshape(4, 192, 1024),
            jnp.broadcast_to(saved.T[None], (4, 192, 512)),
        ],
        axis=2,
    )
    swapped = lax.all_to_all(
        swap, BOTH, 0, 0, tiled=True, axis_index_groups=groups("x")
    ).reshape(768, 1536)

    arrived = lax.all_to_all(
        outgoing.reshape(experts, slot_count, -1), "expert", 0, 0, tiled=True
    ).reshape(slot_total, -1)
    own = lax.all_gather(arrived, BOTH, axis=0, tiled=False, axis_index_groups=groups("hi"))
    other = lax.ppermute(own, "replica", [(i, i ^ 1) for i in range(32)])

    smem = pl.BlockSpec(memory_space=pltpu.SMEM)
    vmem = pl.BlockSpec(memory_space=pltpu.VMEM)
    params = pltpu.CompilerParams(vmem_limit_bytes=40 * 1024 * 1024)
    cost = pl.CostEstimate(
        flops=2 * 512 * 4096 * 192, bytes_accessed=6 * 1024 * 1024, transcendentals=0
    )
    sums, partial_value = pl.pallas_call(
        project_kernel,
        out_shape=(
            jax.ShapeDtypeStruct((768, 512), jnp.bfloat16),
            jax.ShapeDtypeStruct((1, slot_total), jnp.float32),
        ),
        in_specs=[smem, vmem, vmem, vmem],
        out_specs=(vmem, vmem),
        compiler_params=params,
        cost_estimate=cost,
        name="project",
    )(at, own, other, swapped)
    chunks = pl.pallas_call(
        weight_kernel,
        out_shape=(jax.ShapeDtypeStruct((192, 1536), jnp.bfloat16),) * 4,
        in_specs=[smem, vmem, vmem, vmem, vmem],
        out_specs=(vmem,) * 4,
        compiler_params=params,
        cost_estimate=cost,
        name="weight",
    )(at, own, other, swapped, sums)
    from_plane = lax.all_to_all(
        jnp.broadcast_to(partial_value.reshape(4, 1, 128), (4, 8, 128)).reshape(32, 128),
        BOTH, 0, 0, tiled=True, axis_index_groups=groups("y", "x", "core"),
    )
    from_plane, chunks = lax.optimization_barrier((from_plane, chunks))
    received = [chunks[0]] + [
        lax.ppermute(
            chunks[k],
            "replica",
            [(i, i // 8 * 8 + (i % 8 // 2 + k) % 4 * 2 + i % 2) for i in range(32)],
        )
        for k in range(1, 4)
    ]
    hidden_out, weight_out = pl.pallas_call(
        finish_kernel,
        out_shape=(
            jax.ShapeDtypeStruct(saved.shape, jnp.bfloat16),
            jax.ShapeDtypeStruct(weight.shape, jnp.bfloat16),
        ),
        in_specs=[smem] + [vmem] * 4,
        out_specs=(vmem, vmem),
        compiler_params=params,
        cost_estimate=cost,
        name="finish",
    )(at, *received)

    to_z = jnp.sum(from_plane.reshape(4, 8, 8, 16), axis=1).transpose(1, 0, 2).reshape(8, 64)
    from_z = lax.all_to_all(
        jnp.broadcast_to(to_z[None], (4, 8, 64)).reshape(32, 64),
        BOTH, 0, 0, tiled=True, axis_index_groups=groups("hi", "lo"),
    )
    returned = (
        jnp.sum(from_z.reshape(4, 8, 4, 16), axis=0).transpose(1, 0, 2).reshape(slot_total, 1)
    )
    grad_gate = jnp.sum(jnp.where(placing, returned, 0.0), axis=0) / gate
    return (hidden_out.reshape(hidden_saved.shape), weight_out[None], grad_gate)


def solution(mesh):
    placed = (
        P("expert", "replica"),
        P("expert"),
        P("expert", None),
        P("expert", None, None, "replica"),
        P("expert", "replica", None),
    )
    return jax.shard_map(
        per_device,
        mesh=mesh,
        in_specs=placed,
        out_specs=(P("expert", None, None, "replica"), P("expert", "replica", None), P("expert")),
        check_vma=False,
    )
```

time: 183 us -> 168 us (0.918)
  blocking collectives: 147 us -> 88.7 us
  starting transfers between devices: 11 us -> 42.6 us
  local copies, waits for them, and re-layouts: 3.48 us -> 12.8 us
  Pallas kernels: 8.17 us -> 6.03 us
    all_to_all x2 -> x0, blocking collectives: 55 us -> none  [the longest x1 27.7 us: per_device(): lax.all_to_all(outgoing.reshape(experts, slot_count, -1), 'expert', 0, 0,...]
    all_to_all x1 -> x3, starting transfers between devices: 5.23 us -> 27.5 us  [the longest x1 16.1 us: per_device(): lax.all_to_all(outgoing.reshape(experts, slot_count, -1), 'expert', 0, 0,...]
    ppermute x0 -> x3, starting transfers between devices: none -> 10.6 us  [per_device(): lax.ppermute(chunks[k], 'replica', [(i, i // 8 * 8 + (i % 8 // 2 + k) % 4...]
    unnamed x6 -> x18, local copies, waits for them, and re-layouts: 1.42 us -> 6.35 us
    all_to_all x1, blocking collectives: 35.6 us -> 32.6 us  [per_device(): lax.all_to_all(jnp.broadcast_to(to_z[None], (4, 8, 64)).reshape(32, 64),...]
    all_to_all x1 -> x3, waiting for transfers between devices: 2.45 us -> 5.38 us  [the longest x1 5.33 us: per_device(): lax.all_to_all(outgoing.reshape(experts, slot_count, -1), 'expert', 0, 0,...]
    another operation x1 -> x2, local copies, waits for them, and re-layouts: 0.01 us -> 2.89 us  [the longest x1 2.89 us: per_device(): weight.reshape(192, 4, 4, 256).transpose(2, 0, 1, 3).reshape(4, 192, 1024)]
    ppermute x1, waiting for transfers between devices: 3.89 us -> 1.42 us  [per_device(): other = lax.ppermute(own, 'replica', [(i, i ^ 1) for i in range(32)])]
  transfers between devices with their start and end apart: 2 -> 7, of which waited for: 2 -> 2; matrix products, arithmetic and copies ran while one was open for 0% -> 5% of each run, Pallas kernels for 3% -> 1%
where the time goes in v2:
time: 168 us; the launch traced here: 166 us
  blocking collectives  88.7 us (53%)
  starting transfers between devices  42.6 us (25%)
  local copies, waits for them, and re-layouts  12.8 us (8%)
  waiting for transfers between devices  6.81 us (4%)
  other arithmetic  6.52 us (4%)
  Pallas kernels  6.03 us (4%)
  matrix products  1.81 us (1%)
    all_gather x1, blocking collectives, per_device(): lax.all_gather(arrived, BOTH, axis=0, tiled=False, axis_index_groups=grou...  56.1 us
    all_to_all x1, blocking collectives, per_device(): lax.all_to_all(jnp.broadcast_to(to_z[None], (4, 8, 64)).reshape(32, 64),...  32.6 us
    all_to_all x1, starting transfers between devices, per_device(): lax.all_to_all(outgoing.reshape(experts, slot_count, -1), 'expert', 0, 0,...  16.1 us
    ppermute x3, starting transfers between devices, per_device(): lax.ppermute(chunks[k], 'replica', [(i, i // 8 * 8 + (i % 8 // 2 + k) % 4...  10.6 us
    all_to_all x1, starting transfers between devices, per_device(): lax.all_to_all(jnp.broadcast_to(partial_value.reshape(4, 1, 128), (4, 8,...  7.41 us
    unnamed x18, local copies, waits for them, and re-layouts  6.35 us
    all_to_all x1, waiting for transfers between devices, per_device(): lax.all_to_all(outgoing.reshape(experts, slot_count, -1), 'expert', 0, 0,...  5.33 us
    ppermute x1, starting transfers between devices, per_device(): other = lax.ppermute(own, 'replica', [(i, i ^ 1) for i in range(32)])  4.42 us
  transfers between devices with their start and end apart: 7, of which 2 were waited for; matrix products, arithmetic and copies ran while one was open for 5% of the time, Pallas kernels for 1%

profile of v2, /device:TPU:1, one launch (start us, length us, event | category | flops | bytes accessed | tf_op | source)
XLA Modules:
  0.0 166.1 jit_solution(5647498801341738439)
XLA Ops:
  0.6 0.7 fusion.4
  1.3 0.6 reduce-window.6
  1.9 0.2 slice_reduce_fusion
  2.1 0.8 fusion.3
  2.9 0.7 multiply_add_fusion
  3.6 0.7 convert_element_type.19
  4.2 1.8 %convolution_convert_fusion = bf16[512,128]{1,0:T(8,128)(2,1)} fusion(s32[256]{0:T(256)S(1)} %multiply_add_fusion, bf16[256,128]{1,0:T(8,128)(2,1)} %param.5, f32[256]{0:T(256)S(1)} %convert_element_type.19), kind=kOutput, calls=%fused_computation.1 | convolution fusion | flops 33849344 | bytes 198656 | tf_op jit(solution)/shard_map/dot_general | solution.py:87
  6.0 16.1 %all-to-all-start = ((bf16[32,16,128]{2,1,0:T(8,128)(2,1)}), bf16[32,16,128]{2,1,0:T(8,128)(2,1)S(1)}, u32[]{:S(2)}, u32[]{:S(2)}) async-start(bf16[32,16,128]{2,1,0:T(8,128)(2,1)} %bitcast.5), calls=%async_computation | async-start | bytes 262144 | tf_op jit(solution)/shard_map/all_to_all | solution.py:106
  22.2 2.9 %reshape_squeeze.3 = bf16[192,4,4,256]{3,2,1,0:T(4,128)(2,1)S(1)} reshape(bf16[1,192,4096]{2,1,0:T(8,128)(2,1)} %param.9) | data formatting | bytes 3145728 | tf_op jit(solution)/shard_map/reshape;squeeze | solution.py:97
  25.0 0.6 copy.22
  25.7 0.0 copy-start.7
  25.7 1.1 reshape.71
  26.8 0.1 copy.23
  27.0 0.1 broadcast_in_dim.41
  27.0 1.6 pad_maximum_fusion
  28.6 5.3 %all-to-all-done = bf16[32,16,128]{2,1,0:T(8,128)(2,1)S(1)} async-done(((bf16[32,16,128]{2,1,0:T(8,128)(2,1)}), bf16[32,16,128]{2,1,0:T(8,128)(2,1)S(1)}, u32[]{:S(2)}, u32[]{:S(2)}) %all-to-all-start) | async-done | bytes 131104 | tf_op jit(solution)/shard_map/all_to_all | solution.py:106
  33.9 4.0 %all-to-all-start.1 = ((bf16[4,192,1536]{2,1,0:T(8,128)(2,1)}), bf16[4,192,1536]{2,1,0:T(8,128)(2,1)S(1)}, u32[]{:S(2)}, u32[]{:S(2)}) async-start(bf16[4,192,1536]{2,1,0:T(8,128)(2,1)} %pad_maximum_fusion), calls=%async_computation.1 | async-start | bytes 4718592 | tf_op jit(solution)/shard_map/all_to_all | solution.py:102
  37.9 56.1 %all_gather.3.own_ref = bf16[4,512,128]{2,1,0:T(8,128)(2,1)S(1)} all-gather(bf16[1,512,128]{2,1,0:T(8,128)(2,1)S(1)} %bitcast.38), channel_id=1, replica_groups={{0,8,16,24},{1,9,17,25},{2,10,18,26},{3,11,19,27},{4,12,20,28},{5,13,21..., dimensions={0}, use_global_device_ids=true | all-gather | bytes 655360 | tf_op jit(solution)/shard_map/all_gather | solution.py:109
  94.1 4.4 %collective-permute-start = (bf16[4,512,128]{2,1,0:T(8,128)(2,1)S(1)}, bf16[4,512,128]{2,1,0:T(8,128)(2,1)S(1)}, u32[]{:S(2)}, u32[]{:S(2)}) collective-permute-start(bf16[4,512,128]{2,1,0:T(8,128)(2,1)S(1)} %all_gather.3.own_ref), channel_id=1, source_target_pairs={{0,1},{1,0},{2,3},{3,2},{4,5},{5,4},{6,7},{7,6},{8,9},{9,8},{10,11... | collective-permute-start | bytes 1572872 | tf_op jit(solution)/shard_map/ppermute | solution.py:110
  98.5 0.1 pad_add_fusion.at_ref
  98.6 1.4 collective-permute-done.other_ref
  100.0 1.6 project.1
  101.6 0.0 copy-start
  101.6 0.9 copy-done
  102.4 0.6 broadcast_in_dim.43
  103.1 7.4 %all-to-all-start.2 = ((f32[32,1,128]{2,1,0:T(1,128)}), f32[32,1,128]{2,1,0:T(1,128)S(1)}, u32[]{:S(2)}, u32[]{:S(2)}) async-start(f32[32,1,128]{2,1,0:T(1,128)} %bitcast.12), calls=%async_computation.2 | async-start | bytes 32768 | tf_op jit(solution)/shard_map/all_to_all | solution.py:139
  110.5 1.1 copy-done.1
  111.6 2.4 %weight.1 = (bf16[192,1536]{1,0:T(8,128)(2,1)S(1)}, bf16[192,1536]{1,0:T(8,128)(2,1)S(1)}, bf16[192,1536]{1,0:T(8,128)(2,1)S(1)}, bf16[192,1536]{1,0:T(8,128)(2,1)S(1)}) custom-call(s32[2]{0:T(128)S(1)} %pad_add_fusion.at_ref, bf16[4,512,128]{2,1,0:T(8,128)(2,1)S(1)} %all_gather.3.own_ref, bf16[4,512,128]{2,1,0:T(8,128)(2,1)S(1)} %collective-permute-done.other_ref, ...), custom_call_target="tpu_custom_call" | custom-call | flops 805306368 | bytes 6291456 | tf_op jit(solution)/shard_map/weight/pallas_call | solution.py:130
  114.0 0.8 copy-done.2
  114.8 0.8 copy-done.4
  115.6 0.8 copy-done.5
  116.4 0.8 copy-done.6
  117.3 0.0 all-to-all-done.2
  117.3 3.2 %collective-permute-start.1 = (bf16[192,1536]{1,0:T(8,128)(2,1)}, bf16[192,1536]{1,0:T(8,128)(2,1)S(1)}, u32[]{:S(2)}, u32[]{:S(2)}) collective-permute-start(bf16[192,1536]{1,0:T(8,128)(2,1)} %copy-done.6), channel_id=1, source_target_pairs={{0,2},{1,3},{2,4},{3,5},{4,6},{5,7},{6,0},{7,1},{8,10},{9,11},{10,... | collective-permute-start | bytes 1769480 | tf_op jit(solution)/shard_map/ppermute | solution.py:145
  120.6 4.3 %collective-permute-start.2 = (bf16[192,1536]{1,0:T(8,128)(2,1)}, bf16[192,1536]{1,0:T(8,128)(2,1)S(1)}, u32[]{:S(2)}, u32[]{:S(2)}) collective-permute-start(bf16[192,1536]{1,0:T(8,128)(2,1)} %copy-done.5), channel_id=1, source_target_pairs={{0,4},{1,5},{2,6},{3,7},{4,0},{5,1},{6,2},{7,3},{8,12},{9,13},{10,... | collective-permute-start | bytes 1769480 | tf_op jit(solution)/shard_map/ppermute | solution.py:145
  124.9 3.1 %collective-permute-start.3 = (bf16[192,1536]{1,0:T(8,128)(2,1)}, bf16[192,1536]{1,0:T(8,128)(2,1)S(1)}, u32[]{:S(2)}, u32[]{:S(2)}) collective-permute-start(bf16[192,1536]{1,0:T(8,128)(2,1)} %copy-done.4), channel_id=1, source_target_pairs={{0,6},{1,7},{2,0},{3,1},{4,2},{5,3},{6,4},{7,5},{8,14},{9,15},{10,... | collective-permute-start | bytes 1769480 | tf_op jit(solution)/shard_map/ppermute | solution.py:145
  128.0 0.1 reshape.75
  128.1 0.1 broadcast_in_dim.45
  128.2 32.6 %all_to_all.31 = f32[32,1,64]{2,1,0:T(1,128)S(1)} all-to-all(f32[32,1,64]{2,1,0:T(1,128)S(1)} %bitcast.43), channel_id=1, replica_groups={{0,32,64,96,128,160,192,224,8,40,72,104,136,168,200,232,16,48,80,112,14..., dimensions={0} | all-to-all | bytes 16384 | tf_op jit(solution)/shard_map/all_to_all | solution.py:166
  160.8 0.5 broadcast.39
  161.3 0.7 reduce.5
  162.0 0.1 reshape.76
  162.1 0.1 broadcast_in_dim.47
  162.2 0.2 select_reduce_fusion
  162.4 0.6 convert_divide_fusion
  163.0 0.0 copy-start.3
  163.0 1.1 copy-done.3
  164.0 2.1 %finish.1 = (bf16[512,192]{1,0:T(8,128)(2,1)}, bf16[192,4096]{1,0:T(8,128)(2,1)}) custom-call(s32[2]{0:T(128)S(1)} %pad_add_fusion.at_ref, bf16[192,1536]{1,0:T(8,128)(2,1)S(1)} %copy-done.3, bf16[192,1536]{1,0:T(8,128)(2,1)S(1)} %collective-permute-done.1.refs_1_, bf16[192,1536]{1,0:T(8,128)(2,1)S(1)} %collective-permute-done.2.refs_2_, ...), custom_call_target="tpu_custom_call" | custom-call | flops 805306368 | bytes 6291456 | tf_op jit(solution)/shard_map/finish/pallas_call | solution.py:152
  (19 shorter events, 0.1 us)
Async XLA Ops:
  6.0 27.9 %all-to-all-start = ((bf16[32,16,128]{2,1,0:T(8,128)(2,1)}), bf16[32,16,128]{2,1,0:T(8,128)(2,1)S(1)}, u32[]{:S(2)}, u32[]{:S(2)}) async-start(bf16[32,16,128]{2,1,0:T(8,128)(2,1)} %bitcast.5), calls=%async_computation | async-start | bytes 262144 | tf_op jit(solution)/shard_map/all_to_all | solution.py:106
  25.7 1.2 copy-start.7
  33.9 66.1 %all-to-all-start.1 = ((bf16[4,192,1536]{2,1,0:T(8,128)(2,1)}), bf16[4,192,1536]{2,1,0:T(8,128)(2,1)S(1)}, u32[]{:S(2)}, u32[]{:S(2)}) async-start(bf16[4,192,1536]{2,1,0:T(8,128)(2,1)} %pad_maximum_fusion), calls=%async_computation.1 | async-start | bytes 4718592 | tf_op jit(solution)/shard_map/all_to_all | solution.py:102
  94.1 5.9 %collective-permute-start = (bf16[4,512,128]{2,1,0:T(8,128)(2,1)S(1)}, bf16[4,512,128]{2,1,0:T(8,128)(2,1)S(1)}, u32[]{:S(2)}, u32[]{:S(2)}) collective-permute-start(bf16[4,512,128]{2,1,0:T(8,128)(2,1)S(1)} %all_gather.3.own_ref), channel_id=1, source_target_pairs={{0,1},{1,0},{2,3},{3,2},{4,5},{5,4},{6,7},{7,6},{8,9},{9,8},{10,11... | collective-permute-start | bytes 1572872 | tf_op jit(solution)/shard_map/ppermute | solution.py:110
  101.6 0.9 copy-start
  103.1 14.3 %all-to-all-start.2 = ((f32[32,1,128]{2,1,0:T(1,128)}), f32[32,1,128]{2,1,0:T(1,128)S(1)}, u32[]{:S(2)}, u32[]{:S(2)}) async-start(f32[32,1,128]{2,1,0:T(1,128)} %bitcast.12), calls=%async_computation.2 | async-start | bytes 32768 | tf_op jit(solution)/shard_map/all_to_all | solution.py:139
  110.5 1.1 copy-start.1
  111.6 50.8 %copy-start.8 = (bf16[256]{0:T(256)(128)(2,1)S(1)}, bf16[256]{0:T(256)(128)(2,1)}, u32[]{:S(2)}) copy-start(bf16[256]{0:T(256)(128)(2,1)} %param.6) | copy-start | bytes 1540
  114.0 0.8 copy-start.2
  114.8 0.8 copy-start.4
  115.6 0.8 copy-start.5
  116.4 0.8 copy-start.6
  117.3 45.6 %collective-permute-start.1 = (bf16[192,1536]{1,0:T(8,128)(2,1)}, bf16[192,1536]{1,0:T(8,128)(2,1)S(1)}, u32[]{:S(2)}, u32[]{:S(2)}) collective-permute-start(bf16[192,1536]{1,0:T(8,128)(2,1)} %copy-done.6), channel_id=1, source_target_pairs={{0,2},{1,3},{2,4},{3,5},{4,6},{5,7},{6,0},{7,1},{8,10},{9,11},{10,... | collective-permute-start | bytes 1769480 | tf_op jit(solution)/shard_map/ppermute | solution.py:145
  120.6 42.4 %collective-permute-start.2 = (bf16[192,1536]{1,0:T(8,128)(2,1)}, bf16[192,1536]{1,0:T(8,128)(2,1)S(1)}, u32[]{:S(2)}, u32[]{:S(2)}) collective-permute-start(bf16[192,1536]{1,0:T(8,128)(2,1)} %copy-done.5), channel_id=1, source_target_pairs={{0,4},{1,5},{2,6},{3,7},{4,0},{5,1},{6,2},{7,3},{8,12},{9,13},{10,... | collective-permute-start | bytes 1769480 | tf_op jit(solution)/shard_map/ppermute | solution.py:145
  124.9 38.1 %collective-permute-start.3 = (bf16[192,1536]{1,0:T(8,128)(2,1)}, bf16[192,1536]{1,0:T(8,128)(2,1)S(1)}, u32[]{:S(2)}, u32[]{:S(2)}) collective-permute-start(bf16[192,1536]{1,0:T(8,128)(2,1)} %copy-done.4), channel_id=1, source_target_pairs={{0,6},{1,7},{2,0},{3,1},{4,2},{5,3},{6,4},{7,5},{8,14},{9,15},{10,... | collective-permute-start | bytes 1769480 | tf_op jit(solution)/shard_map/ppermute | solution.py:145
  163.0 1.1 copy-start.3

commit v3 on v2

v3 whole, which is shorter than its diff:
```python
import itertools

import jax
import jax.numpy as jnp
from jax import lax
from jax.experimental import pallas as pl
from jax.experimental.pallas import tpu as pltpu
from jax.sharding import PartitionSpec as P

SIZES = dict(y=4, lo=8, hi=4, x=4, core=2)
BOTH = ("expert", "replica")


def groups(*free):
    fixed = [name for name in SIZES if name not in free]
    out = []
    for held in itertools.product(*[range(SIZES[name]) for name in fixed]):
        at = dict(zip(fixed, held))
        group = []
        for moved in itertools.product(*[range(SIZES[name]) for name in free]):
            at.update(zip(free, moved))
            expert = at["y"] * SIZES["lo"] + at["lo"]
            replica = (at["hi"] * SIZES["x"] + at["x"]) * SIZES["core"] + at["core"]
            group.append(expert * 32 + replica)
        out.append(group)
    return out


def place_kernel(routes_ref, gate_ref, rows_ref, out_ref, target_ref):
    chosen = routes_ref[...]
    experts = lax.broadcasted_iota(jnp.int32, (32, 256), 0)
    onehot = jnp.where(experts == chosen, 1.0, 0.0)
    earlier = jnp.where(
        lax.broadcasted_iota(jnp.int32, (256, 256), 0)
        < lax.broadcasted_iota(jnp.int32, (256, 256), 1),
        1.0,
        0.0,
    ).astype(jnp.bfloat16)
    before = jnp.dot(onehot.astype(jnp.bfloat16), earlier, preferred_element_type=jnp.float32)
    position = jnp.sum(onehot * before, axis=0, keepdims=True).astype(jnp.int32)
    target = chosen * 16 + position
    target_ref[...] = target
    slots = lax.broadcasted_iota(jnp.int32, (512, 256), 0)
    placing = jnp.where(slots == target, gate_ref[...].astype(jnp.float32), 0.0)
    out_ref[...] = jnp.dot(
        placing.astype(jnp.bfloat16), rows_ref[...], preferred_element_type=jnp.float32
    ).astype(jnp.bfloat16)


def both_cores(at_ref, own_ref, other_ref):
    for rows, side in ((own_ref, at_ref[1]), (other_ref, 1 - at_ref[1])):
        for hi in range(4):
            yield rows[hi], pl.multiple_of(hi * 256 + side * 128, 128)


def product(left_ref, first_row, count, blocks):
    return lax.dot_general(
        jnp.concatenate(
            [left_ref[pl.ds(first_row, count), pl.ds(first, 128)] for _, first in blocks], axis=1
        ),
        jnp.concatenate([rows for rows, _ in blocks], axis=1),
        (((1,), (1,)), ((), ())),
        preferred_element_type=jnp.float32,
    )


def slots_kernel(at_ref, own_ref, other_ref, swap_ref, out_ref):
    blocks = list(both_cores(at_ref, own_ref, other_ref))
    total = product(swap_ref, 0, 768, blocks)
    sums = jnp.sum(total * swap_ref[:, 1024:].astype(jnp.float32), axis=0, keepdims=True)
    for y in range(4):
        for i in range(8):
            out_ref[y * 8 + i] = sums[:, y * 128 : y * 128 + 128]


def results_kernel(at_ref, own_ref, other_ref, swap_ref, *out_refs):
    blocks = list(both_cores(at_ref, own_ref, other_ref))
    for k in range(4):
        first_row = pl.multiple_of(lax.rem(at_ref[0] + k, 4) * 192, 64)
        left = swap_ref[pl.ds(first_row, 192), 1024:]
        out_refs[k][:, 1024:] = product(swap_ref, first_row, 192, blocks).astype(jnp.bfloat16)
        for rows, first in blocks:
            out_refs[k][:, pl.ds(first, 128)] = jnp.dot(
                left, rows, preferred_element_type=jnp.float32
            ).astype(jnp.bfloat16)


def gate_kernel(sums_ref, target_ref, gate_ref, out_ref):
    total = sums_ref[0:8, 0] + sums_ref[8:16, 0] + sums_ref[16:24, 0] + sums_ref[24:32, 0]
    columns = total.T
    target = target_ref[...]
    expert, slot = target // 16, target % 16
    place = expert // 8 * 16 + slot
    rows = lax.broadcasted_iota(jnp.int32, (64, 256), 0)
    found = jnp.zeros((64, 256), jnp.float32)
    for lo in range(8):
        hit = (rows == place) & (expert % 8 == lo)
        found = jnp.where(hit, columns[:, lo : lo + 1], found)
    out_ref[...] = jnp.sum(found, axis=0, keepdims=True) / gate_ref[...].astype(jnp.float32)


def finish_kernel(at_ref, *refs):
    *in_refs, hidden_ref, weight_ref = refs
    total = None
    for k in range(4):
        source = lax.rem(at_ref[0] + 4 - k, 4)
        for hi in range(4):
            column = pl.multiple_of((hi * 4 + source) * 256, 256)
            weight_ref[:, pl.ds(column, 256)] = in_refs[k][:, hi * 256 : hi * 256 + 256]
        term = in_refs[k][:, 1024:].astype(jnp.float32)
        total = term if total is None else total + term
    hidden_ref[...] = total.T.astype(jnp.bfloat16)


def per_device(grad_out, gate_prob, routes, hidden_saved, w_out):
    experts, slot_count, slot_total = 32, 16, 512
    smem = pl.BlockSpec(memory_space=pltpu.SMEM)
    vmem = pl.BlockSpec(memory_space=pltpu.VMEM)
    params = pltpu.CompilerParams(vmem_limit_bytes=40 * 1024 * 1024)
    cost = pl.CostEstimate(
        flops=2 * 512 * 4096 * 192, bytes_accessed=6 * 1024 * 1024, transcendentals=0
    )
    gate_row = gate_prob.reshape(1, 256)
    outgoing, target = pl.pallas_call(
        place_kernel,
        out_shape=(
            jax.ShapeDtypeStruct((slot_total, 128), jnp.bfloat16),
            jax.ShapeDtypeStruct((1, 256), jnp.int32),
        ),
        in_specs=[vmem] * 3,
        out_specs=(vmem,) * 2,
        compiler_params=params,
        name="place",
    )(routes.reshape(1, 256), gate_row, grad_out)
    weight = w_out[0]
    saved = hidden_saved.reshape(slot_total, -1)
    replica = lax.axis_index("replica").astype(jnp.int32)
    at = jnp.stack([lax.rem(replica // 2, 4), lax.rem(replica, 2)])

    swap = jnp.concatenate(
        [
            weight.reshape(192, 4, 4, 256).transpose(2, 0, 1, 3).reshape(4, 192, 1024),
            jnp.broadcast_to(saved.T[None], (4, 192, 512)),
        ],
        axis=2,
    )
    swapped = lax.all_to_all(
        swap, BOTH, 0, 0, tiled=True, axis_index_groups=groups("x")
    ).reshape(768, 1536)

    arrived = lax.all_to_all(
        outgoing.reshape(experts, slot_count, -1), "expert", 0, 0, tiled=True
    ).reshape(slot_total, -1)
    own = lax.all_gather(arrived, BOTH, axis=0, tiled=False, axis_index_groups=groups("hi"))
    other = lax.ppermute(own, "replica", [(i, i ^ 1) for i in range(32)])

    slot_sums = pl.pallas_call(
        slots_kernel,
        out_shape=jax.ShapeDtypeStruct((32, 1, 128), jnp.float32),
        in_specs=[smem, vmem, vmem, vmem],
        out_specs=vmem,
        compiler_params=params,
        cost_estimate=cost,
        name="slots",
    )(at, own, other, swapped)
    chunks = pl.pallas_call(
        results_kernel,
        out_shape=(jax.ShapeDtypeStruct((192, 1536), jnp.bfloat16),) * 4,
        in_specs=[smem, vmem, vmem, vmem],
        out_specs=(vmem,) * 4,
        compiler_params=params,
        cost_estimate=cost,
        name="results",
    )(at, own, other, swapped)
    from_plane = lax.all_to_all(
        slot_sums, BOTH, 0, 0, tiled=True, axis_index_groups=groups("y", "x", "core")
    )
    from_plane, chunks = lax.optimization_barrier((from_plane, chunks))
    received = [chunks[0]] + [
        lax.ppermute(
            chunks[k],
            "replica",
            [(i, i // 8 * 8 + (i % 8 // 2 + k) % 4 * 2 + i % 2) for i in range(32)],
        )
        for k in range(1, 4)
    ]
    hidden_out, weight_out = pl.pallas_call(
        finish_kernel,
        out_shape=(
            jax.ShapeDtypeStruct(saved.shape, jnp.bfloat16),
            jax.ShapeDtypeStruct(weight.shape, jnp.bfloat16),
        ),
        in_specs=[smem] + [vmem] * 4,
        out_specs=(vmem, vmem),
        compiler_params=params,
        cost_estimate=cost,
        name="finish",
    )(at, *received)
    to_z = jnp.sum(from_plane.reshape(4, 8, 8, 16), axis=1).transpose(1, 0, 2).reshape(8, 1, 64)
    from_z = lax.all_to_all(
        jnp.broadcast_to(to_z[None], (4, 8, 1, 64)).reshape(32, 1, 64),
        BOTH, 0, 0, tiled=True, axis_index_groups=groups("hi", "lo"),
    )
    from_z, hidden_out, weight_out = lax.optimization_barrier((from_z, hidden_out, weight_out))
    grad_gate = pl.pallas_call(
        gate_kernel,
        out_shape=jax.ShapeDtypeStruct((1, 256), jnp.float32),
        in_specs=[vmem] * 3,
        out_specs=vmem,
        compiler_params=params,
        name="gate",
    )(from_z, target, gate_row)
    return (hidden_out.reshape(hidden_saved.shape), weight_out[None], grad_gate.reshape(256))


def solution(mesh):
    placed = (
        P("expert", "replica"),
        P("expert"),
        P("expert", None),
        P("expert", None, None, "replica"),
        P("expert", "replica", None),
    )
    return jax.shard_map(
        per_device,
        mesh=mesh,
        in_specs=placed,
        out_specs=(P("expert", None, None, "replica"), P("expert", "replica", None), P("expert")),
        check_vma=False,
    )
```

time: 168 us -> 163 us (0.970)
  blocking collectives: 88.7 us -> 56 us
  waiting for transfers between devices: 6.81 us -> 24.7 us
  starting transfers between devices: 42.6 us -> 54.4 us
  other arithmetic: 6.52 us -> 2.37 us
  Pallas kernels: 6.03 us -> 9.86 us
  matrix products: 1.81 us -> 0 us
    all_to_all x1 -> x0, blocking collectives: 32.6 us -> none  [per_device(): lax.all_to_all(jnp.broadcast_to(to_z[None], (4, 8, 64)).reshape(32, 64),...]
    all_to_all x1 -> x2, starting transfers between devices: 7.41 us -> 19.1 us  [the longest x1 11.6 us: per_device(): lax.all_to_all(jnp.broadcast_to(to_z[None], (4, 8, 1, 64)).reshape(32, 1,...]
    all_to_all x1 -> x2, waiting for transfers between devices: 0.05 us -> 9.53 us  [the longest x1 9.53 us: per_device(): lax.all_to_all(jnp.broadcast_to(to_z[None], (4, 8, 1, 64)).reshape(32, 1,...]
    ppermute x3, waiting for transfers between devices: 0.01 us -> 8.47 us  [per_device(): lax.ppermute(chunks[k], 'replica', [(i, i // 8 * 8 + (i % 8 // 2 + k) % 4...]
    pallas_call x2 -> x4, Pallas kernels: 3.95 us -> 7.79 us  [the longest x1 3.73 us: per_device(): pl.pallas_call(results_kernel, out_shape=(jax.ShapeDtypeStruct((192, 1536...]
    dot_general x1 -> x0, matrix products: 1.81 us -> none  [per_device(): jnp.dot(placing.astype(jnp.bfloat16), scaled, preferred_element_type=jnp....]
    unnamed x18 -> x16, local copies, waits for them, and re-layouts: 6.35 us -> 5.88 us
  transfers between devices with their start and end apart: 7 -> 8, of which waited for: 2 -> 5; matrix products, arithmetic and copies ran while one was open for 5% -> 5% of each run, Pallas kernels for 1% -> 4%
where the time goes in v3:
time: 163 us; the launch traced here: 161 us
  blocking collectives  56 us (34%)
  starting transfers between devices  54.4 us (33%)
  waiting for transfers between devices  24.7 us (15%)
  local copies, waits for them, and re-layouts  12.6 us (8%)
  Pallas kernels  9.86 us (6%)
  other arithmetic  2.37 us (1%)
    all_gather x1, blocking collectives, per_device(): lax.all_gather(arrived, BOTH, axis=0, tiled=False, axis_index_groups=grou...  56 us
    all_to_all x1, starting transfers between devices, per_device(): lax.all_to_all(outgoing.reshape(experts, slot_count, -1), 'expert', 0, 0,...  16.1 us
    all_to_all x1, starting transfers between devices, per_device(): lax.all_to_all(jnp.broadcast_to(to_z[None], (4, 8, 1, 64)).reshape(32, 1,...  11.6 us
    ppermute x3, starting transfers between devices, per_device(): lax.ppermute(chunks[k], 'replica', [(i, i // 8 * 8 + (i % 8 // 2 + k) % 4...  10.7 us
    all_to_all x1, waiting for transfers between devices, per_device(): lax.all_to_all(jnp.broadcast_to(to_z[None], (4, 8, 1, 64)).reshape(32, 1,...  9.53 us
    ppermute x3, waiting for transfers between devices, per_device(): lax.ppermute(chunks[k], 'replica', [(i, i // 8 * 8 + (i % 8 // 2 + k) % 4...  8.47 us
    all_to_all x1, starting transfers between devices, per_device(): lax.all_to_all(slot_sums, BOTH, 0, 0, tiled=True, axis_index_groups=group...  7.55 us
    unnamed x16, local copies, waits for them, and re-layouts  5.88 us
  transfers between devices with their start and end apart: 8, of which 5 were waited for; matrix products, arithmetic and copies ran while one was open for 5% of the time, Pallas kernels for 4%

profile of v3, /device:TPU:1, one launch (start us, length us, event | category | flops | bytes accessed | tf_op | source)
XLA Modules:
  0.0 160.9 jit_solution(14446601122725644167)
XLA Ops:
  0.6 0.7 reshape.42.gate_ref
  1.3 0.0 copy-start
  1.3 0.8 copy-done
  2.1 0.0 copy-start.1
  2.1 0.7 copy-done.1
  2.8 1.0 place.1
  3.9 16.1 %all-to-all-start = ((bf16[32,16,128]{2,1,0:T(8,128)(2,1)}), bf16[32,16,128]{2,1,0:T(8,128)(2,1)S(1)}, u32[]{:S(2)}, u32[]{:S(2)}) async-start(bf16[32,16,128]{2,1,0:T(8,128)(2,1)} %bitcast.3), calls=%async_computation | async-start | bytes 262144 | tf_op jit(solution)/shard_map/all_to_all | solution.py:151
  20.0 2.9 %reshape_squeeze.3 = bf16[192,4,4,256]{3,2,1,0:T(4,128)(2,1)S(1)} reshape(bf16[1,192,4096]{2,1,0:T(8,128)(2,1)} %param.9) | data formatting | bytes 3145728 | tf_op jit(solution)/shard_map/reshape;squeeze | solution.py:142
  22.8 0.6 copy.12
  23.5 0.0 copy-start.7
  23.5 1.1 reshape.44
  24.6 0.0 copy-done.7
  24.6 0.1 copy.13
  24.8 0.1 broadcast_in_dim.18
  24.8 1.6 pad_maximum_fusion
  26.4 5.3 %all-to-all-done = bf16[32,16,128]{2,1,0:T(8,128)(2,1)S(1)} async-done(((bf16[32,16,128]{2,1,0:T(8,128)(2,1)}), bf16[32,16,128]{2,1,0:T(8,128)(2,1)S(1)}, u32[]{:S(2)}, u32[]{:S(2)}) %all-to-all-start) | async-done | bytes 131104 | tf_op jit(solution)/shard_map/all_to_all | solution.py:151
  31.7 4.0 %all-to-all-start.1 = ((bf16[4,192,1536]{2,1,0:T(8,128)(2,1)}), bf16[4,192,1536]{2,1,0:T(8,128)(2,1)S(1)}, u32[]{:S(2)}, u32[]{:S(2)}) async-start(bf16[4,192,1536]{2,1,0:T(8,128)(2,1)} %pad_maximum_fusion), calls=%async_computation.1 | async-start | bytes 4718592 | tf_op jit(solution)/shard_map/all_to_all | solution.py:147
  35.7 56.0 %all_gather.3.own_ref = bf16[4,512,128]{2,1,0:T(8,128)(2,1)S(1)} all-gather(bf16[1,512,128]{2,1,0:T(8,128)(2,1)S(1)} %bitcast.19), channel_id=1, replica_groups={{0,8,16,24},{1,9,17,25},{2,10,18,26},{3,11,19,27},{4,12,20,28},{5,13,21..., dimensions={0}, use_global_device_ids=true | all-gather | bytes 655360 | tf_op jit(solution)/shard_map/all_gather | solution.py:154
  91.8 4.5 %collective-permute-start = (bf16[4,512,128]{2,1,0:T(8,128)(2,1)S(1)}, bf16[4,512,128]{2,1,0:T(8,128)(2,1)S(1)}, u32[]{:S(2)}, u32[]{:S(2)}) collective-permute-start(bf16[4,512,128]{2,1,0:T(8,128)(2,1)S(1)} %all_gather.3.own_ref), channel_id=1, source_target_pairs={{0,1},{1,0},{2,3},{3,2},{4,5},{5,4},{6,7},{7,6},{8,9},{9,8},{10,11... | collective-permute-start | bytes 1572872 | tf_op jit(solution)/shard_map/ppermute | solution.py:155
  96.3 0.1 pad_add_fusion.at_ref
  96.4 1.4 collective-permute-done.other_ref
  97.8 0.0 all-to-all-done.1
  97.8 2.2 %slots.1 = f32[32,1,128]{2,1,0:T(1,128)} custom-call(s32[2]{0:T(128)S(1)} %pad_add_fusion.at_ref, bf16[4,512,128]{2,1,0:T(8,128)(2,1)S(1)} %all_gather.3.own_ref, bf16[4,512,128]{2,1,0:T(8,128)(2,1)S(1)} %collective-permute-done.other_ref, bf16[768,1536]{1,0:T(8,128)(2,1)S(1)} %bitcast.15), custom_call_target="tpu_custom_call" | custom-call | flops 805306368 | bytes 6291456 | tf_op jit(solution)/shard_map/slots/pallas_call | solution.py:157
  100.0 7.6 %all-to-all-start.2 = ((f32[32,1,128]{2,1,0:T(1,128)}), f32[32,1,128]{2,1,0:T(1,128)S(1)}, u32[]{:S(2)}, u32[]{:S(2)}) async-start(f32[32,1,128]{2,1,0:T(1,128)} %slots.1), calls=%async_computation.2 | async-start | bytes 32768 | tf_op jit(solution)/shard_map/all_to_all | solution.py:175
  107.5 3.7 %results.1 = (bf16[192,1536]{1,0:T(8,128)(2,1)S(1)}, bf16[192,1536]{1,0:T(8,128)(2,1)S(1)}, bf16[192,1536]{1,0:T(8,128)(2,1)S(1)}, bf16[192,1536]{1,0:T(8,128)(2,1)S(1)}) custom-call(s32[2]{0:T(128)S(1)} %pad_add_fusion.at_ref, bf16[4,512,128]{2,1,0:T(8,128)(2,1)S(1)} %all_gather.3.own_ref, bf16[4,512,128]{2,1,0:T(8,128)(2,1)S(1)} %collective-permute-done.other_ref, ...), custom_call_target="tpu_custom_call" | custom-call | flops 805306368 | bytes 6291456 | tf_op jit(solution)/shard_map/results/pallas_call | solution.py:166
  111.3 0.0 copy-start.2
  111.3 0.8 copy-done.2
  112.1 0.0 copy-start.4
  112.1 0.8 copy-done.4
  112.9 0.8 copy-done.5
  113.7 0.8 copy-done.6
  114.6 0.0 all-to-all-done.2
  114.6 3.3 %collective-permute-start.1 = (bf16[192,1536]{1,0:T(8,128)(2,1)}, bf16[192,1536]{1,0:T(8,128)(2,1)S(1)}, u32[]{:S(2)}, u32[]{:S(2)}) collective-permute-start(bf16[192,1536]{1,0:T(8,128)(2,1)} %copy-done.6), channel_id=1, source_target_pairs={{0,2},{1,3},{2,4},{3,5},{4,6},{5,7},{6,0},{7,1},{8,10},{9,11},{10,... | collective-permute-start | bytes 1769480 | tf_op jit(solution)/shard_map/ppermute | solution.py:180
  117.9 4.3 %collective-permute-start.2 = (bf16[192,1536]{1,0:T(8,128)(2,1)}, bf16[192,1536]{1,0:T(8,128)(2,1)S(1)}, u32[]{:S(2)}, u32[]{:S(2)}) collective-permute-start(bf16[192,1536]{1,0:T(8,128)(2,1)} %copy-done.5), channel_id=1, source_target_pairs={{0,4},{1,5},{2,6},{3,7},{4,0},{5,1},{6,2},{7,3},{8,12},{9,13},{10,... | collective-permute-start | bytes 1769480 | tf_op jit(solution)/shard_map/ppermute | solution.py:180
  122.2 3.1 %collective-permute-start.3 = (bf16[192,1536]{1,0:T(8,128)(2,1)}, bf16[192,1536]{1,0:T(8,128)(2,1)S(1)}, u32[]{:S(2)}, u32[]{:S(2)}) collective-permute-start(bf16[192,1536]{1,0:T(8,128)(2,1)} %copy-done.4), channel_id=1, source_target_pairs={{0,6},{1,7},{2,0},{3,1},{4,2},{5,3},{6,4},{7,5},{8,14},{9,15},{10,... | collective-permute-start | bytes 1769480 | tf_op jit(solution)/shard_map/ppermute | solution.py:180
  125.3 0.5 broadcast.9
  125.8 0.7 reduce.3
  126.5 0.1 reshape.47
  126.6 0.1 broadcast_in_dim.19
  126.7 0.6 broadcast_in_dim.20
  127.3 11.6 %all-to-all-start.3 = ((f32[32,1,64]{2,1,0:T(1,128)}), f32[32,1,64]{2,1,0:T(1,128)S(1)}, u32[]{:S(2)}, u32[]{:S(2)}) async-start(f32[32,1,64]{2,1,0:T(1,128)} %bitcast.10), calls=%async_computation.3 | async-start | bytes 32768 | tf_op jit(solution)/shard_map/all_to_all | solution.py:200
  138.9 0.0 collective-permute-done.1.refs_1_
  138.9 7.3 %collective-permute-done.2.refs_2_ = bf16[192,1536]{1,0:T(8,128)(2,1)S(1)} collective-permute-done((bf16[192,1536]{1,0:T(8,128)(2,1)}, bf16[192,1536]{1,0:T(8,128)(2,1)S(1)}, u32[]{:S(2)}, u32[]{:S(2)}) %collective-permute-start.2) | collective-permute-done | bytes 589856 | tf_op jit(solution)/shard_map/ppermute | solution.py:180
  146.2 1.2 collective-permute-done.3.refs_3_
  147.4 1.1 copy-done.3
  148.4 2.1 %finish.1 = (bf16[512,192]{1,0:T(8,128)(2,1)}, bf16[192,4096]{1,0:T(8,128)(2,1)}) custom-call(s32[2]{0:T(128)S(1)} %pad_add_fusion.at_ref, bf16[192,1536]{1,0:T(8,128)(2,1)S(1)} %copy-done.3, bf16[192,1536]{1,0:T(8,128)(2,1)S(1)} %collective-permute-done.1.refs_1_, bf16[192,1536]{1,0:T(8,128)(2,1)S(1)} %collective-permute-done.2.refs_2_, ...), custom_call_target="tpu_custom_call" | custom-call | flops 805306368 | bytes 6291456 | tf_op jit(solution)/shard_map/finish/pallas_call | solution.py:187
  150.5 9.5 %all-to-all-done.3.sums_ref = f32[32,1,64]{2,1,0:T(1,128)S(1)} async-done(((f32[32,1,64]{2,1,0:T(1,128)}), f32[32,1,64]{2,1,0:T(1,128)S(1)}, u32[]{:S(2)}, u32[]{:S(2)}) %all-to-all-start.3) | async-done | bytes 8224 | tf_op jit(solution)/shard_map/all_to_all | solution.py:200
  160.0 0.8 gate.1
  (5 shorter events, 0.0 us)
Async XLA Ops:
  1.3 0.8 copy-start
  2.1 0.7 copy-start.1
  3.9 27.9 %all-to-all-start = ((bf16[32,16,128]{2,1,0:T(8,128)(2,1)}), bf16[32,16,128]{2,1,0:T(8,128)(2,1)S(1)}, u32[]{:S(2)}, u32[]{:S(2)}) async-start(bf16[32,16,128]{2,1,0:T(8,128)(2,1)} %bitcast.3), calls=%async_computation | async-start | bytes 262144 | tf_op jit(solution)/shard_map/all_to_all | solution.py:151
  23.5 1.2 copy-start.7
  31.7 66.1 %all-to-all-start.1 = ((bf16[4,192,1536]{2,1,0:T(8,128)(2,1)}), bf16[4,192,1536]{2,1,0:T(8,128)(2,1)S(1)}, u32[]{:S(2)}, u32[]{:S(2)}) async-start(bf16[4,192,1536]{2,1,0:T(8,128)(2,1)} %pad_maximum_fusion), calls=%async_computation.1 | async-start | bytes 4718592 | tf_op jit(solution)/shard_map/all_to_all | solution.py:147
  91.8 6.0 %collective-permute-start = (bf16[4,512,128]{2,1,0:T(8,128)(2,1)S(1)}, bf16[4,512,128]{2,1,0:T(8,128)(2,1)S(1)}, u32[]{:S(2)}, u32[]{:S(2)}) collective-permute-start(bf16[4,512,128]{2,1,0:T(8,128)(2,1)S(1)} %all_gather.3.own_ref), channel_id=1, source_target_pairs={{0,1},{1,0},{2,3},{3,2},{4,5},{5,4},{6,7},{7,6},{8,9},{9,8},{10,11... | collective-permute-start | bytes 1572872 | tf_op jit(solution)/shard_map/ppermute | solution.py:155
  100.0 14.6 %all-to-all-start.2 = ((f32[32,1,128]{2,1,0:T(1,128)}), f32[32,1,128]{2,1,0:T(1,128)S(1)}, u32[]{:S(2)}, u32[]{:S(2)}) async-start(f32[32,1,128]{2,1,0:T(1,128)} %slots.1), calls=%async_computation.2 | async-start | bytes 32768 | tf_op jit(solution)/shard_map/all_to_all | solution.py:175
  111.3 0.8 copy-start.2
  112.1 0.8 copy-start.4
  112.9 0.8 copy-start.5
  113.7 0.8 copy-start.6
  114.6 24.3 %collective-permute-start.1 = (bf16[192,1536]{1,0:T(8,128)(2,1)}, bf16[192,1536]{1,0:T(8,128)(2,1)S(1)}, u32[]{:S(2)}, u32[]{:S(2)}) collective-permute-start(bf16[192,1536]{1,0:T(8,128)(2,1)} %copy-done.6), channel_id=1, source_target_pairs={{0,2},{1,3},{2,4},{3,5},{4,6},{5,7},{6,0},{7,1},{8,10},{9,11},{10,... | collective-permute-start | bytes 1769480 | tf_op jit(solution)/shard_map/ppermute | solution.py:180
  117.9 28.3 %collective-permute-start.2 = (bf16[192,1536]{1,0:T(8,128)(2,1)}, bf16[192,1536]{1,0:T(8,128)(2,1)S(1)}, u32[]{:S(2)}, u32[]{:S(2)}) collective-permute-start(bf16[192,1536]{1,0:T(8,128)(2,1)} %copy-done.5), channel_id=1, source_target_pairs={{0,4},{1,5},{2,6},{3,7},{4,0},{5,1},{6,2},{7,3},{8,12},{9,13},{10,... | collective-permute-start | bytes 1769480 | tf_op jit(solution)/shard_map/ppermute | solution.py:180
  122.2 25.2 %collective-permute-start.3 = (bf16[192,1536]{1,0:T(8,128)(2,1)}, bf16[192,1536]{1,0:T(8,128)(2,1)S(1)}, u32[]{:S(2)}, u32[]{:S(2)}) collective-permute-start(bf16[192,1536]{1,0:T(8,128)(2,1)} %copy-done.4), channel_id=1, source_target_pairs={{0,6},{1,7},{2,0},{3,1},{4,2},{5,3},{6,4},{7,5},{8,14},{9,15},{10,... | collective-permute-start | bytes 1769480 | tf_op jit(solution)/shard_map/ppermute | solution.py:180
  127.3 32.7 %all-to-all-start.3 = ((f32[32,1,64]{2,1,0:T(1,128)}), f32[32,1,64]{2,1,0:T(1,128)S(1)}, u32[]{:S(2)}, u32[]{:S(2)}) async-start(f32[32,1,64]{2,1,0:T(1,128)} %bitcast.10), calls=%async_computation.3 | async-start | bytes 32768 | tf_op jit(solution)/shard_map/all_to_all | solution.py:200
  147.4 1.1 copy-start.3

commit v4 on v3

--- a/solution.py
+++ b/solution.py
@@ -175,7 +175,9 @@
     from_plane = lax.all_to_all(
         slot_sums, BOTH, 0, 0, tiled=True, axis_index_groups=groups("y", "x", "core")
     )
-    from_plane, chunks = lax.optimization_barrier((from_plane, chunks))
+    to_z = jnp.sum(from_plane.reshape(4, 8, 8, 16), axis=1).transpose(1, 0, 2).reshape(8, 1, 64)
+    to_z = jnp.broadcast_to(to_z[None], (4, 8, 1, 64)).reshape(32, 1, 64)
+    to_z, chunks = lax.optimization_barrier((to_z, chunks))
     received = [chunks[0]] + [
         lax.ppermute(
             chunks[k],
@@ -193,21 +195,19 @@
         in_specs=[smem] + [vmem] * 4,
         out_specs=(vmem, vmem),
         compiler_params=params,
-        cost_estimate=cost,
+        cost_estimate=pl.CostEstimate(flops=1000, bytes_accessed=1000, transcendentals=0),
         name="finish",
     )(at, *received)
-    to_z = jnp.sum(from_plane.reshape(4, 8, 8, 16), axis=1).transpose(1, 0, 2).reshape(8, 1, 64)
     from_z = lax.all_to_all(
-        jnp.broadcast_to(to_z[None], (4, 8, 1, 64)).reshape(32, 1, 64),
-        BOTH, 0, 0, tiled=True, axis_index_groups=groups("hi", "lo"),
-    )
-    from_z, hidden_out, weight_out = lax.optimization_barrier((from_z, hidden_out, weight_out))
+        to_z, BOTH, 0, 0, tiled=True, axis_index_groups=groups("hi", "lo")
+    )
     grad_gate = pl.pallas_call(
         gate_kernel,
         out_shape=jax.ShapeDtypeStruct((1, 256), jnp.float32),
         in_specs=[vmem] * 3,
         out_specs=vmem,
         compiler_params=params,
+        cost_estimate=pl.CostEstimate(flops=int(2e10), bytes_accessed=1000, transcendentals=0),
         name="gate",
     )(from_z, target, gate_row)
     return (hidden_out.reshape(hidden_saved.shape), weight_out[None], grad_gate.reshape(256))

time: 163 us -> 165 us (1.012)
  waiting for transfers between devices: 24.7 us -> 28 us
    ppermute x3, waiting for transfers between devices: 8.47 us -> 10.8 us  [per_device(): lax.ppermute(chunks[k], 'replica', [(i, i // 8 * 8 + (i % 8 // 2 + k) % 4...]
  transfers between devices with their start and end apart: 8 -> 8, of which waited for: 5 -> 5; matrix products, arithmetic and copies ran while one was open for 5% -> 4% of each run, Pallas kernels for 4% -> 3%
where the time goes in v4:
time: 165 us; the launch traced here: 163 us
  blocking collectives  56 us (34%)
  starting transfers between devices  54.4 us (33%)
  waiting for transfers between devices  28 us (17%)
  local copies, waits for them, and re-layouts  11.6 us (7%)
  Pallas kernels  9.87 us (6%)
  other arithmetic  2.37 us (1%)
    all_gather x1, blocking collectives, per_device(): lax.all_gather(arrived, BOTH, axis=0, tiled=False, axis_index_groups=grou...  56 us
    all_to_all x1, starting transfers between devices, per_device(): lax.all_to_all(outgoing.reshape(experts, slot_count, -1), 'expert', 0, 0,...  16.1 us
    all_to_all x1, starting transfers between devices, per_device(): lax.all_to_all(to_z, BOTH, 0, 0, tiled=True, axis_index_groups=groups('hi...  11.6 us
    ppermute x3, waiting for transfers between devices, per_device(): lax.ppermute(chunks[k], 'replica', [(i, i // 8 * 8 + (i % 8 // 2 + k) % 4...  10.8 us
    ppermute x3, starting transfers between devices, per_device(): lax.ppermute(chunks[k], 'replica', [(i, i // 8 * 8 + (i % 8 // 2 + k) % 4...  10.7 us
    all_to_all x1, waiting for transfers between devices, per_device(): lax.all_to_all(to_z, BOTH, 0, 0, tiled=True, axis_index_groups=groups('hi...  10.5 us
    all_to_all x1, starting transfers between devices, per_device(): lax.all_to_all(slot_sums, BOTH, 0, 0, tiled=True, axis_index_groups=group...  7.55 us
    all_to_all x1, waiting for transfers between devices, per_device(): lax.all_to_all(outgoing.reshape(experts, slot_count, -1), 'expert', 0, 0,...  5.31 us
  transfers between devices with their start and end apart: 8, of which 5 were waited for; matrix products, arithmetic and copies ran while one was open for 4% of the time, Pallas kernels for 3%

profile of v4, /device:TPU:1, one launch (start us, length us, event | category | flops | bytes accessed | tf_op | source)
XLA Modules:
  0.0 163.0 jit_solution(13484559866937406223)
XLA Ops:
  0.6 0.7 reshape.42.gate_ref
  1.3 0.0 copy-start.2
  1.3 0.8 copy-done.2
  2.1 0.0 copy-start.3
  2.1 0.7 copy-done.3
  2.8 1.0 place.1
  3.9 16.1 %all-to-all-start = ((bf16[32,16,128]{2,1,0:T(8,128)(2,1)}), bf16[32,16,128]{2,1,0:T(8,128)(2,1)S(1)}, u32[]{:S(2)}, u32[]{:S(2)}) async-start(bf16[32,16,128]{2,1,0:T(8,128)(2,1)} %bitcast.3), calls=%async_computation | async-start | bytes 262144 | tf_op jit(solution)/shard_map/all_to_all | solution.py:151
  20.0 2.9 %reshape_squeeze.3 = bf16[192,4,4,256]{3,2,1,0:T(4,128)(2,1)S(1)} reshape(bf16[1,192,4096]{2,1,0:T(8,128)(2,1)} %param.9) | data formatting | bytes 3145728 | tf_op jit(solution)/shard_map/reshape;squeeze | solution.py:142
  22.8 0.6 copy.12
  23.5 0.0 copy-start.7
  23.5 1.1 reshape.44
  24.6 0.0 copy-done.7
  24.6 0.1 copy.13
  24.8 0.1 broadcast_in_dim.18
  24.8 1.6 pad_maximum_fusion
  26.4 5.3 %all-to-all-done = bf16[32,16,128]{2,1,0:T(8,128)(2,1)S(1)} async-done(((bf16[32,16,128]{2,1,0:T(8,128)(2,1)}), bf16[32,16,128]{2,1,0:T(8,128)(2,1)S(1)}, u32[]{:S(2)}, u32[]{:S(2)}) %all-to-all-start) | async-done | bytes 131104 | tf_op jit(solution)/shard_map/all_to_all | solution.py:151
  31.7 4.0 %all-to-all-start.1 = ((bf16[4,192,1536]{2,1,0:T(8,128)(2,1)}), bf16[4,192,1536]{2,1,0:T(8,128)(2,1)S(1)}, u32[]{:S(2)}, u32[]{:S(2)}) async-start(bf16[4,192,1536]{2,1,0:T(8,128)(2,1)} %pad_maximum_fusion), calls=%async_computation.1 | async-start | bytes 4718592 | tf_op jit(solution)/shard_map/all_to_all | solution.py:147
  35.7 56.0 %all_gather.3.own_ref = bf16[4,512,128]{2,1,0:T(8,128)(2,1)S(1)} all-gather(bf16[1,512,128]{2,1,0:T(8,128)(2,1)S(1)} %bitcast.19), channel_id=1, replica_groups={{0,8,16,24},{1,9,17,25},{2,10,18,26},{3,11,19,27},{4,12,20,28},{5,13,21..., dimensions={0}, use_global_device_ids=true | all-gather | bytes 655360 | tf_op jit(solution)/shard_map/all_gather | solution.py:154
  91.8 4.5 %collective-permute-start = (bf16[4,512,128]{2,1,0:T(8,128)(2,1)S(1)}, bf16[4,512,128]{2,1,0:T(8,128)(2,1)S(1)}, u32[]{:S(2)}, u32[]{:S(2)}) collective-permute-start(bf16[4,512,128]{2,1,0:T(8,128)(2,1)S(1)} %all_gather.3.own_ref), channel_id=1, source_target_pairs={{0,1},{1,0},{2,3},{3,2},{4,5},{5,4},{6,7},{7,6},{8,9},{9,8},{10,11... | collective-permute-start | bytes 1572872 | tf_op jit(solution)/shard_map/ppermute | solution.py:155
  96.3 0.1 pad_add_fusion.at_ref
  96.4 1.4 collective-permute-done.other_ref
  97.8 0.0 all-to-all-done.1
  97.8 2.2 %slots.1 = f32[32,1,128]{2,1,0:T(1,128)} custom-call(s32[2]{0:T(128)S(1)} %pad_add_fusion.at_ref, bf16[4,512,128]{2,1,0:T(8,128)(2,1)S(1)} %all_gather.3.own_ref, bf16[4,512,128]{2,1,0:T(8,128)(2,1)S(1)} %collective-permute-done.other_ref, bf16[768,1536]{1,0:T(8,128)(2,1)S(1)} %bitcast.15), custom_call_target="tpu_custom_call" | custom-call | flops 805306368 | bytes 6291456 | tf_op jit(solution)/shard_map/slots/pallas_call | solution.py:157
  100.0 7.6 %all-to-all-start.2 = ((f32[32,1,128]{2,1,0:T(1,128)}), f32[32,1,128]{2,1,0:T(1,128)S(1)}, u32[]{:S(2)}, u32[]{:S(2)}) async-start(f32[32,1,128]{2,1,0:T(1,128)} %slots.1), calls=%async_computation.2 | async-start | bytes 32768 | tf_op jit(solution)/shard_map/all_to_all | solution.py:175
  107.5 3.7 %results.1 = (bf16[192,1536]{1,0:T(8,128)(2,1)S(1)}, bf16[192,1536]{1,0:T(8,128)(2,1)S(1)}, bf16[192,1536]{1,0:T(8,128)(2,1)S(1)}, bf16[192,1536]{1,0:T(8,128)(2,1)S(1)}) custom-call(s32[2]{0:T(128)S(1)} %pad_add_fusion.at_ref, bf16[4,512,128]{2,1,0:T(8,128)(2,1)S(1)} %all_gather.3.own_ref, bf16[4,512,128]{2,1,0:T(8,128)(2,1)S(1)} %collective-permute-done.other_ref, ...), custom_call_target="tpu_custom_call" | custom-call | flops 805306368 | bytes 6291456 | tf_op jit(solution)/shard_map/results/pallas_call | solution.py:166
  111.3 0.0 copy-start
  111.3 0.8 copy-done
  112.1 0.0 copy-start.4
  112.1 0.8 copy-done.4
  112.9 0.8 copy-done.5
  113.7 0.8 copy-done.6
  114.6 0.0 all-to-all-done.2
  114.6 0.5 broadcast.9
  115.1 0.7 reduce.3
  115.8 0.1 reshape.47
  115.9 0.1 broadcast_in_dim.19
  116.0 0.6 broadcast_in_dim.20
  116.6 11.6 %all-to-all-start.3 = ((f32[32,1,64]{2,1,0:T(1,128)}), f32[32,1,64]{2,1,0:T(1,128)S(1)}, u32[]{:S(2)}, u32[]{:S(2)}) async-start(f32[32,1,64]{2,1,0:T(1,128)} %bitcast.10), calls=%async_computation.3 | async-start | bytes 32768 | tf_op jit(solution)/shard_map/all_to_all | solution.py:201
  128.2 3.3 %collective-permute-start.1 = (bf16[192,1536]{1,0:T(8,128)(2,1)}, bf16[192,1536]{1,0:T(8,128)(2,1)S(1)}, u32[]{:S(2)}, u32[]{:S(2)}) collective-permute-start(bf16[192,1536]{1,0:T(8,128)(2,1)} %copy-done.6), channel_id=1, source_target_pairs={{0,2},{1,3},{2,4},{3,5},{4,6},{5,7},{6,0},{7,1},{8,10},{9,11},{10,... | collective-permute-start | bytes 1769480 | tf_op jit(solution)/shard_map/ppermute | solution.py:182
  131.5 4.3 %collective-permute-start.2 = (bf16[192,1536]{1,0:T(8,128)(2,1)}, bf16[192,1536]{1,0:T(8,128)(2,1)S(1)}, u32[]{:S(2)}, u32[]{:S(2)}) collective-permute-start(bf16[192,1536]{1,0:T(8,128)(2,1)} %copy-done.5), channel_id=1, source_target_pairs={{0,4},{1,5},{2,6},{3,7},{4,0},{5,1},{6,2},{7,3},{8,12},{9,13},{10,... | collective-permute-start | bytes 1769480 | tf_op jit(solution)/shard_map/ppermute | solution.py:182
  135.8 3.1 %collective-permute-start.3 = (bf16[192,1536]{1,0:T(8,128)(2,1)}, bf16[192,1536]{1,0:T(8,128)(2,1)S(1)}, u32[]{:S(2)}, u32[]{:S(2)}) collective-permute-start(bf16[192,1536]{1,0:T(8,128)(2,1)} %copy-done.4), channel_id=1, source_target_pairs={{0,6},{1,7},{2,0},{3,1},{4,2},{5,3},{6,4},{7,5},{8,14},{9,15},{10,... | collective-permute-start | bytes 1769480 | tf_op jit(solution)/shard_map/ppermute | solution.py:182
  138.9 10.5 %all-to-all-done.3.sums_ref = f32[32,1,64]{2,1,0:T(1,128)S(1)} async-done(((f32[32,1,64]{2,1,0:T(1,128)}), f32[32,1,64]{2,1,0:T(1,128)S(1)}, u32[]{:S(2)}, u32[]{:S(2)}) %all-to-all-start.3) | async-done | bytes 8224 | tf_op jit(solution)/shard_map/all_to_all | solution.py:201
  149.4 0.8 gate.1
  150.2 0.0 collective-permute-done.1.refs_1_
  150.2 9.3 %collective-permute-done.2.refs_2_ = bf16[192,1536]{1,0:T(8,128)(2,1)S(1)} collective-permute-done((bf16[192,1536]{1,0:T(8,128)(2,1)}, bf16[192,1536]{1,0:T(8,128)(2,1)S(1)}, u32[]{:S(2)}, u32[]{:S(2)}) %collective-permute-start.2) | collective-permute-done | bytes 589856 | tf_op jit(solution)/shard_map/ppermute | solution.py:182
  159.5 1.5 collective-permute-done.3.refs_3_
  161.0 0.0 copy-done.1
  161.0 2.1 %finish.1 = (bf16[512,192]{1,0:T(8,128)(2,1)}, bf16[192,4096]{1,0:T(8,128)(2,1)}) custom-call(s32[2]{0:T(128)S(1)} %pad_add_fusion.at_ref, bf16[192,1536]{1,0:T(8,128)(2,1)S(1)} %copy-done.1, bf16[192,1536]{1,0:T(8,128)(2,1)S(1)} %collective-permute-done.1.refs_1_, bf16[192,1536]{1,0:T(8,128)(2,1)S(1)} %collective-permute-done.2.refs_2_, ...), custom_call_target="tpu_custom_call" | custom-call | flops 1000 | bytes 1000 | tf_op jit(solution)/shard_map/finish/pallas_call | solution.py:189
  (5 shorter events, 0.0 us)
Async XLA Ops:
  1.3 0.8 copy-start.2
  2.1 0.7 copy-start.3
  3.9 27.9 %all-to-all-start = ((bf16[32,16,128]{2,1,0:T(8,128)(2,1)}), bf16[32,16,128]{2,1,0:T(8,128)(2,1)S(1)}, u32[]{:S(2)}, u32[]{:S(2)}) async-start(bf16[32,16,128]{2,1,0:T(8,128)(2,1)} %bitcast.3), calls=%async_computation | async-start | bytes 262144 | tf_op jit(solution)/shard_map/all_to_all | solution.py:151
  23.5 1.2 copy-start.7
  31.7 66.1 %all-to-all-start.1 = ((bf16[4,192,1536]{2,1,0:T(8,128)(2,1)}), bf16[4,192,1536]{2,1,0:T(8,128)(2,1)S(1)}, u32[]{:S(2)}, u32[]{:S(2)}) async-start(bf16[4,192,1536]{2,1,0:T(8,128)(2,1)} %pad_maximum_fusion), calls=%async_computation.1 | async-start | bytes 4718592 | tf_op jit(solution)/shard_map/all_to_all | solution.py:147
  91.8 6.0 %collective-permute-start = (bf16[4,512,128]{2,1,0:T(8,128)(2,1)S(1)}, bf16[4,512,128]{2,1,0:T(8,128)(2,1)S(1)}, u32[]{:S(2)}, u32[]{:S(2)}) collective-permute-start(bf16[4,512,128]{2,1,0:T(8,128)(2,1)S(1)} %all_gather.3.own_ref), channel_id=1, source_target_pairs={{0,1},{1,0},{2,3},{3,2},{4,5},{5,4},{6,7},{7,6},{8,9},{9,8},{10,11... | collective-permute-start | bytes 1572872 | tf_op jit(solution)/shard_map/ppermute | solution.py:155
  100.0 14.6 %all-to-all-start.2 = ((f32[32,1,128]{2,1,0:T(1,128)}), f32[32,1,128]{2,1,0:T(1,128)S(1)}, u32[]{:S(2)}, u32[]{:S(2)}) async-start(f32[32,1,128]{2,1,0:T(1,128)} %slots.1), calls=%async_computation.2 | async-start | bytes 32768 | tf_op jit(solution)/shard_map/all_to_all | solution.py:175
  111.3 0.8 copy-start
  112.1 0.8 copy-start.4
  112.9 0.8 copy-start.5
  113.7 0.8 copy-start.6
  116.6 32.8 %all-to-all-start.3 = ((f32[32,1,64]{2,1,0:T(1,128)}), f32[32,1,64]{2,1,0:T(1,128)S(1)}, u32[]{:S(2)}, u32[]{:S(2)}) async-start(f32[32,1,64]{2,1,0:T(1,128)} %bitcast.10), calls=%async_computation.3 | async-start | bytes 32768 | tf_op jit(solution)/shard_map/all_to_all | solution.py:201
  128.2 22.0 %collective-permute-start.1 = (bf16[192,1536]{1,0:T(8,128)(2,1)}, bf16[192,1536]{1,0:T(8,128)(2,1)S(1)}, u32[]{:S(2)}, u32[]{:S(2)}) collective-permute-start(bf16[192,1536]{1,0:T(8,128)(2,1)} %copy-done.6), channel_id=1, source_target_pairs={{0,2},{1,3},{2,4},{3,5},{4,6},{5,7},{6,0},{7,1},{8,10},{9,11},{10,... | collective-permute-start | bytes 1769480 | tf_op jit(solution)/shard_map/ppermute | solution.py:182
  131.5 28.0 %collective-permute-start.2 = (bf16[192,1536]{1,0:T(8,128)(2,1)}, bf16[192,1536]{1,0:T(8,128)(2,1)S(1)}, u32[]{:S(2)}, u32[]{:S(2)}) collective-permute-start(bf16[192,1536]{1,0:T(8,128)(2,1)} %copy-done.5), channel_id=1, source_target_pairs={{0,4},{1,5},{2,6},{3,7},{4,0},{5,1},{6,2},{7,3},{8,12},{9,13},{10,... | collective-permute-start | bytes 1769480 | tf_op jit(solution)/shard_map/ppermute | solution.py:182
  135.8 25.2 %collective-permute-start.3 = (bf16[192,1536]{1,0:T(8,128)(2,1)}, bf16[192,1536]{1,0:T(8,128)(2,1)S(1)}, u32[]{:S(2)}, u32[]{:S(2)}) collective-permute-start(bf16[192,1536]{1,0:T(8,128)(2,1)} %copy-done.4), channel_id=1, source_target_pairs={{0,6},{1,7},{2,0},{3,1},{4,2},{5,3},{6,4},{7,5},{8,14},{9,15},{10,... | collective-permute-start | bytes 1769480 | tf_op jit(solution)/shard_map/ppermute | solution.py:182
  149.4 11.6 %copy-start.1 = (bf16[192,1536]{1,0:T(8,128)(2,1)S(1)}, bf16[192,1536]{1,0:T(8,128)(2,1)}, u32[]{:S(2)}) copy-start(bf16[192,1536]{1,0:T(8,128)(2,1)} %copy-done) | copy-start | bytes 1769476

commit v5 on v3

--- a/solution.py
+++ b/solution.py
@@ -73,20 +73,44 @@
             out_ref[y * 8 + i] = sums[:, y * 128 : y * 128 + 128]
 
 
-def results_kernel(at_ref, own_ref, other_ref, swap_ref, *out_refs):
-    blocks = list(both_cores(at_ref, own_ref, other_ref))
+def turn_kernel(sums_ref, out_ref):
+    rows = []
+    for y in range(4):
+        row = sums_ref[y * 8]
+        for i in range(1, 8):
+            row = row + sums_ref[y * 8 + i]
+        rows.append(row)
+    for lo in range(8):
+        line = jnp.concatenate([row[:, lo * 16 : lo * 16 + 16] for row in rows], axis=1)
+        for hi in range(4):
+            out_ref[hi * 8 + lo] = jnp.concatenate([line] * (1024 // 64), axis=1)
+
+
+def results_kernel(at_ref, w_ref, saved_ref, *refs):
+    own_refs, other_refs, (hidden_ref, weight_ref) = refs[:4], refs[4:8], refs[8:]
+    left = saved_ref[...].T
+    total = None
     for k in range(4):
-        first_row = pl.multiple_of(lax.rem(at_ref[0] + k, 4) * 192, 64)
-        left = swap_ref[pl.ds(first_row, 192), 1024:]
-        out_refs[k][:, 1024:] = product(swap_ref, first_row, 192, blocks).astype(jnp.bfloat16)
+        source = lax.rem(at_ref[0] + 4 - k, 4)
+        blocks = [
+            (rows, pl.multiple_of((hi * 4 + source) * 256 + side * 128, 128))
+            for hi in range(4)
+            for rows, side in (
+                (own_refs[k][hi], at_ref[1]),
+                (other_refs[k][hi], 1 - at_ref[1]),
+            )
+        ]
+        term = product(w_ref, 0, 192, blocks)
+        total = term if total is None else total + term
         for rows, first in blocks:
-            out_refs[k][:, pl.ds(first, 128)] = jnp.dot(
+            weight_ref[:, pl.ds(first, 128)] = jnp.dot(
                 left, rows, preferred_element_type=jnp.float32
             ).astype(jnp.bfloat16)
+    hidden_ref[...] = total.T.astype(jnp.bfloat16)
 
 
 def gate_kernel(sums_ref, target_ref, gate_ref, out_ref):
-    total = sums_ref[0:8, 0] + sums_ref[8:16, 0] + sums_ref[16:24, 0] + sums_ref[24:32, 0]
+    total = sum(sums_ref[hi * 8 : hi * 8 + 8, 0, :64] for hi in range(4))
     columns = total.T
     target = target_ref[...]
     expert, slot = target // 16, target % 16
@@ -99,19 +123,6 @@
     out_ref[...] = jnp.sum(found, axis=0, keepdims=True) / gate_ref[...].astype(jnp.float32)
 
 
-def finish_kernel(at_ref, *refs):
-    *in_refs, hidden_ref, weight_ref = refs
-    total = None
-    for k in range(4):
-        source = lax.rem(at_ref[0] + 4 - k, 4)
-        for hi in range(4):
-            column = pl.multiple_of((hi * 4 + source) * 256, 256)
-            weight_ref[:, pl.ds(column, 256)] = in_refs[k][:, hi * 256 : hi * 256 + 256]
-        term = in_refs[k][:, 1024:].astype(jnp.float32)
-        total = term if total is None else total + term
-    hidden_ref[...] = total.T.astype(jnp.bfloat16)
-
-
 def per_device(grad_out, gate_prob, routes, hidden_saved, w_out):
     experts, slot_count, slot_total = 32, 16, 512
     smem = pl.BlockSpec(memory_space=pltpu.SMEM)
@@ -163,44 +174,45 @@
         cost_estimate=cost,
         name="slots",
     )(at, own, other, swapped)
-    chunks = pl.pallas_call(
-        results_kernel,
-        out_shape=(jax.ShapeDtypeStruct((192, 1536), jnp.bfloat16),) * 4,
-        in_specs=[smem, vmem, vmem, vmem],
-        out_specs=(vmem,) * 4,
-        compiler_params=params,
-        cost_estimate=cost,
-        name="results",
-    )(at, own, other, swapped)
     from_plane = lax.all_to_all(
         slot_sums, BOTH, 0, 0, tiled=True, axis_index_groups=groups("y", "x", "core")
     )
-    from_plane, chunks = lax.optimization_barrier((from_plane, chunks))
-    received = [chunks[0]] + [
+    to_z = pl.pallas_call(
+        turn_kernel,
+        out_shape=jax.ShapeDtypeStruct((32, 1, 1024), jnp.float32),
+        in_specs=[vmem],
+        out_specs=vmem,
+        compiler_params=params,
+        cost_estimate=pl.CostEstimate(flops=int(1e+10), bytes_accessed=1000, transcendentals=0),
+        name="turn",
+    )(from_plane)
+    from_z = lax.all_to_all(
+        to_z, BOTH, 0, 0, tiled=True, axis_index_groups=groups("hi", "lo")
+    )
+    going, _ = lax.optimization_barrier((own, slot_sums))
+    own_rows = [own] + [
         lax.ppermute(
-            chunks[k],
+            going,
             "replica",
             [(i, i // 8 * 8 + (i % 8 // 2 + k) % 4 * 2 + i % 2) for i in range(32)],
         )
         for k in range(1, 4)
     ]
+    other_rows = [other] + [
+        lax.ppermute(rows, "replica", [(i, i ^ 1) for i in range(32)]) for rows in own_rows[1:]
+    ]
     hidden_out, weight_out = pl.pallas_call(
-        finish_kernel,
+        results_kernel,
         out_shape=(
             jax.ShapeDtypeStruct(saved.shape, jnp.bfloat16),
             jax.ShapeDtypeStruct(weight.shape, jnp.bfloat16),
         ),
-        in_specs=[smem] + [vmem] * 4,
+        in_specs=[smem] + [vmem] * 10,
         out_specs=(vmem, vmem),
         compiler_params=params,
-        cost_estimate=cost,
-        name="finish",
-    )(at, *received)
-    to_z = jnp.sum(from_plane.reshape(4, 8, 8, 16), axis=1).transpose(1, 0, 2).reshape(8, 1, 64)
-    from_z = lax.all_to_all(
-        jnp.broadcast_to(to_z[None], (4, 8, 1, 64)).reshape(32, 1, 64),
-        BOTH, 0, 0, tiled=True, axis_index_groups=groups("hi", "lo"),
-    )
+        cost_estimate=pl.CostEstimate(flops=int(1000), bytes_accessed=1000, transcendentals=0),
+        name="results",
+    )(at, weight, saved, *own_rows, *other_rows)
     from_z, hidden_out, weight_out = lax.optimization_barrier((from_z, hidden_out, weight_out))
     grad_gate = pl.pallas_call(
         gate_kernel,
@@ -208,6 +220,7 @@
         in_specs=[vmem] * 3,
         out_specs=vmem,
         compiler_params=params,
+        cost_estimate=pl.CostEstimate(flops=int(1000), bytes_accessed=1000, transcendentals=0),
         name="gate",
     )(from_z, target, gate_row)
     return (hidden_out.reshape(hidden_saved.shape), weight_out[None], grad_gate.reshape(256))

time: 163 us -> 168 us (1.031)
  starting transfers between devices: 54.4 us -> 77.4 us
  blocking collectives: 56 us -> 45.9 us
  waiting for transfers between devices: 24.7 us -> 17.5 us
    all_gather x1, blocking collectives: 56 us -> 45.9 us  [per_device(): lax.all_gather(arrived, BOTH, axis=0, tiled=False, axis_index_groups=grou...]
    ppermute x1, starting transfers between devices: 4.52 us -> 14.4 us  [per_device(): other = lax.ppermute(own, 'replica', [(i, i ^ 1) for i in range(32)])]
    ppermute x3 -> x6, starting transfers between devices: 10.7 us -> 18.5 us  [the longest x3 10.8 us: per_device(): lax.ppermute(going, 'replica', [(i, i // 8 * 8 + (i % 8 // 2 + k) % 4 * 2...]
    all_to_all x1, starting transfers between devices: 11.6 us -> 19.4 us  [per_device(): lax.all_to_all(to_z, BOTH, 0, 0, tiled=True, axis_index_groups=groups('hi...]
    ppermute x3 -> x6, waiting for transfers between devices: 8.47 us -> 1.72 us  [the longest x3 1.71 us: per_device(): lax.ppermute(rows, 'replica', [(i, i ^ 1) for i in range(32)])]
    all_to_all x1, waiting for transfers between devices: 5.31 us -> 0.34 us  [per_device(): lax.all_to_all(outgoing.reshape(experts, slot_count, -1), 'expert', 0, 0,...]
    all_to_all x1, waiting for transfers between devices: 9.53 us -> 14.1 us  [per_device(): lax.all_to_all(to_z, BOTH, 0, 0, tiled=True, axis_index_groups=groups('hi...]
    unnamed x16 -> x12, local copies, waits for them, and re-layouts: 5.88 us -> 2.19 us
  transfers between devices with their start and end apart: 8 -> 11, of which waited for: 5 -> 4; matrix products, arithmetic and copies ran while one was open for 5% -> 7% of each run, Pallas kernels for 4% -> 3%
where the time goes in v5:
time: 168 us; the launch traced here: 166 us
  starting transfers between devices  77.4 us (46%)
  blocking collectives  45.9 us (27%)
  waiting for transfers between devices  17.5 us (10%)
  local copies, waits for them, and re-layouts  11.2 us (7%)
  Pallas kernels  9.81 us (6%)
  other arithmetic  3.09 us (2%)
    all_gather x1, blocking collectives, per_device(): lax.all_gather(arrived, BOTH, axis=0, tiled=False, axis_index_groups=grou...  45.9 us
    all_to_all x1, starting transfers between devices, per_device(): lax.all_to_all(to_z, BOTH, 0, 0, tiled=True, axis_index_groups=groups('hi...  19.4 us
    all_to_all x1, starting transfers between devices, per_device(): lax.all_to_all(outgoing.reshape(experts, slot_count, -1), 'expert', 0, 0,...  16.1 us
    ppermute x1, starting transfers between devices, per_device(): other = lax.ppermute(own, 'replica', [(i, i ^ 1) for i in range(32)])  14.4 us
    all_to_all x1, waiting for transfers between devices, per_device(): lax.all_to_all(to_z, BOTH, 0, 0, tiled=True, axis_index_groups=groups('hi...  14.1 us
    ppermute x3, starting transfers between devices, per_device(): lax.ppermute(going, 'replica', [(i, i // 8 * 8 + (i % 8 // 2 + k) % 4 * 2...  10.8 us
    ppermute x3, starting transfers between devices, per_device(): lax.ppermute(rows, 'replica', [(i, i ^ 1) for i in range(32)])  7.72 us
    pallas_call x1, Pallas kernels, per_device(): pl.pallas_call(results_kernel, out_shape=(jax.ShapeDtypeStruct(saved.shap...  5.58 us
  transfers between devices with their start and end apart: 11, of which 4 were waited for; matrix products, arithmetic and copies ran while one was open for 7% of the time, Pallas kernels for 3%

profile of v5, /device:TPU:1, one launch (start us, length us, event | category | flops | bytes accessed | tf_op | source)
XLA Modules:
  0.0 165.9 jit_solution(1578206944124370087)
XLA Ops:
  0.6 0.7 reshape.32.gate_ref
  1.3 0.0 copy-start.4
  1.3 0.8 copy-done.4
  2.1 0.0 copy-start.5
  2.1 0.7 copy-done.5
  2.8 1.0 place.1
  3.9 16.1 %all-to-all-start = ((bf16[32,16,128]{2,1,0:T(8,128)(2,1)}), bf16[32,16,128]{2,1,0:T(8,128)(2,1)S(1)}, u32[]{:S(2)}, u32[]{:S(2)}) async-start(bf16[32,16,128]{2,1,0:T(8,128)(2,1)} %bitcast.3), calls=%async_computation | async-start | bytes 262144 | tf_op jit(solution)/shard_map/all_to_all | solution.py:162
  20.0 3.9 %reshape_squeeze.3 = bf16[192,4,4,256]{3,2,1,0:T(4,128)(2,1)} reshape(bf16[1,192,4096]{2,1,0:T(8,128)(2,1)} %param.9) | data formatting | bytes 3145728 | tf_op jit(solution)/shard_map/reshape;squeeze | solution.py:153
  23.8 2.0 %copy.10 = bf16[4,192,4,256]{3,2,1,0:T(4,128)(2,1)S(1)} copy(bf16[4,192,4,256]{3,0,2,1:T(4,128)(2,1)} %bitcast.19) | data formatting | bytes 3145728 | tf_op jit(solution)/shard_map/transpose | solution.py:153
  25.8 0.0 copy-start.1
  25.8 2.3 %reshape.34 = bf16[4,192,1024]{2,1,0:T(8,128)(2,1)} reshape(bf16[4,192,4,256]{3,2,1,0:T(4,128)(2,1)S(1)} %copy.10) | data formatting | bytes 3145728 | tf_op jit(solution)/shard_map/reshape | solution.py:153
  28.2 0.0 copy-done.1
  28.2 0.1 copy.11
  28.3 0.1 broadcast_in_dim.4
  28.4 3.0 %pad_maximum_fusion = bf16[4,192,1536]{2,1,0:T(8,128)(2,1)} fusion(bf16[4,192,512]{2,1,0:T(8,128)(2,1)S(1)} %broadcast_in_dim.4, bf16[4,192,1024]{2,1,0:T(8,128)(2,1)} %reshape.34), kind=kLoop, calls=%fused_computation | loop fusion | flops 4718592 | bytes 4718592 | tf_op jit(solution)/shard_map/concatenate | solution.py:151
  31.4 0.3 all-to-all-done
  31.7 4.0 %all-to-all-start.1 = ((bf16[4,192,1536]{2,1,0:T(8,128)(2,1)}), bf16[4,192,1536]{2,1,0:T(8,128)(2,1)S(1)}, u32[]{:S(2)}, u32[]{:S(2)}) async-start(bf16[4,192,1536]{2,1,0:T(8,128)(2,1)} %pad_maximum_fusion), calls=%async_computation.1 | async-start | bytes 4718592 | tf_op jit(solution)/shard_map/all_to_all | solution.py:158
  35.7 45.9 %all_gather.3.own_ref.refs_0_ = bf16[4,512,128]{2,1,0:T(8,128)(2,1)S(1)} all-gather(bf16[1,512,128]{2,1,0:T(8,128)(2,1)S(1)} %bitcast.20), channel_id=1, replica_groups={{0,8,16,24},{1,9,17,25},{2,10,18,26},{3,11,19,27},{4,12,20,28},{5,13,21..., dimensions={0}, use_global_device_ids=true | all-gather | bytes 655360 | tf_op jit(solution)/shard_map/all_gather | solution.py:165
  81.7 14.4 %collective-permute-start = (bf16[4,512,128]{2,1,0:T(8,128)(2,1)S(1)}, bf16[4,512,128]{2,1,0:T(8,128)(2,1)S(1)}, u32[]{:S(2)}, u32[]{:S(2)}) collective-permute-start(bf16[4,512,128]{2,1,0:T(8,128)(2,1)S(1)} %all_gather.3.own_ref.refs_0_), channel_id=1, source_target_pairs={{0,1},{1,0},{2,3},{3,2},{4,5},{5,4},{6,7},{7,6},{8,9},{9,8},{10,11... | collective-permute-start | bytes 1572872 | tf_op jit(solution)/shard_map/ppermute | solution.py:166
  96.1 0.1 pad_add_fusion.at_ref
  96.2 1.4 collective-permute-done.other_ref.refs_4_
  97.6 0.0 all-to-all-done.1
  97.6 2.2 %slots.1 = f32[32,1,128]{2,1,0:T(1,128)} custom-call(s32[2]{0:T(128)S(1)} %pad_add_fusion.at_ref, bf16[4,512,128]{2,1,0:T(8,128)(2,1)S(1)} %all_gather.3.own_ref.refs_0_, bf16[4,512,128]{2,1,0:T(8,128)(2,1)S(1)} %collective-permute-done.other_ref.refs_4_, bf16[768,1536]{1,0:T(8,128)(2,1)S(1)} %bitcast.14), custom_call_target="tpu_custom_call" | custom-call | flops 805306368 | bytes 6291456 | tf_op jit(solution)/shard_map/slots/pallas_call | solution.py:168
  99.8 5.0 %all-to-all-start.2 = ((f32[32,1,128]{2,1,0:T(1,128)}), f32[32,1,128]{2,1,0:T(1,128)S(1)}, u32[]{:S(2)}, u32[]{:S(2)}) async-start(f32[32,1,128]{2,1,0:T(1,128)} %slots.1), calls=%async_computation.2 | async-start | bytes 32768 | tf_op jit(solution)/shard_map/all_to_all | solution.py:177
  104.8 0.0 copy-start
  104.8 0.0 copy-start.2
  104.8 3.4 %collective-permute-start.1 = (bf16[4,512,128]{2,1,0:T(8,128)(2,1)S(1)}, bf16[4,512,128]{2,1,0:T(8,128)(2,1)S(1)}, u32[]{:S(2)}, u32[]{:S(2)}) collective-permute-start(bf16[4,512,128]{2,1,0:T(8,128)(2,1)S(1)} %all_gather.3.own_ref.refs_0_), channel_id=1, source_target_pairs={{0,2},{1,3},{2,4},{3,5},{4,6},{5,7},{6,0},{7,1},{8,10},{9,11},{10,... | collective-permute-start | bytes 1572872 | tf_op jit(solution)/shard_map/ppermute | solution.py:194
  108.3 4.3 %collective-permute-start.2 = (bf16[4,512,128]{2,1,0:T(8,128)(2,1)S(1)}, bf16[4,512,128]{2,1,0:T(8,128)(2,1)}, u32[]{:S(2)}, u32[]{:S(2)}) collective-permute-start(bf16[4,512,128]{2,1,0:T(8,128)(2,1)S(1)} %all_gather.3.own_ref.refs_0_), channel_id=1, source_target_pairs={{0,4},{1,5},{2,6},{3,7},{4,0},{5,1},{6,2},{7,3},{8,12},{9,13},{10,... | collective-permute-start | bytes 1572872 | tf_op jit(solution)/shard_map/ppermute | solution.py:194
  112.6 3.1 %collective-permute-start.3 = (bf16[4,512,128]{2,1,0:T(8,128)(2,1)S(1)}, bf16[4,512,128]{2,1,0:T(8,128)(2,1)}, u32[]{:S(2)}, u32[]{:S(2)}) collective-permute-start(bf16[4,512,128]{2,1,0:T(8,128)(2,1)S(1)} %all_gather.3.own_ref.refs_0_), channel_id=1, source_target_pairs={{0,6},{1,7},{2,0},{3,1},{4,2},{5,3},{6,4},{7,5},{8,14},{9,15},{10,... | collective-permute-start | bytes 1572872 | tf_op jit(solution)/shard_map/ppermute | solution.py:194
  115.7 0.0 all-to-all-done.2.sums_ref
  115.7 0.2 turn.1
  115.9 0.0 copy-start.3
  115.9 0.7 copy-done.3
  116.5 19.4 %all-to-all-start.3 = ((f32[32,1,1024]{2,1,0:T(1,128)}), f32[32,1,1024]{2,1,0:T(1,128)S(1)}, u32[]{:S(2)}, u32[]{:S(2)}) async-start(f32[32,1,1024]{2,1,0:T(1,128)} %copy-done.3), calls=%async_computation.3 | async-start | bytes 262144 | tf_op jit(solution)/shard_map/all_to_all | solution.py:189
  135.9 0.0 collective-permute-done.1.refs_1_
  135.9 3.4 %collective-permute-start.4 = (bf16[4,512,128]{2,1,0:T(8,128)(2,1)S(1)}, bf16[4,512,128]{2,1,0:T(8,128)(2,1)S(1)}, u32[]{:S(2)}, u32[]{:S(2)}) collective-permute-start(bf16[4,512,128]{2,1,0:T(8,128)(2,1)S(1)} %collective-permute-done.1.refs_1_), channel_id=1, source_target_pairs={{0,1},{1,0},{2,3},{3,2},{4,5},{5,4},{6,7},{7,6},{8,9},{9,8},{10,11... | collective-permute-start | bytes 1572872 | tf_op jit(solution)/shard_map/ppermute | solution.py:202
  139.3 0.0 collective-permute-done.2.refs_2_
  139.3 1.9 %collective-permute-start.5 = (bf16[4,512,128]{2,1,0:T(8,128)(2,1)}, bf16[4,512,128]{2,1,0:T(8,128)(2,1)S(1)}, u32[]{:S(2)}, u32[]{:S(2)}) collective-permute-start(bf16[4,512,128]{2,1,0:T(8,128)(2,1)} %collective-permute-done.2.refs_2_), channel_id=1, source_target_pairs={{0,1},{1,0},{2,3},{3,2},{4,5},{5,4},{6,7},{7,6},{8,9},{9,8},{10,11... | collective-permute-start | bytes 1572872 | tf_op jit(solution)/shard_map/ppermute | solution.py:202
  141.2 0.0 collective-permute-done.3.refs_3_
  141.3 2.4 %collective-permute-start.6 = (bf16[4,512,128]{2,1,0:T(8,128)(2,1)}, bf16[4,512,128]{2,1,0:T(8,128)(2,1)S(1)}, u32[]{:S(2)}, u32[]{:S(2)}) collective-permute-start(bf16[4,512,128]{2,1,0:T(8,128)(2,1)} %collective-permute-done.3.refs_3_), channel_id=1, source_target_pairs={{0,1},{1,0},{2,3},{3,2},{4,5},{5,4},{6,7},{7,6},{8,9},{9,8},{10,11... | collective-permute-start | bytes 1572872 | tf_op jit(solution)/shard_map/ppermute | solution.py:202
  143.7 0.0 collective-permute-done.4.refs_5_
  143.7 0.0 collective-permute-done.5.refs_6_
  143.7 1.7 %collective-permute-done.6.refs_7_ = bf16[4,512,128]{2,1,0:T(8,128)(2,1)S(1)} collective-permute-done((bf16[4,512,128]{2,1,0:T(8,128)(2,1)}, bf16[4,512,128]{2,1,0:T(8,128)(2,1)S(1)}, u32[]{:S(2)}, u32[]{:S(2)}) %collective-permute-start.6) | collective-permute-done | bytes 524320 | tf_op jit(solution)/shard_map/ppermute | solution.py:202
  145.4 0.0 copy-done
  145.4 0.0 copy-done.2
  145.4 5.6 %results.1 = (bf16[512,192]{1,0:T(8,128)(2,1)}, bf16[192,4096]{1,0:T(8,128)(2,1)}) custom-call(s32[2]{0:T(128)S(1)} %pad_add_fusion.at_ref, bf16[192,4096]{1,0:T(8,128)(2,1)S(1)} %bitcast.15, bf16[512,192]{1,0:T(8,128)(2,1)S(1)} %bitcast.17, bf16[4,512,128]{2,1,0:T(8,128)(2,1)S(1)} %all_gather.3.own_ref.refs_0_, ...), custom_call_target="tpu_custom_call" | custom-call | flops 1000 | bytes 1000 | tf_op jit(solution)/shard_map/results/pallas_call | solution.py:204
  151.0 14.1 %all-to-all-done.3.sums_ref = f32[32,1,1024]{2,1,0:T(1,128)S(1)} async-done(((f32[32,1,1024]{2,1,0:T(1,128)}), f32[32,1,1024]{2,1,0:T(1,128)S(1)}, u32[]{:S(2)}, u32[]{:S(2)}) %all-to-all-start.3) | async-done | bytes 131104 | tf_op jit(solution)/shard_map/all_to_all | solution.py:189
  165.0 0.8 gate.1
Async XLA Ops:
  1.3 0.8 copy-start.4
  2.1 0.7 copy-start.5
  3.9 27.9 %all-to-all-start = ((bf16[32,16,128]{2,1,0:T(8,128)(2,1)}), bf16[32,16,128]{2,1,0:T(8,128)(2,1)S(1)}, u32[]{:S(2)}, u32[]{:S(2)}) async-start(bf16[32,16,128]{2,1,0:T(8,128)(2,1)} %bitcast.3), calls=%async_computation | async-start | bytes 262144 | tf_op jit(solution)/shard_map/all_to_all | solution.py:162
  25.8 2.3 %copy-start.1 = (bf16[1,32,16,192]{3,2,1,0:T(8,128)(2,1)S(1)}, bf16[1,32,16,192]{3,2,1,0:T(8,128)(2,1)}, u32[]{:S(2)}) copy-start(bf16[1,32,16,192]{3,2,1,0:T(8,128)(2,1)} %param.8) | copy-start | bytes 589828
  31.7 65.9 %all-to-all-start.1 = ((bf16[4,192,1536]{2,1,0:T(8,128)(2,1)}), bf16[4,192,1536]{2,1,0:T(8,128)(2,1)S(1)}, u32[]{:S(2)}, u32[]{:S(2)}) async-start(bf16[4,192,1536]{2,1,0:T(8,128)(2,1)} %pad_maximum_fusion), calls=%async_computation.1 | async-start | bytes 4718592 | tf_op jit(solution)/shard_map/all_to_all | solution.py:158
  81.7 15.9 %collective-permute-start = (bf16[4,512,128]{2,1,0:T(8,128)(2,1)S(1)}, bf16[4,512,128]{2,1,0:T(8,128)(2,1)S(1)}, u32[]{:S(2)}, u32[]{:S(2)}) collective-permute-start(bf16[4,512,128]{2,1,0:T(8,128)(2,1)S(1)} %all_gather.3.own_ref.refs_0_), channel_id=1, source_target_pairs={{0,1},{1,0},{2,3},{3,2},{4,5},{5,4},{6,7},{7,6},{8,9},{9,8},{10,11... | collective-permute-start | bytes 1572872 | tf_op jit(solution)/shard_map/ppermute | solution.py:166
  99.8 15.9 %all-to-all-start.2 = ((f32[32,1,128]{2,1,0:T(1,128)}), f32[32,1,128]{2,1,0:T(1,128)S(1)}, u32[]{:S(2)}, u32[]{:S(2)}) async-start(f32[32,1,128]{2,1,0:T(1,128)} %slots.1), calls=%async_computation.2 | async-start | bytes 32768 | tf_op jit(solution)/shard_map/all_to_all | solution.py:177
  104.8 40.6 %copy-start = (bf16[1,192,4096]{2,1,0:T(8,128)(2,1)S(1)}, bf16[1,192,4096]{2,1,0:T(8,128)(2,1)}, u32[]{:S(2)}) copy-start(bf16[1,192,4096]{2,1,0:T(8,128)(2,1)} %param.9) | copy-start | bytes 4718596
  104.8 40.6 %copy-start.2 = (bf16[1,32,16,192]{3,2,1,0:T(8,128)(2,1)S(1)}, bf16[1,32,16,192]{3,2,1,0:T(8,128)(2,1)}, u32[]{:S(2)}) copy-start(bf16[1,32,16,192]{3,2,1,0:T(8,128)(2,1)} %param.8) | copy-start | bytes 589828
  104.8 31.1 %collective-permute-start.1 = (bf16[4,512,128]{2,1,0:T(8,128)(2,1)S(1)}, bf16[4,512,128]{2,1,0:T(8,128)(2,1)S(1)}, u32[]{:S(2)}, u32[]{:S(2)}) collective-permute-start(bf16[4,512,128]{2,1,0:T(8,128)(2,1)S(1)} %all_gather.3.own_ref.refs_0_), channel_id=1, source_target_pairs={{0,2},{1,3},{2,4},{3,5},{4,6},{5,7},{6,0},{7,1},{8,10},{9,11},{10,... | collective-permute-start | bytes 1572872 | tf_op jit(solution)/shard_map/ppermute | solution.py:194
  108.3 31.0 %collective-permute-start.2 = (bf16[4,512,128]{2,1,0:T(8,128)(2,1)S(1)}, bf16[4,512,128]{2,1,0:T(8,128)(2,1)}, u32[]{:S(2)}, u32[]{:S(2)}) collective-permute-start(bf16[4,512,128]{2,1,0:T(8,128)(2,1)S(1)} %all_gather.3.own_ref.refs_0_), channel_id=1, source_target_pairs={{0,4},{1,5},{2,6},{3,7},{4,0},{5,1},{6,2},{7,3},{8,12},{9,13},{10,... | collective-permute-start | bytes 1572872 | tf_op jit(solution)/shard_map/ppermute | solution.py:194
  112.6 28.7 %collective-permute-start.3 = (bf16[4,512,128]{2,1,0:T(8,128)(2,1)S(1)}, bf16[4,512,128]{2,1,0:T(8,128)(2,1)}, u32[]{:S(2)}, u32[]{:S(2)}) collective-permute-start(bf16[4,512,128]{2,1,0:T(8,128)(2,1)S(1)} %all_gather.3.own_ref.refs_0_), channel_id=1, source_target_pairs={{0,6},{1,7},{2,0},{3,1},{4,2},{5,3},{6,4},{7,5},{8,14},{9,15},{10,... | collective-permute-start | bytes 1572872 | tf_op jit(solution)/shard_map/ppermute | solution.py:194
  115.9 0.7 copy-start.3
  116.5 48.5 %all-to-all-start.3 = ((f32[32,1,1024]{2,1,0:T(1,128)}), f32[32,1,1024]{2,1,0:T(1,128)S(1)}, u32[]{:S(2)}, u32[]{:S(2)}) async-start(f32[32,1,1024]{2,1,0:T(1,128)} %copy-done.3), calls=%async_computation.3 | async-start | bytes 262144 | tf_op jit(solution)/shard_map/all_to_all | solution.py:189
  135.9 7.8 %collective-permute-start.4 = (bf16[4,512,128]{2,1,0:T(8,128)(2,1)S(1)}, bf16[4,512,128]{2,1,0:T(8,128)(2,1)S(1)}, u32[]{:S(2)}, u32[]{:S(2)}) collective-permute-start(bf16[4,512,128]{2,1,0:T(8,128)(2,1)S(1)} %collective-permute-done.1.refs_1_), channel_id=1, source_target_pairs={{0,1},{1,0},{2,3},{3,2},{4,5},{5,4},{6,7},{7,6},{8,9},{9,8},{10,11... | collective-permute-start | bytes 1572872 | tf_op jit(solution)/shard_map/ppermute | solution.py:202
  139.3 4.4 %collective-permute-start.5 = (bf16[4,512,128]{2,1,0:T(8,128)(2,1)}, bf16[4,512,128]{2,1,0:T(8,128)(2,1)S(1)}, u32[]{:S(2)}, u32[]{:S(2)}) collective-permute-start(bf16[4,512,128]{2,1,0:T(8,128)(2,1)} %collective-permute-done.2.refs_2_), channel_id=1, source_target_pairs={{0,1},{1,0},{2,3},{3,2},{4,5},{5,4},{6,7},{7,6},{8,9},{9,8},{10,11... | collective-permute-start | bytes 1572872 | tf_op jit(solution)/shard_map/ppermute | solution.py:202
  141.3 4.1 %collective-permute-start.6 = (bf16[4,512,128]{2,1,0:T(8,128)(2,1)}, bf16[4,512,128]{2,1,0:T(8,128)(2,1)S(1)}, u32[]{:S(2)}, u32[]{:S(2)}) collective-permute-start(bf16[4,512,128]{2,1,0:T(8,128)(2,1)} %collective-permute-done.3.refs_3_), channel_id=1, source_target_pairs={{0,1},{1,0},{2,3},{3,2},{4,5},{5,4},{6,7},{7,6},{8,9},{9,8},{10,11... | collective-permute-start | bytes 1572872 | tf_op jit(solution)/shard_map/ppermute | solution.py:202

commit v6 on v5

--- a/solution.py
+++ b/solution.py
@@ -47,6 +47,16 @@
     ).astype(jnp.bfloat16)
 
 
+def pack_kernel(w_ref, saved_ref, out_ref):
+    saved = saved_ref[...].T
+    for x in range(4):
+        for hi in range(4):
+            out_ref[x, :, hi * 256 : hi * 256 + 256] = w_ref[
+                :, (hi * 4 + x) * 256 : (hi * 4 + x) * 256 + 256
+            ]
+        out_ref[x, :, 1024:] = saved
+
+
 def both_cores(at_ref, own_ref, other_ref):
     for rows, side in ((own_ref, at_ref[1]), (other_ref, 1 - at_ref[1])):
         for hi in range(4):
@@ -83,29 +93,50 @@
     for lo in range(8):
         line = jnp.concatenate([row[:, lo * 16 : lo * 16 + 16] for row in rows], axis=1)
         for hi in range(4):
-            out_ref[hi * 8 + lo] = jnp.concatenate([line] * (1024 // 64), axis=1)
-
-
-def results_kernel(at_ref, w_ref, saved_ref, *refs):
-    own_refs, other_refs, (hidden_ref, weight_ref) = refs[:4], refs[4:8], refs[8:]
+            out_ref[hi * 8 + lo] = line
+
+
+def half_results(at_ref, side, w_ref, saved_ref, row_refs, write):
     left = saved_ref[...].T
-    total = None
+    blocks = []
     for k in range(4):
         source = lax.rem(at_ref[0] + 4 - k, 4)
-        blocks = [
-            (rows, pl.multiple_of((hi * 4 + source) * 256 + side * 128, 128))
+        some = [
+            (row_refs[k][hi], pl.multiple_of((hi * 4 + source) * 256 + side * 128, 128))
             for hi in range(4)
-            for rows, side in (
-                (own_refs[k][hi], at_ref[1]),
-                (other_refs[k][hi], 1 - at_ref[1]),
-            )
         ]
-        term = product(w_ref, 0, 192, blocks)
-        total = term if total is None else total + term
-        for rows, first in blocks:
-            weight_ref[:, pl.ds(first, 128)] = jnp.dot(
-                left, rows, preferred_element_type=jnp.float32
-            ).astype(jnp.bfloat16)
+        for hi, (rows, _) in enumerate(some):
+            write(k, hi, source, left, rows)
+        blocks += some
+    return product(w_ref, 0, 192, blocks)
+
+
+def own_kernel(at_ref, w_ref, saved_ref, *refs):
+    *row_refs, sums_ref, part_ref = refs
+
+    def write(k, hi, source, left, rows):
+        first = pl.multiple_of((hi * 4 + source) * 128, 128)
+        part_ref[:, pl.ds(first, 128)] = jnp.dot(
+            left, rows, preferred_element_type=jnp.float32
+        ).astype(jnp.bfloat16)
+
+    sums_ref[...] = half_results(at_ref, at_ref[1], w_ref, saved_ref, row_refs, write)
+
+
+def other_kernel(at_ref, w_ref, saved_ref, sums_ref, part_ref, *refs):
+    *row_refs, hidden_ref, weight_ref = refs
+    core = at_ref[1]
+
+    def write(k, hi, source, left, rows):
+        first = (hi * 4 + source) * 128
+        weight_ref[:, pl.ds(pl.multiple_of(2 * first + core * 128, 128), 128)] = part_ref[
+            :, pl.ds(pl.multiple_of(first, 128), 128)
+        ]
+        weight_ref[:, pl.ds(pl.multiple_of(2 * first + (1 - core) * 128, 128), 128)] = jnp.dot(
+            left, rows, preferred_element_type=jnp.float32
+        ).astype(jnp.bfloat16)
+
+    total = sums_ref[...] + half_results(at_ref, 1 - core, w_ref, saved_ref, row_refs, write)
     hidden_ref[...] = total.T.astype(jnp.bfloat16)
 
 
@@ -148,13 +179,15 @@
     replica = lax.axis_index("replica").astype(jnp.int32)
     at = jnp.stack([lax.rem(replica // 2, 4), lax.rem(replica, 2)])
 
-    swap = jnp.concatenate(
-        [
-            weight.reshape(192, 4, 4, 256).transpose(2, 0, 1, 3).reshape(4, 192, 1024),
-            jnp.broadcast_to(saved.T[None], (4, 192, 512)),
-        ],
-        axis=2,
-    )
+    swap = pl.pallas_call(
+        pack_kernel,
+        out_shape=jax.ShapeDtypeStruct((4, 192, 1536), jnp.bfloat16),
+        in_specs=[vmem] * 2,
+        out_specs=vmem,
+        compiler_params=params,
+        cost_estimate=pl.CostEstimate(flops=0, bytes_accessed=4 * 1024 * 1024, transcendentals=0),
+        name="pack",
+    )(weight, saved)
     swapped = lax.all_to_all(
         swap, BOTH, 0, 0, tiled=True, axis_index_groups=groups("x")
     ).reshape(768, 1536)
@@ -179,7 +212,7 @@
     )
     to_z = pl.pallas_call(
         turn_kernel,
-        out_shape=jax.ShapeDtypeStruct((32, 1, 1024), jnp.float32),
+        out_shape=jax.ShapeDtypeStruct((32, 1, 64), jnp.float32),
         in_specs=[vmem],
         out_specs=vmem,
         compiler_params=params,
@@ -201,26 +234,39 @@
     other_rows = [other] + [
         lax.ppermute(rows, "replica", [(i, i ^ 1) for i in range(32)]) for rows in own_rows[1:]
     ]
+    small = pl.CostEstimate(flops=1000, bytes_accessed=1000, transcendentals=0)
+    sums, part = pl.pallas_call(
+        own_kernel,
+        out_shape=(
+            jax.ShapeDtypeStruct((192, slot_total), jnp.float32),
+            jax.ShapeDtypeStruct((192, 2048), jnp.bfloat16),
+        ),
+        in_specs=[smem] + [vmem] * 6,
+        out_specs=(vmem, vmem),
+        compiler_params=params,
+        cost_estimate=small,
+        name="own",
+    )(at, weight, saved, *own_rows)
+    from_z, sums, part = lax.optimization_barrier((from_z, sums, part))
     hidden_out, weight_out = pl.pallas_call(
-        results_kernel,
+        other_kernel,
         out_shape=(
             jax.ShapeDtypeStruct(saved.shape, jnp.bfloat16),
             jax.ShapeDtypeStruct(weight.shape, jnp.bfloat16),
         ),
-        in_specs=[smem] + [vmem] * 10,
+        in_specs=[smem] + [vmem] * 8,
         out_specs=(vmem, vmem),
         compiler_params=params,
-        cost_estimate=pl.CostEstimate(flops=int(1000), bytes_accessed=1000, transcendentals=0),
-        name="results",
-    )(at, weight, saved, *own_rows, *other_rows)
-    from_z, hidden_out, weight_out = lax.optimization_barrier((from_z, hidden_out, weight_out))
+        cost_estimate=small,
+        name="other",
+    )(at, weight, saved, sums, part, *other_rows)
     grad_gate = pl.pallas_call(
         gate_kernel,
         out_shape=jax.ShapeDtypeStruct((1, 256), jnp.float32),
         in_specs=[vmem] * 3,
         out_specs=vmem,
         compiler_params=params,
-        cost_estimate=pl.CostEstimate(flops=int(1000), bytes_accessed=1000, transcendentals=0),
+        cost_estimate=pl.CostEstimate(flops=int(5.5e+09), bytes_accessed=1000, transcendentals=0),
         name="gate",
     )(from_z, target, gate_row)
     return (hidden_out.reshape(hidden_saved.shape), weight_out[None], grad_gate.reshape(256))

time: 168 us -> 158 us (0.940)
  starting transfers between devices: 77.4 us -> 60.4 us
  blocking collectives: 45.9 us -> 56 us
  local copies, waits for them, and re-layouts: 11.2 us -> 6.54 us
  Pallas kernels: 9.81 us -> 13.8 us
  other arithmetic: 3.09 us -> 0.08 us
    all_to_all x1, waiting for transfers between devices: 14.1 us -> 2.74 us  [per_device(): lax.all_to_all(to_z, BOTH, 0, 0, tiled=True, axis_index_groups=groups('hi...]
    all_gather x1, blocking collectives: 45.9 us -> 56 us  [per_device(): lax.all_gather(arrived, BOTH, axis=0, tiled=False, axis_index_groups=grou...]
    ppermute x1, starting transfers between devices: 14.4 us -> 4.52 us  [per_device(): other = lax.ppermute(own, 'replica', [(i, i ^ 1) for i in range(32)])]
    all_to_all x1, starting transfers between devices: 19.4 us -> 11.6 us  [per_device(): lax.all_to_all(to_z, BOTH, 0, 0, tiled=True, axis_index_groups=groups('hi...]
    all_to_all x1, waiting for transfers between devices: 0.34 us -> 7.74 us  [per_device(): lax.all_to_all(outgoing.reshape(experts, slot_count, -1), 'expert', 0, 0,...]
    ppermute x3, waiting for transfers between devices: 0.01 us -> 6.13 us  [per_device(): lax.ppermute(going, 'replica', [(i, i // 8 * 8 + (i % 8 // 2 + k) % 4 * 2...]
    pallas_call x2 -> x4, Pallas kernels: 5.76 us -> 9.79 us  [the longest x1 4.34 us: per_device(): pl.pallas_call(other_kernel, out_shape=(jax.ShapeDtypeStruct(saved.shape,...]
    another operation x1 -> x0, local copies, waits for them, and re-layouts: 3.86 us -> none  [per_device(): weight.reshape(192, 4, 4, 256).transpose(2, 0, 1, 3).reshape(4, 192, 1024)]
  transfers between devices with their start and end apart: 11 -> 11, of which waited for: 4 -> 5; matrix products, arithmetic and copies ran while one was open for 7% -> 0% of each run, Pallas kernels for 3% -> 4%
where the time goes in v6:
time: 158 us; the launch traced here: 156 us
  starting transfers between devices  60.4 us (38%)
  blocking collectives  56 us (35%)
  waiting for transfers between devices  18 us (11%)
  Pallas kernels  13.8 us (9%)
  local copies, waits for them, and re-layouts  6.54 us (4%)
    all_gather x1, blocking collectives, per_device(): lax.all_gather(arrived, BOTH, axis=0, tiled=False, axis_index_groups=grou...  56 us
    all_to_all x1, starting transfers between devices, per_device(): lax.all_to_all(outgoing.reshape(experts, slot_count, -1), 'expert', 0, 0,...  16.1 us
    all_to_all x1, starting transfers between devices, per_device(): lax.all_to_all(to_z, BOTH, 0, 0, tiled=True, axis_index_groups=groups('hi...  11.6 us
    ppermute x3, starting transfers between devices, per_device(): lax.ppermute(going, 'replica', [(i, i // 8 * 8 + (i % 8 // 2 + k) % 4 * 2...  9.61 us
    all_to_all x1, waiting for transfers between devices, per_device(): lax.all_to_all(outgoing.reshape(experts, slot_count, -1), 'expert', 0, 0,...  7.74 us
    ppermute x3, starting transfers between devices, per_device(): lax.ppermute(rows, 'replica', [(i, i ^ 1) for i in range(32)])  7.54 us
    all_to_all x1, starting transfers between devices, per_device(): lax.all_to_all(slot_sums, BOTH, 0, 0, tiled=True, axis_index_groups=group...  7.04 us
    ppermute x3, waiting for transfers between devices, per_device(): lax.ppermute(going, 'replica', [(i, i // 8 * 8 + (i % 8 // 2 + k) % 4 * 2...  6.13 us
  transfers between devices with their start and end apart: 11, of which 5 were waited for; matrix products, arithmetic and copies ran while one was open for 0% of the time, Pallas kernels for 4%

profile of v6, /device:TPU:1, one launch (start us, length us, event | category | flops | bytes accessed | tf_op | source)
XLA Modules:
  0.0 155.7 jit_solution(5105054986127854853)
XLA Ops:
  0.6 0.7 reshape.29.gate_ref
  1.3 0.0 copy-start.8
  1.3 0.8 copy-done.8
  2.1 0.0 copy-start.9
  2.1 0.7 copy-done.9
  2.8 1.0 place.1
  3.9 16.1 %all-to-all-start = ((bf16[32,16,128]{2,1,0:T(8,128)(2,1)}), bf16[32,16,128]{2,1,0:T(8,128)(2,1)S(1)}, u32[]{:S(2)}, u32[]{:S(2)}) async-start(bf16[32,16,128]{2,1,0:T(8,128)(2,1)} %bitcast.5), calls=%async_computation | async-start | bytes 262144 | tf_op jit(solution)/shard_map/all_to_all | solution.py:195
  20.0 0.0 copy-start
  20.0 1.4 copy-done
  21.4 0.9 copy-done.2
  22.3 1.7 %pack.1 = bf16[4,192,1536]{2,1,0:T(8,128)(2,1)} custom-call(bf16[192,4096]{1,0:T(8,128)(2,1)S(1)} %bitcast.11, bf16[512,192]{1,0:T(8,128)(2,1)S(1)} %bitcast.15), custom_call_target="tpu_custom_call" | custom-call | bytes 4194304 | tf_op jit(solution)/shard_map/pack/pallas_call | solution.py:182
  24.0 7.7 %all-to-all-done = bf16[32,16,128]{2,1,0:T(8,128)(2,1)S(1)} async-done(((bf16[32,16,128]{2,1,0:T(8,128)(2,1)}), bf16[32,16,128]{2,1,0:T(8,128)(2,1)S(1)}, u32[]{:S(2)}, u32[]{:S(2)}) %all-to-all-start) | async-done | bytes 131104 | tf_op jit(solution)/shard_map/all_to_all | solution.py:195
  31.7 4.0 %all-to-all-start.1 = ((bf16[4,192,1536]{2,1,0:T(8,128)(2,1)}), bf16[4,192,1536]{2,1,0:T(8,128)(2,1)S(1)}, u32[]{:S(2)}, u32[]{:S(2)}) async-start(bf16[4,192,1536]{2,1,0:T(8,128)(2,1)} %pack.1), calls=%async_computation.1 | async-start | bytes 4718592 | tf_op jit(solution)/shard_map/all_to_all | solution.py:191
  35.7 56.0 %all_gather.3.own_ref.refs_0_ = bf16[4,512,128]{2,1,0:T(8,128)(2,1)S(1)} all-gather(bf16[1,512,128]{2,1,0:T(8,128)(2,1)S(1)} %bitcast.19), channel_id=1, replica_groups={{0,8,16,24},{1,9,17,25},{2,10,18,26},{3,11,19,27},{4,12,20,28},{5,13,21..., dimensions={0}, use_global_device_ids=true | all-gather | bytes 655360 | tf_op jit(solution)/shard_map/all_gather | solution.py:198
  91.8 4.5 %collective-permute-start = (bf16[4,512,128]{2,1,0:T(8,128)(2,1)S(1)}, bf16[4,512,128]{2,1,0:T(8,128)(2,1)S(1)}, u32[]{:S(2)}, u32[]{:S(2)}) collective-permute-start(bf16[4,512,128]{2,1,0:T(8,128)(2,1)S(1)} %all_gather.3.own_ref.refs_0_), channel_id=1, source_target_pairs={{0,1},{1,0},{2,3},{3,2},{4,5},{5,4},{6,7},{7,6},{8,9},{9,8},{10,11... | collective-permute-start | bytes 1572872 | tf_op jit(solution)/shard_map/ppermute | solution.py:199
  96.3 0.1 pad_add_fusion.at_ref
  96.4 1.4 collective-permute-done.other_ref.refs_0_
  97.8 0.0 all-to-all-done.1
  97.8 2.2 %slots.1 = f32[32,1,128]{2,1,0:T(1,128)} custom-call(s32[2]{0:T(128)S(1)} %pad_add_fusion.at_ref, bf16[4,512,128]{2,1,0:T(8,128)(2,1)S(1)} %all_gather.3.own_ref.refs_0_, bf16[4,512,128]{2,1,0:T(8,128)(2,1)S(1)} %collective-permute-done.other_ref.refs_0_, bf16[768,1536]{1,0:T(8,128)(2,1)S(1)} %bitcast.14), custom_call_target="tpu_custom_call" | custom-call | flops 805306368 | bytes 6291456 | tf_op jit(solution)/shard_map/slots/pallas_call | solution.py:201
  100.0 7.0 %all-to-all-start.2 = ((f32[32,1,128]{2,1,0:T(1,128)}), f32[32,1,128]{2,1,0:T(1,128)S(1)}, u32[]{:S(2)}, u32[]{:S(2)}) async-start(f32[32,1,128]{2,1,0:T(1,128)} %slots.1), calls=%async_computation.2 | async-start | bytes 32768 | tf_op jit(solution)/shard_map/all_to_all | solution.py:210
  107.0 0.0 copy-start.1
  107.0 0.0 copy-start.3
  107.0 4.6 %collective-permute-start.3 = (bf16[4,512,128]{2,1,0:T(8,128)(2,1)S(1)}, bf16[4,512,128]{2,1,0:T(8,128)(2,1)}, u32[]{:S(2)}, u32[]{:S(2)}) collective-permute-start(bf16[4,512,128]{2,1,0:T(8,128)(2,1)S(1)} %all_gather.3.own_ref.refs_0_), channel_id=1, source_target_pairs={{0,6},{1,7},{2,0},{3,1},{4,2},{5,3},{6,4},{7,5},{8,14},{9,15},{10,... | collective-permute-start | bytes 1572872 | tf_op jit(solution)/shard_map/ppermute | solution.py:227
  111.7 2.5 %collective-permute-start.2 = (bf16[4,512,128]{2,1,0:T(8,128)(2,1)S(1)}, bf16[4,512,128]{2,1,0:T(8,128)(2,1)}, u32[]{:S(2)}, u32[]{:S(2)}) collective-permute-start(bf16[4,512,128]{2,1,0:T(8,128)(2,1)S(1)} %all_gather.3.own_ref.refs_0_), channel_id=1, source_target_pairs={{0,4},{1,5},{2,6},{3,7},{4,0},{5,1},{6,2},{7,3},{8,12},{9,13},{10,... | collective-permute-start | bytes 1572872 | tf_op jit(solution)/shard_map/ppermute | solution.py:227
  114.2 2.5 %collective-permute-start.1 = (bf16[4,512,128]{2,1,0:T(8,128)(2,1)S(1)}, bf16[4,512,128]{2,1,0:T(8,128)(2,1)}, u32[]{:S(2)}, u32[]{:S(2)}) collective-permute-start(bf16[4,512,128]{2,1,0:T(8,128)(2,1)S(1)} %all_gather.3.own_ref.refs_0_), channel_id=1, source_target_pairs={{0,2},{1,3},{2,4},{3,5},{4,6},{5,7},{6,0},{7,1},{8,10},{9,11},{10,... | collective-permute-start | bytes 1572872 | tf_op jit(solution)/shard_map/ppermute | solution.py:227
  116.7 0.0 all-to-all-done.2.sums_ref
  116.7 0.7 turn.1
  117.4 11.6 %all-to-all-start.3 = ((f32[32,1,64]{2,1,0:T(1,128)}), f32[32,1,64]{2,1,0:T(1,128)S(1)}, u32[]{:S(2)}, u32[]{:S(2)}) async-start(f32[32,1,64]{2,1,0:T(1,128)} %turn.1), calls=%async_computation.3 | async-start | bytes 32768 | tf_op jit(solution)/shard_map/all_to_all | solution.py:222
  129.0 4.7 %collective-permute-done.3.refs_3_ = bf16[4,512,128]{2,1,0:T(8,128)(2,1)} collective-permute-done((bf16[4,512,128]{2,1,0:T(8,128)(2,1)S(1)}, bf16[4,512,128]{2,1,0:T(8,128)(2,1)}, u32[]{:S(2)}, u32[]{:S(2)}) %collective-permute-start.3) | collective-permute-done | bytes 524320 | tf_op jit(solution)/shard_map/ppermute | solution.py:227
  133.7 3.2 %collective-permute-start.6 = (bf16[4,512,128]{2,1,0:T(8,128)(2,1)}, bf16[4,512,128]{2,1,0:T(8,128)(2,1)}, u32[]{:S(2)}, u32[]{:S(2)}) collective-permute-start(bf16[4,512,128]{2,1,0:T(8,128)(2,1)} %collective-permute-done.3.refs_3_), channel_id=1, source_target_pairs={{0,1},{1,0},{2,3},{3,2},{4,5},{5,4},{6,7},{7,6},{8,9},{9,8},{10,11... | collective-permute-start | bytes 1572872 | tf_op jit(solution)/shard_map/ppermute | solution.py:235
  136.9 0.0 collective-permute-done.2.refs_2_
  137.0 1.9 %collective-permute-start.5 = (bf16[4,512,128]{2,1,0:T(8,128)(2,1)}, bf16[4,512,128]{2,1,0:T(8,128)(2,1)}, u32[]{:S(2)}, u32[]{:S(2)}) collective-permute-start(bf16[4,512,128]{2,1,0:T(8,128)(2,1)} %collective-permute-done.2.refs_2_), channel_id=1, source_target_pairs={{0,1},{1,0},{2,3},{3,2},{4,5},{5,4},{6,7},{7,6},{8,9},{9,8},{10,11... | collective-permute-start | bytes 1572872 | tf_op jit(solution)/shard_map/ppermute | solution.py:235
  138.9 1.4 collective-permute-done.1.refs_1_
  140.3 2.4 %collective-permute-start.4 = (bf16[4,512,128]{2,1,0:T(8,128)(2,1)}, bf16[4,512,128]{2,1,0:T(8,128)(2,1)}, u32[]{:S(2)}, u32[]{:S(2)}) collective-permute-start(bf16[4,512,128]{2,1,0:T(8,128)(2,1)} %collective-permute-done.1.refs_1_), channel_id=1, source_target_pairs={{0,1},{1,0},{2,3},{3,2},{4,5},{5,4},{6,7},{7,6},{8,9},{9,8},{10,11... | collective-permute-start | bytes 1572872 | tf_op jit(solution)/shard_map/ppermute | solution.py:235
  142.7 0.0 copy-done.1
  142.7 0.0 copy-done.3
  142.7 3.1 %own.1 = (f32[192,512]{1,0:T(8,128)S(1)}, bf16[192,2048]{1,0:T(8,128)(2,1)S(1)}) custom-call(s32[2]{0:T(128)S(1)} %pad_add_fusion.at_ref, bf16[192,4096]{1,0:T(8,128)(2,1)S(1)} %bitcast.12, bf16[512,192]{1,0:T(8,128)(2,1)S(1)} %bitcast.16, bf16[4,512,128]{2,1,0:T(8,128)(2,1)S(1)} %all_gather.3.own_ref.refs_0_, ...), custom_call_target="tpu_custom_call" | custom-call | flops 1000 | bytes 1000 | tf_op jit(solution)/shard_map/own/pallas_call | solution.py:238
  145.8 0.0 copy-start.4
  145.8 0.9 copy-done.4
  146.7 0.7 copy-done.6
  147.4 2.7 %all-to-all-done.3.sums_ref = f32[32,1,64]{2,1,0:T(1,128)S(1)} async-done(((f32[32,1,64]{2,1,0:T(1,128)}), f32[32,1,64]{2,1,0:T(1,128)S(1)}, u32[]{:S(2)}, u32[]{:S(2)}) %all-to-all-start.3) | async-done | bytes 8224 | tf_op jit(solution)/shard_map/all_to_all | solution.py:222
  150.1 0.8 gate.1
  151.0 0.0 collective-permute-done.6.refs_3_
  151.0 0.0 collective-permute-done.5.refs_2_
  151.0 0.0 collective-permute-done.4.refs_1_
  151.0 0.3 copy-done.5
  151.3 0.1 copy-done.7
  151.4 4.3 %other.1 = (bf16[512,192]{1,0:T(8,128)(2,1)}, bf16[192,4096]{1,0:T(8,128)(2,1)}) custom-call(s32[2]{0:T(128)S(1)} %pad_add_fusion.at_ref, bf16[192,4096]{1,0:T(8,128)(2,1)S(1)} %bitcast.13, bf16[512,192]{1,0:T(8,128)(2,1)S(1)} %bitcast.17, f32[192,512]{1,0:T(8,128)S(1)} %copy-done.7, bf16[192,2048]{1,0:T(8,128)(2,1)S(1)} %copy-done.5, ...), custom_call_target="tpu_custom_call" | custom-call | flops 1000 | bytes 1000 | tf_op jit(solution)/shard_map/other/pallas_call | solution.py:251
  (4 shorter events, 0.0 us)
Async XLA Ops:
  1.3 0.8 copy-start.8
  2.1 0.7 copy-start.9
  3.9 27.9 %all-to-all-start = ((bf16[32,16,128]{2,1,0:T(8,128)(2,1)}), bf16[32,16,128]{2,1,0:T(8,128)(2,1)S(1)}, u32[]{:S(2)}, u32[]{:S(2)}) async-start(bf16[32,16,128]{2,1,0:T(8,128)(2,1)} %bitcast.5), calls=%async_computation | async-start | bytes 262144 | tf_op jit(solution)/shard_map/all_to_all | solution.py:195
  20.0 1.4 copy-start
  21.4 0.9 copy-start.2
  31.7 66.1 %all-to-all-start.1 = ((bf16[4,192,1536]{2,1,0:T(8,128)(2,1)}), bf16[4,192,1536]{2,1,0:T(8,128)(2,1)S(1)}, u32[]{:S(2)}, u32[]{:S(2)}) async-start(bf16[4,192,1536]{2,1,0:T(8,128)(2,1)} %pack.1), calls=%async_computation.1 | async-start | bytes 4718592 | tf_op jit(solution)/shard_map/all_to_all | solution.py:191
  91.8 6.0 %collective-permute-start = (bf16[4,512,128]{2,1,0:T(8,128)(2,1)S(1)}, bf16[4,512,128]{2,1,0:T(8,128)(2,1)S(1)}, u32[]{:S(2)}, u32[]{:S(2)}) collective-permute-start(bf16[4,512,128]{2,1,0:T(8,128)(2,1)S(1)} %all_gather.3.own_ref.refs_0_), channel_id=1, source_target_pairs={{0,1},{1,0},{2,3},{3,2},{4,5},{5,4},{6,7},{7,6},{8,9},{9,8},{10,11... | collective-permute-start | bytes 1572872 | tf_op jit(solution)/shard_map/ppermute | solution.py:199
  100.0 16.7 %all-to-all-start.2 = ((f32[32,1,128]{2,1,0:T(1,128)}), f32[32,1,128]{2,1,0:T(1,128)S(1)}, u32[]{:S(2)}, u32[]{:S(2)}) async-start(f32[32,1,128]{2,1,0:T(1,128)} %slots.1), calls=%async_computation.2 | async-start | bytes 32768 | tf_op jit(solution)/shard_map/all_to_all | solution.py:210
  107.0 35.7 %copy-start.1 = (bf16[1,192,4096]{2,1,0:T(8,128)(2,1)S(1)}, bf16[1,192,4096]{2,1,0:T(8,128)(2,1)}, u32[]{:S(2)}) copy-start(bf16[1,192,4096]{2,1,0:T(8,128)(2,1)} %param.9) | copy-start | bytes 4718596
  107.0 35.7 %copy-start.3 = (bf16[1,32,16,192]{3,2,1,0:T(8,128)(2,1)S(1)}, bf16[1,32,16,192]{3,2,1,0:T(8,128)(2,1)}, u32[]{:S(2)}) copy-start(bf16[1,32,16,192]{3,2,1,0:T(8,128)(2,1)} %param.8) | copy-start | bytes 589828
  107.0 26.7 %collective-permute-start.3 = (bf16[4,512,128]{2,1,0:T(8,128)(2,1)S(1)}, bf16[4,512,128]{2,1,0:T(8,128)(2,1)}, u32[]{:S(2)}, u32[]{:S(2)}) collective-permute-start(bf16[4,512,128]{2,1,0:T(8,128)(2,1)S(1)} %all_gather.3.own_ref.refs_0_), channel_id=1, source_target_pairs={{0,6},{1,7},{2,0},{3,1},{4,2},{5,3},{6,4},{7,5},{8,14},{9,15},{10,... | collective-permute-start | bytes 1572872 | tf_op jit(solution)/shard_map/ppermute | solution.py:227
  111.7 25.3 %collective-permute-start.2 = (bf16[4,512,128]{2,1,0:T(8,128)(2,1)S(1)}, bf16[4,512,128]{2,1,0:T(8,128)(2,1)}, u32[]{:S(2)}, u32[]{:S(2)}) collective-permute-start(bf16[4,512,128]{2,1,0:T(8,128)(2,1)S(1)} %all_gather.3.own_ref.refs_0_), channel_id=1, source_target_pairs={{0,4},{1,5},{2,6},{3,7},{4,0},{5,1},{6,2},{7,3},{8,12},{9,13},{10,... | collective-permute-start | bytes 1572872 | tf_op jit(solution)/shard_map/ppermute | solution.py:227
  114.2 26.1 %collective-permute-start.1 = (bf16[4,512,128]{2,1,0:T(8,128)(2,1)S(1)}, bf16[4,512,128]{2,1,0:T(8,128)(2,1)}, u32[]{:S(2)}, u32[]{:S(2)}) collective-permute-start(bf16[4,512,128]{2,1,0:T(8,128)(2,1)S(1)} %all_gather.3.own_ref.refs_0_), channel_id=1, source_target_pairs={{0,2},{1,3},{2,4},{3,5},{4,6},{5,7},{6,0},{7,1},{8,10},{9,11},{10,... | collective-permute-start | bytes 1572872 | tf_op jit(solution)/shard_map/ppermute | solution.py:227
  117.4 32.7 %all-to-all-start.3 = ((f32[32,1,64]{2,1,0:T(1,128)}), f32[32,1,64]{2,1,0:T(1,128)S(1)}, u32[]{:S(2)}, u32[]{:S(2)}) async-start(f32[32,1,64]{2,1,0:T(1,128)} %turn.1), calls=%async_computation.3 | async-start | bytes 32768 | tf_op jit(solution)/shard_map/all_to_all | solution.py:222
  133.7 17.3 %collective-permute-start.6 = (bf16[4,512,128]{2,1,0:T(8,128)(2,1)}, bf16[4,512,128]{2,1,0:T(8,128)(2,1)}, u32[]{:S(2)}, u32[]{:S(2)}) collective-permute-start(bf16[4,512,128]{2,1,0:T(8,128)(2,1)} %collective-permute-done.3.refs_3_), channel_id=1, source_target_pairs={{0,1},{1,0},{2,3},{3,2},{4,5},{5,4},{6,7},{7,6},{8,9},{9,8},{10,11... | collective-permute-start | bytes 1572872 | tf_op jit(solution)/shard_map/ppermute | solution.py:235
  137.0 14.0 %collective-permute-start.5 = (bf16[4,512,128]{2,1,0:T(8,128)(2,1)}, bf16[4,512,128]{2,1,0:T(8,128)(2,1)}, u32[]{:S(2)}, u32[]{:S(2)}) collective-permute-start(bf16[4,512,128]{2,1,0:T(8,128)(2,1)} %collective-permute-done.2.refs_2_), channel_id=1, source_target_pairs={{0,1},{1,0},{2,3},{3,2},{4,5},{5,4},{6,7},{7,6},{8,9},{9,8},{10,11... | collective-permute-start | bytes 1572872 | tf_op jit(solution)/shard_map/ppermute | solution.py:235
  140.3 10.7 %collective-permute-start.4 = (bf16[4,512,128]{2,1,0:T(8,128)(2,1)}, bf16[4,512,128]{2,1,0:T(8,128)(2,1)}, u32[]{:S(2)}, u32[]{:S(2)}) collective-permute-start(bf16[4,512,128]{2,1,0:T(8,128)(2,1)} %collective-permute-done.1.refs_1_), channel_id=1, source_target_pairs={{0,1},{1,0},{2,3},{3,2},{4,5},{5,4},{6,7},{7,6},{8,9},{9,8},{10,11... | collective-permute-start | bytes 1572872 | tf_op jit(solution)/shard_map/ppermute | solution.py:235
  145.8 0.9 copy-start.4
  146.7 0.7 copy-start.6
  150.1 1.1 copy-start.5
  150.1 1.2 copy-start.7

commit v7 on v6

--- a/solution.py
+++ b/solution.py
@@ -78,22 +78,20 @@
     blocks = list(both_cores(at_ref, own_ref, other_ref))
     total = product(swap_ref, 0, 768, blocks)
     sums = jnp.sum(total * swap_ref[:, 1024:].astype(jnp.float32), axis=0, keepdims=True)
-    for y in range(4):
-        for i in range(8):
-            out_ref[y * 8 + i] = sums[:, y * 128 : y * 128 + 128]
-
-
-def turn_kernel(sums_ref, out_ref):
-    rows = []
-    for y in range(4):
-        row = sums_ref[y * 8]
-        for i in range(1, 8):
-            row = row + sums_ref[y * 8 + i]
-        rows.append(row)
-    for lo in range(8):
-        line = jnp.concatenate([row[:, lo * 16 : lo * 16 + 16] for row in rows], axis=1)
-        for hi in range(4):
-            out_ref[hi * 8 + lo] = line
+    for block in range(32):
+        out_ref[block] = sums[:, block * 16 : block * 16 + 16]
+
+
+def turn_kernel(sums_ref, target_ref, out_ref):
+    columns = sums_ref[:, 0].T
+    expert, slot = target_ref[...] // 16, target_ref[...] % 16
+    rows = lax.broadcasted_iota(jnp.int32, (16, 256), 0)
+    found = jnp.zeros((16, 256), jnp.float32)
+    for i in range(32):
+        found = jnp.where((rows == slot) & (expert == i), columns[:, i : i + 1], found)
+    line = jnp.sum(found, axis=0, keepdims=True)
+    for i in range(32):
+        out_ref[i] = line
 
 
 def half_results(at_ref, side, w_ref, saved_ref, row_refs, write):
@@ -140,18 +138,8 @@
     hidden_ref[...] = total.T.astype(jnp.bfloat16)
 
 
-def gate_kernel(sums_ref, target_ref, gate_ref, out_ref):
-    total = sum(sums_ref[hi * 8 : hi * 8 + 8, 0, :64] for hi in range(4))
-    columns = total.T
-    target = target_ref[...]
-    expert, slot = target // 16, target % 16
-    place = expert // 8 * 16 + slot
-    rows = lax.broadcasted_iota(jnp.int32, (64, 256), 0)
-    found = jnp.zeros((64, 256), jnp.float32)
-    for lo in range(8):
-        hit = (rows == place) & (expert % 8 == lo)
-        found = jnp.where(hit, columns[:, lo : lo + 1], found)
-    out_ref[...] = jnp.sum(found, axis=0, keepdims=True) / gate_ref[...].astype(jnp.float32)
+def gate_kernel(sums_ref, gate_ref, out_ref):
+    out_ref[...] = jnp.sum(sums_ref[...], axis=0) / gate_ref[...].astype(jnp.float32)
 
 
 def per_device(grad_out, gate_prob, routes, hidden_saved, w_out):
@@ -200,28 +188,24 @@
 
     slot_sums = pl.pallas_call(
         slots_kernel,
-        out_shape=jax.ShapeDtypeStruct((32, 1, 128), jnp.float32),
+        out_shape=jax.ShapeDtypeStruct((32, 1, 16), jnp.float32),
         in_specs=[smem, vmem, vmem, vmem],
         out_specs=vmem,
         compiler_params=params,
         cost_estimate=cost,
         name="slots",
     )(at, own, other, swapped)
-    from_plane = lax.all_to_all(
-        slot_sums, BOTH, 0, 0, tiled=True, axis_index_groups=groups("y", "x", "core")
-    )
-    to_z = pl.pallas_call(
+    from_experts = lax.all_to_all(slot_sums, "expert", 0, 0, tiled=True)
+    token_sums = pl.pallas_call(
         turn_kernel,
-        out_shape=jax.ShapeDtypeStruct((32, 1, 64), jnp.float32),
-        in_specs=[vmem],
+        out_shape=jax.ShapeDtypeStruct((32, 1, 256), jnp.float32),
+        in_specs=[vmem] * 2,
         out_specs=vmem,
         compiler_params=params,
         cost_estimate=pl.CostEstimate(flops=int(1e+10), bytes_accessed=1000, transcendentals=0),
         name="turn",
-    )(from_plane)
-    from_z = lax.all_to_all(
-        to_z, BOTH, 0, 0, tiled=True, axis_index_groups=groups("hi", "lo")
-    )
+    )(from_experts, target)
+    from_all = lax.all_to_all(token_sums, "replica", 0, 0, tiled=True)
     going, _ = lax.optimization_barrier((own, slot_sums))
     own_rows = [own] + [
         lax.ppermute(
@@ -247,7 +231,7 @@
         cost_estimate=small,
         name="own",
     )(at, weight, saved, *own_rows)
-    from_z, sums, part = lax.optimization_barrier((from_z, sums, part))
+    from_all, sums, part = lax.optimization_barrier((from_all, sums, part))
     hidden_out, weight_out = pl.pallas_call(
         other_kernel,
         out_shape=(
@@ -263,12 +247,12 @@
     grad_gate = pl.pallas_call(
         gate_kernel,
         out_shape=jax.ShapeDtypeStruct((1, 256), jnp.float32),
-        in_specs=[vmem] * 3,
-        out_specs=vmem,
-        compiler_params=params,
-        cost_estimate=pl.CostEstimate(flops=int(5.5e+09), bytes_accessed=1000, transcendentals=0),
+        in_specs=[vmem] * 2,
+        out_specs=vmem,
+        compiler_params=params,
+        cost_estimate=pl.CostEstimate(flops=int(4e+09), bytes_accessed=1000, transcendentals=0),
         name="gate",
-    )(from_z, target, gate_row)
+    )(from_all, gate_row)
     return (hidden_out.reshape(hidden_saved.shape), weight_out[None], grad_gate.reshape(256))
 
 

time: 158 us -> 167 us (1.057); the launches traced: 156 us -> 167 us
  starting transfers between devices: 60.4 us -> 66.3 us
  waiting for transfers between devices: 18 us -> 22.8 us
    all_to_all x2, waiting for transfers between devices: 2.74 us -> 12.9 us  [the longest x1 11.9 us: per_device(): from_all = lax.all_to_all(token_sums, 'replica', 0, 0, tiled=True)]
    all_to_all x2, starting transfers between devices: 18.6 us -> 24.6 us  [the longest x1 16.6 us: per_device(): from_all = lax.all_to_all(token_sums, 'replica', 0, 0, tiled=True)]
    ppermute x3, waiting for transfers between devices: 6.13 us -> 0.76 us  [per_device(): lax.ppermute(going, 'replica', [(i, i // 8 * 8 + (i % 8 // 2 + k) % 4 * 2...]
where the time goes in v7:
time: 167 us
  starting transfers between devices  66.3 us (40%)
  blocking collectives  56 us (34%)
  waiting for transfers between devices  22.8 us (14%)
  Pallas kernels  13.9 us (8%)
  local copies, waits for them, and re-layouts  6.77 us (4%)
    all_gather x1, blocking collectives, per_device(): lax.all_gather(arrived, BOTH, axis=0, tiled=False, axis_index_groups=grou...  56 us
    all_to_all x1, starting transfers between devices, per_device(): from_all = lax.all_to_all(token_sums, 'replica', 0, 0, tiled=True)  16.6 us
    all_to_all x1, starting transfers between devices, per_device(): lax.all_to_all(outgoing.reshape(experts, slot_count, -1), 'expert', 0, 0,...  16.1 us
    all_to_all x1, waiting for transfers between devices, per_device(): from_all = lax.all_to_all(token_sums, 'replica', 0, 0, tiled=True)  11.9 us
    ppermute x3, starting transfers between devices, per_device(): lax.ppermute(going, 'replica', [(i, i // 8 * 8 + (i % 8 // 2 + k) % 4 * 2...  10.2 us
    all_to_all x1, starting transfers between devices, per_device(): from_experts = lax.all_to_all(slot_sums, 'expert', 0, 0, tiled=True)  8.05 us
    all_to_all x1, waiting for transfers between devices, per_device(): lax.all_to_all(outgoing.reshape(experts, slot_count, -1), 'expert', 0, 0,...  7.74 us
    ppermute x3, starting transfers between devices, per_device(): lax.ppermute(rows, 'replica', [(i, i ^ 1) for i in range(32)])  6.74 us
  transfers between devices with their start and end apart: 11, of which 5 were waited for; matrix products, arithmetic and copies ran while one was open for 0% of the time, Pallas kernels for 4%

profile of v7, /device:TPU:1, one launch (start us, length us, event | category | flops | bytes accessed | tf_op | source)
XLA Modules:
  0.0 166.6 jit_solution(4858173957333381053)
XLA Ops:
  0.6 0.7 reshape.29.gate_ref
  1.3 0.0 copy-start.8
  1.3 0.8 copy-done.8
  2.1 0.0 copy-start.9
  2.1 0.7 copy-done.9
  2.8 1.0 place.1
  3.9 16.1 %all-to-all-start = ((bf16[32,16,128]{2,1,0:T(8,128)(2,1)}), bf16[32,16,128]{2,1,0:T(8,128)(2,1)S(1)}, u32[]{:S(2)}, u32[]{:S(2)}) async-start(bf16[32,16,128]{2,1,0:T(8,128)(2,1)} %bitcast.5), calls=%async_computation | async-start | bytes 262144 | tf_op jit(solution)/shard_map/all_to_all | solution.py:183
  20.0 0.0 copy-start
  20.0 1.4 copy-done
  21.4 0.0 copy-start.2
  21.4 0.9 copy-done.2
  22.3 1.7 %pack.1 = bf16[4,192,1536]{2,1,0:T(8,128)(2,1)} custom-call(bf16[192,4096]{1,0:T(8,128)(2,1)S(1)} %bitcast.11, bf16[512,192]{1,0:T(8,128)(2,1)S(1)} %bitcast.15), custom_call_target="tpu_custom_call" | custom-call | bytes 4194304 | tf_op jit(solution)/shard_map/pack/pallas_call | solution.py:170
  24.0 7.7 %all-to-all-done = bf16[32,16,128]{2,1,0:T(8,128)(2,1)S(1)} async-done(((bf16[32,16,128]{2,1,0:T(8,128)(2,1)}), bf16[32,16,128]{2,1,0:T(8,128)(2,1)S(1)}, u32[]{:S(2)}, u32[]{:S(2)}) %all-to-all-start) | async-done | bytes 131104 | tf_op jit(solution)/shard_map/all_to_all | solution.py:183
  31.7 4.0 %all-to-all-start.1 = ((bf16[4,192,1536]{2,1,0:T(8,128)(2,1)}), bf16[4,192,1536]{2,1,0:T(8,128)(2,1)S(1)}, u32[]{:S(2)}, u32[]{:S(2)}) async-start(bf16[4,192,1536]{2,1,0:T(8,128)(2,1)} %pack.1), calls=%async_computation.1 | async-start | bytes 4718592 | tf_op jit(solution)/shard_map/all_to_all | solution.py:179
  35.7 56.0 %all_gather.3.own_ref.refs_0_ = bf16[4,512,128]{2,1,0:T(8,128)(2,1)S(1)} all-gather(bf16[1,512,128]{2,1,0:T(8,128)(2,1)S(1)} %bitcast.19), channel_id=1, replica_groups={{0,8,16,24},{1,9,17,25},{2,10,18,26},{3,11,19,27},{4,12,20,28},{5,13,21..., dimensions={0}, use_global_device_ids=true | all-gather | bytes 655360 | tf_op jit(solution)/shard_map/all_gather | solution.py:186
  91.8 4.5 %collective-permute-start = (bf16[4,512,128]{2,1,0:T(8,128)(2,1)S(1)}, bf16[4,512,128]{2,1,0:T(8,128)(2,1)S(1)}, u32[]{:S(2)}, u32[]{:S(2)}) collective-permute-start(bf16[4,512,128]{2,1,0:T(8,128)(2,1)S(1)} %all_gather.3.own_ref.refs_0_), channel_id=1, source_target_pairs={{0,1},{1,0},{2,3},{3,2},{4,5},{5,4},{6,7},{7,6},{8,9},{9,8},{10,11... | collective-permute-start | bytes 1572872 | tf_op jit(solution)/shard_map/ppermute | solution.py:187
  96.3 0.1 pad_add_fusion.at_ref
  96.4 1.4 collective-permute-done.other_ref.refs_0_
  97.8 0.0 all-to-all-done.1
  97.8 2.3 %slots.1 = f32[32,1,16]{2,1,0:T(1,128)} custom-call(s32[2]{0:T(128)S(1)} %pad_add_fusion.at_ref, bf16[4,512,128]{2,1,0:T(8,128)(2,1)S(1)} %all_gather.3.own_ref.refs_0_, bf16[4,512,128]{2,1,0:T(8,128)(2,1)S(1)} %collective-permute-done.other_ref.refs_0_, bf16[768,1536]{1,0:T(8,128)(2,1)S(1)} %bitcast.14), custom_call_target="tpu_custom_call" | custom-call | flops 805306368 | bytes 6291456 | tf_op jit(solution)/shard_map/slots/pallas_call | solution.py:189
  100.1 8.1 %all-to-all-start.2 = ((f32[32,1,16]{2,1,0:T(1,128)}), f32[32,1,16]{2,1,0:T(1,128)S(1)}, u32[]{:S(2)}, u32[]{:S(2)}) async-start(f32[32,1,16]{2,1,0:T(1,128)} %slots.1), calls=%async_computation.2 | async-start | bytes 32768 | tf_op jit(solution)/shard_map/all_to_all | solution.py:198
  108.1 5.3 %collective-permute-start.3 = (bf16[4,512,128]{2,1,0:T(8,128)(2,1)S(1)}, bf16[4,512,128]{2,1,0:T(8,128)(2,1)}, u32[]{:S(2)}, u32[]{:S(2)}) collective-permute-start(bf16[4,512,128]{2,1,0:T(8,128)(2,1)S(1)} %all_gather.3.own_ref.refs_0_), channel_id=1, source_target_pairs={{0,6},{1,7},{2,0},{3,1},{4,2},{5,3},{6,4},{7,5},{8,14},{9,15},{10,... | collective-permute-start | bytes 1572872 | tf_op jit(solution)/shard_map/ppermute | solution.py:211
  113.4 2.5 %collective-permute-start.2 = (bf16[4,512,128]{2,1,0:T(8,128)(2,1)S(1)}, bf16[4,512,128]{2,1,0:T(8,128)(2,1)}, u32[]{:S(2)}, u32[]{:S(2)}) collective-permute-start(bf16[4,512,128]{2,1,0:T(8,128)(2,1)S(1)} %all_gather.3.own_ref.refs_0_), channel_id=1, source_target_pairs={{0,4},{1,5},{2,6},{3,7},{4,0},{5,1},{6,2},{7,3},{8,12},{9,13},{10,... | collective-permute-start | bytes 1572872 | tf_op jit(solution)/shard_map/ppermute | solution.py:211
  115.9 2.5 %collective-permute-start.1 = (bf16[4,512,128]{2,1,0:T(8,128)(2,1)S(1)}, bf16[4,512,128]{2,1,0:T(8,128)(2,1)}, u32[]{:S(2)}, u32[]{:S(2)}) collective-permute-start(bf16[4,512,128]{2,1,0:T(8,128)(2,1)S(1)} %all_gather.3.own_ref.refs_0_), channel_id=1, source_target_pairs={{0,2},{1,3},{2,4},{3,5},{4,6},{5,7},{6,0},{7,1},{8,10},{9,11},{10,... | collective-permute-start | bytes 1572872 | tf_op jit(solution)/shard_map/ppermute | solution.py:211
  118.4 1.0 all-to-all-done.2.sums_ref
  119.4 0.0 copy-start.1
  119.4 0.9 turn.1
  120.3 16.6 %all-to-all-start.3 = ((f32[32,1,256]{2,1,0:T(1,128)}), f32[32,1,256]{2,1,0:T(1,128)S(1)}, u32[]{:S(2)}, u32[]{:S(2)}) async-start(f32[32,1,256]{2,1,0:T(1,128)} %turn.1), calls=%async_computation.3 | async-start | bytes 65536 | tf_op jit(solution)/shard_map/all_to_all | solution.py:208
  136.9 0.0 collective-permute-done.3.refs_3_
  136.9 2.1 %collective-permute-start.6 = (bf16[4,512,128]{2,1,0:T(8,128)(2,1)}, bf16[4,512,128]{2,1,0:T(8,128)(2,1)}, u32[]{:S(2)}, u32[]{:S(2)}) collective-permute-start(bf16[4,512,128]{2,1,0:T(8,128)(2,1)} %collective-permute-done.3.refs_3_), channel_id=1, source_target_pairs={{0,1},{1,0},{2,3},{3,2},{4,5},{5,4},{6,7},{7,6},{8,9},{9,8},{10,11... | collective-permute-start | bytes 1572872 | tf_op jit(solution)/shard_map/ppermute | solution.py:219
  139.0 0.0 collective-permute-done.2.refs_2_
  139.1 2.2 %collective-permute-start.5 = (bf16[4,512,128]{2,1,0:T(8,128)(2,1)}, bf16[4,512,128]{2,1,0:T(8,128)(2,1)}, u32[]{:S(2)}, u32[]{:S(2)}) collective-permute-start(bf16[4,512,128]{2,1,0:T(8,128)(2,1)} %collective-permute-done.2.refs_2_), channel_id=1, source_target_pairs={{0,1},{1,0},{2,3},{3,2},{4,5},{5,4},{6,7},{7,6},{8,9},{9,8},{10,11... | collective-permute-start | bytes 1572872 | tf_op jit(solution)/shard_map/ppermute | solution.py:219
  141.2 0.8 collective-permute-done.1.refs_1_
  142.0 2.4 %collective-permute-start.4 = (bf16[4,512,128]{2,1,0:T(8,128)(2,1)}, bf16[4,512,128]{2,1,0:T(8,128)(2,1)}, u32[]{:S(2)}, u32[]{:S(2)}) collective-permute-start(bf16[4,512,128]{2,1,0:T(8,128)(2,1)} %collective-permute-done.1.refs_1_), channel_id=1, source_target_pairs={{0,1},{1,0},{2,3},{3,2},{4,5},{5,4},{6,7},{7,6},{8,9},{9,8},{10,11... | collective-permute-start | bytes 1572872 | tf_op jit(solution)/shard_map/ppermute | solution.py:219
  144.4 0.0 copy-done.1
  144.4 0.0 copy-done.3
  144.4 3.1 %own.1 = (f32[192,512]{1,0:T(8,128)S(1)}, bf16[192,2048]{1,0:T(8,128)(2,1)S(1)}) custom-call(s32[2]{0:T(128)S(1)} %pad_add_fusion.at_ref, bf16[192,4096]{1,0:T(8,128)(2,1)S(1)} %bitcast.12, bf16[512,192]{1,0:T(8,128)(2,1)S(1)} %bitcast.16, bf16[4,512,128]{2,1,0:T(8,128)(2,1)S(1)} %all_gather.3.own_ref.refs_0_, ...), custom_call_target="tpu_custom_call" | custom-call | flops 1000 | bytes 1000 | tf_op jit(solution)/shard_map/own/pallas_call | solution.py:222
  147.5 0.0 copy-start.4
  147.5 0.9 copy-done.4
  148.4 0.7 copy-done.6
  149.1 11.9 %all-to-all-done.3.sums_ref = f32[32,1,256]{2,1,0:T(1,128)S(1)} async-done(((f32[32,1,256]{2,1,0:T(1,128)}), f32[32,1,256]{2,1,0:T(1,128)S(1)}, u32[]{:S(2)}, u32[]{:S(2)}) %all-to-all-start.3) | async-done | bytes 32800 | tf_op jit(solution)/shard_map/all_to_all | solution.py:208
  161.0 0.6 gate.1
  161.6 0.0 collective-permute-done.6.refs_3_
  161.6 0.0 collective-permute-done.5.refs_2_
  161.6 0.0 collective-permute-done.4.refs_1_
  161.6 0.5 copy-done.5
  162.1 0.1 copy-done.7
  162.2 4.3 %other.1 = (bf16[512,192]{1,0:T(8,128)(2,1)}, bf16[192,4096]{1,0:T(8,128)(2,1)}) custom-call(s32[2]{0:T(128)S(1)} %pad_add_fusion.at_ref, bf16[192,4096]{1,0:T(8,128)(2,1)S(1)} %bitcast.13, bf16[512,192]{1,0:T(8,128)(2,1)S(1)} %bitcast.17, f32[192,512]{1,0:T(8,128)S(1)} %copy-done.7, bf16[192,2048]{1,0:T(8,128)(2,1)S(1)} %copy-done.5, ...), custom_call_target="tpu_custom_call" | custom-call | flops 1000 | bytes 1000 | tf_op jit(solution)/shard_map/other/pallas_call | solution.py:235
  (4 shorter events, 0.0 us)
Async XLA Ops:
  1.3 0.8 copy-start.8
  2.1 0.7 copy-start.9
  3.9 27.9 %all-to-all-start = ((bf16[32,16,128]{2,1,0:T(8,128)(2,1)}), bf16[32,16,128]{2,1,0:T(8,128)(2,1)S(1)}, u32[]{:S(2)}, u32[]{:S(2)}) async-start(bf16[32,16,128]{2,1,0:T(8,128)(2,1)} %bitcast.5), calls=%async_computation | async-start | bytes 262144 | tf_op jit(solution)/shard_map/all_to_all | solution.py:183
  20.0 1.4 copy-start
  21.4 0.9 copy-start.2
  31.7 66.1 %all-to-all-start.1 = ((bf16[4,192,1536]{2,1,0:T(8,128)(2,1)}), bf16[4,192,1536]{2,1,0:T(8,128)(2,1)S(1)}, u32[]{:S(2)}, u32[]{:S(2)}) async-start(bf16[4,192,1536]{2,1,0:T(8,128)(2,1)} %pack.1), calls=%async_computation.1 | async-start | bytes 4718592 | tf_op jit(solution)/shard_map/all_to_all | solution.py:179
  91.8 6.0 %collective-permute-start = (bf16[4,512,128]{2,1,0:T(8,128)(2,1)S(1)}, bf16[4,512,128]{2,1,0:T(8,128)(2,1)S(1)}, u32[]{:S(2)}, u32[]{:S(2)}) collective-permute-start(bf16[4,512,128]{2,1,0:T(8,128)(2,1)S(1)} %all_gather.3.own_ref.refs_0_), channel_id=1, source_target_pairs={{0,1},{1,0},{2,3},{3,2},{4,5},{5,4},{6,7},{7,6},{8,9},{9,8},{10,11... | collective-permute-start | bytes 1572872 | tf_op jit(solution)/shard_map/ppermute | solution.py:187
  100.1 19.3 %all-to-all-start.2 = ((f32[32,1,16]{2,1,0:T(1,128)}), f32[32,1,16]{2,1,0:T(1,128)S(1)}, u32[]{:S(2)}, u32[]{:S(2)}) async-start(f32[32,1,16]{2,1,0:T(1,128)} %slots.1), calls=%async_computation.2 | async-start | bytes 32768 | tf_op jit(solution)/shard_map/all_to_all | solution.py:198
  108.1 28.8 %collective-permute-start.3 = (bf16[4,512,128]{2,1,0:T(8,128)(2,1)S(1)}, bf16[4,512,128]{2,1,0:T(8,128)(2,1)}, u32[]{:S(2)}, u32[]{:S(2)}) collective-permute-start(bf16[4,512,128]{2,1,0:T(8,128)(2,1)S(1)} %all_gather.3.own_ref.refs_0_), channel_id=1, source_target_pairs={{0,6},{1,7},{2,0},{3,1},{4,2},{5,3},{6,4},{7,5},{8,14},{9,15},{10,... | collective-permute-start | bytes 1572872 | tf_op jit(solution)/shard_map/ppermute | solution.py:211
  113.4 25.7 %collective-permute-start.2 = (bf16[4,512,128]{2,1,0:T(8,128)(2,1)S(1)}, bf16[4,512,128]{2,1,0:T(8,128)(2,1)}, u32[]{:S(2)}, u32[]{:S(2)}) collective-permute-start(bf16[4,512,128]{2,1,0:T(8,128)(2,1)S(1)} %all_gather.3.own_ref.refs_0_), channel_id=1, source_target_pairs={{0,4},{1,5},{2,6},{3,7},{4,0},{5,1},{6,2},{7,3},{8,12},{9,13},{10,... | collective-permute-start | bytes 1572872 | tf_op jit(solution)/shard_map/ppermute | solution.py:211
  115.9 26.1 %collective-permute-start.1 = (bf16[4,512,128]{2,1,0:T(8,128)(2,1)S(1)}, bf16[4,512,128]{2,1,0:T(8,128)(2,1)}, u32[]{:S(2)}, u32[]{:S(2)}) collective-permute-start(bf16[4,512,128]{2,1,0:T(8,128)(2,1)S(1)} %all_gather.3.own_ref.refs_0_), channel_id=1, source_target_pairs={{0,2},{1,3},{2,4},{3,5},{4,6},{5,7},{6,0},{7,1},{8,10},{9,11},{10,... | collective-permute-start | bytes 1572872 | tf_op jit(solution)/shard_map/ppermute | solution.py:211
  119.4 25.0 %copy-start.1 = (bf16[1,192,4096]{2,1,0:T(8,128)(2,1)S(1)}, bf16[1,192,4096]{2,1,0:T(8,128)(2,1)}, u32[]{:S(2)}) copy-start(bf16[1,192,4096]{2,1,0:T(8,128)(2,1)} %param.9) | copy-start | bytes 4718596
  119.4 25.1 %copy-start.3 = (bf16[1,32,16,192]{3,2,1,0:T(8,128)(2,1)S(1)}, bf16[1,32,16,192]{3,2,1,0:T(8,128)(2,1)}, u32[]{:S(2)}) copy-start(bf16[1,32,16,192]{3,2,1,0:T(8,128)(2,1)} %param.8) | copy-start | bytes 589828
  120.3 40.7 %all-to-all-start.3 = ((f32[32,1,256]{2,1,0:T(1,128)}), f32[32,1,256]{2,1,0:T(1,128)S(1)}, u32[]{:S(2)}, u32[]{:S(2)}) async-start(f32[32,1,256]{2,1,0:T(1,128)} %turn.1), calls=%async_computation.3 | async-start | bytes 65536 | tf_op jit(solution)/shard_map/all_to_all | solution.py:208
  136.9 24.7 %collective-permute-start.6 = (bf16[4,512,128]{2,1,0:T(8,128)(2,1)}, bf16[4,512,128]{2,1,0:T(8,128)(2,1)}, u32[]{:S(2)}, u32[]{:S(2)}) collective-permute-start(bf16[4,512,128]{2,1,0:T(8,128)(2,1)} %collective-permute-done.3.refs_3_), channel_id=1, source_target_pairs={{0,1},{1,0},{2,3},{3,2},{4,5},{5,4},{6,7},{7,6},{8,9},{9,8},{10,11... | collective-permute-start | bytes 1572872 | tf_op jit(solution)/shard_map/ppermute | solution.py:219
  139.1 22.6 %collective-permute-start.5 = (bf16[4,512,128]{2,1,0:T(8,128)(2,1)}, bf16[4,512,128]{2,1,0:T(8,128)(2,1)}, u32[]{:S(2)}, u32[]{:S(2)}) collective-permute-start(bf16[4,512,128]{2,1,0:T(8,128)(2,1)} %collective-permute-done.2.refs_2_), channel_id=1, source_target_pairs={{0,1},{1,0},{2,3},{3,2},{4,5},{5,4},{6,7},{7,6},{8,9},{9,8},{10,11... | collective-permute-start | bytes 1572872 | tf_op jit(solution)/shard_map/ppermute | solution.py:219
  142.0 19.6 %collective-permute-start.4 = (bf16[4,512,128]{2,1,0:T(8,128)(2,1)}, bf16[4,512,128]{2,1,0:T(8,128)(2,1)}, u32[]{:S(2)}, u32[]{:S(2)}) collective-permute-start(bf16[4,512,128]{2,1,0:T(8,128)(2,1)} %collective-permute-done.1.refs_1_), channel_id=1, source_target_pairs={{0,1},{1,0},{2,3},{3,2},{4,5},{5,4},{6,7},{7,6},{8,9},{9,8},{10,11... | collective-permute-start | bytes 1572872 | tf_op jit(solution)/shard_map/ppermute | solution.py:219
  147.5 0.9 copy-start.4
  148.4 0.7 copy-start.6
  161.0 1.1 copy-start.5
  161.0 1.2 copy-start.7

commit v8 on v6

--- a/solution.py
+++ b/solution.py
@@ -57,12 +57,6 @@
         out_ref[x, :, 1024:] = saved
 
 
-def both_cores(at_ref, own_ref, other_ref):
-    for rows, side in ((own_ref, at_ref[1]), (other_ref, 1 - at_ref[1])):
-        for hi in range(4):
-            yield rows[hi], pl.multiple_of(hi * 256 + side * 128, 128)
-
-
 def product(left_ref, first_row, count, blocks):
     return lax.dot_general(
         jnp.concatenate(
@@ -74,10 +68,20 @@
     )
 
 
-def slots_kernel(at_ref, own_ref, other_ref, swap_ref, out_ref):
-    blocks = list(both_cores(at_ref, own_ref, other_ref))
+def slot_sums(rows_ref, side, swap_ref):
+    blocks = [
+        (rows_ref[hi], pl.multiple_of(hi * 256 + side * 128, 128)) for hi in range(4)
+    ]
     total = product(swap_ref, 0, 768, blocks)
-    sums = jnp.sum(total * swap_ref[:, 1024:].astype(jnp.float32), axis=0, keepdims=True)
+    return jnp.sum(total * swap_ref[:, 1024:].astype(jnp.float32), axis=0, keepdims=True)
+
+
+def own_slots_kernel(at_ref, rows_ref, swap_ref, out_ref):
+    out_ref[...] = slot_sums(rows_ref, at_ref[1], swap_ref)
+
+
+def slots_kernel(at_ref, rows_ref, swap_ref, own_ref, out_ref):
+    sums = own_ref[...] + slot_sums(rows_ref, 1 - at_ref[1], swap_ref)
     for y in range(4):
         for i in range(8):
             out_ref[y * 8 + i] = sums[:, y * 128 : y * 128 + 128]
@@ -96,48 +100,42 @@
             out_ref[hi * 8 + lo] = line
 
 
-def half_results(at_ref, side, w_ref, saved_ref, row_refs, write):
+def some_results(at_ref, w_ref, saved_ref, parts, weight_ref, held, sems):
     left = saved_ref[...].T
-    blocks = []
-    for k in range(4):
-        source = lax.rem(at_ref[0] + 4 - k, 4)
-        some = [
-            (row_refs[k][hi], pl.multiple_of((hi * 4 + source) * 256 + side * 128, 128))
-            for hi in range(4)
-        ]
-        for hi, (rows, _) in enumerate(some):
-            write(k, hi, source, left, rows)
-        blocks += some
-    return product(w_ref, 0, 192, blocks)
-
-
-def own_kernel(at_ref, w_ref, saved_ref, *refs):
-    *row_refs, sums_ref, part_ref = refs
-
-    def write(k, hi, source, left, rows):
-        first = pl.multiple_of((hi * 4 + source) * 128, 128)
-        part_ref[:, pl.ds(first, 128)] = jnp.dot(
-            left, rows, preferred_element_type=jnp.float32
-        ).astype(jnp.bfloat16)
-
-    sums_ref[...] = half_results(at_ref, at_ref[1], w_ref, saved_ref, row_refs, write)
-
-
-def other_kernel(at_ref, w_ref, saved_ref, sums_ref, part_ref, *refs):
-    *row_refs, hidden_ref, weight_ref = refs
+    blocks, copies = [], []
+    for row_ref, back, side in parts:
+        source = lax.rem(at_ref[0] + 4 - back, 4)
+        for hi in range(4):
+            rows = row_ref[hi]
+            first = pl.multiple_of((hi * 4 + source) * 256 + side * 128, 128)
+            i = len(blocks)
+            held[i] = jnp.dot(left, rows, preferred_element_type=jnp.float32).astype(jnp.bfloat16)
+            copy = pltpu.make_async_copy(
+                held.at[i], weight_ref.at[:, pl.ds(first, 128)], sems.at[i]
+            )
+            copy.start()
+            blocks.append((rows, first))
+            copies.append(copy)
+    return product(w_ref, 0, 192, blocks), copies
+
+
+def own_kernel(at_ref, w_ref, saved_ref, r0, r1, r2, r3, o0, sums_ref, weight_ref, held, sems):
     core = at_ref[1]
-
-    def write(k, hi, source, left, rows):
-        first = (hi * 4 + source) * 128
-        weight_ref[:, pl.ds(pl.multiple_of(2 * first + core * 128, 128), 128)] = part_ref[
-            :, pl.ds(pl.multiple_of(first, 128), 128)
-        ]
-        weight_ref[:, pl.ds(pl.multiple_of(2 * first + (1 - core) * 128, 128), 128)] = jnp.dot(
-            left, rows, preferred_element_type=jnp.float32
-        ).astype(jnp.bfloat16)
-
-    total = sums_ref[...] + half_results(at_ref, 1 - core, w_ref, saved_ref, row_refs, write)
-    hidden_ref[...] = total.T.astype(jnp.bfloat16)
+    parts = [(r0, 0, core), (o0, 0, 1 - core), (r1, 1, core), (r2, 2, core), (r3, 3, core)]
+    sums_ref[...], copies = some_results(at_ref, w_ref, saved_ref, parts, weight_ref, held, sems)
+    for copy in copies:
+        copy.wait()
+
+
+def other_kernel(
+    at_ref, w_ref, saved_ref, sums_ref, o1, o2, o3, started_ref, hidden_ref, weight_ref, held, sems
+):
+    side = 1 - at_ref[1]
+    parts = [(o1, 1, side), (o2, 2, side), (o3, 3, side)]
+    total, copies = some_results(at_ref, w_ref, saved_ref, parts, weight_ref, held, sems)
+    hidden_ref[...] = (sums_ref[...] + total).T.astype(jnp.bfloat16)
+    for copy in copies:
+        copy.wait()
 
 
 def gate_kernel(sums_ref, target_ref, gate_ref, out_ref):
@@ -198,17 +196,26 @@
     own = lax.all_gather(arrived, BOTH, axis=0, tiled=False, axis_index_groups=groups("hi"))
     other = lax.ppermute(own, "replica", [(i, i ^ 1) for i in range(32)])
 
-    slot_sums = pl.pallas_call(
+    own_sums = pl.pallas_call(
+        own_slots_kernel,
+        out_shape=jax.ShapeDtypeStruct((1, slot_total), jnp.float32),
+        in_specs=[smem, vmem, vmem],
+        out_specs=vmem,
+        compiler_params=params,
+        cost_estimate=cost,
+        name="own_slots",
+    )(at, own, swapped)
+    plane_sums = pl.pallas_call(
         slots_kernel,
         out_shape=jax.ShapeDtypeStruct((32, 1, 128), jnp.float32),
-        in_specs=[smem, vmem, vmem, vmem],
+        in_specs=[smem] + [vmem] * 3,
         out_specs=vmem,
         compiler_params=params,
         cost_estimate=cost,
         name="slots",
-    )(at, own, other, swapped)
+    )(at, other, swapped, own_sums)
     from_plane = lax.all_to_all(
-        slot_sums, BOTH, 0, 0, tiled=True, axis_index_groups=groups("y", "x", "core")
+        plane_sums, BOTH, 0, 0, tiled=True, axis_index_groups=groups("y", "x", "core")
     )
     to_z = pl.pallas_call(
         turn_kernel,
@@ -222,7 +229,7 @@
     from_z = lax.all_to_all(
         to_z, BOTH, 0, 0, tiled=True, axis_index_groups=groups("hi", "lo")
     )
-    going, _ = lax.optimization_barrier((own, slot_sums))
+    going, _ = lax.optimization_barrier((own, plane_sums))
     own_rows = [own] + [
         lax.ppermute(
             going,
@@ -235,38 +242,46 @@
         lax.ppermute(rows, "replica", [(i, i ^ 1) for i in range(32)]) for rows in own_rows[1:]
     ]
     small = pl.CostEstimate(flops=1000, bytes_accessed=1000, transcendentals=0)
-    sums, part = pl.pallas_call(
+    hbm = pl.BlockSpec(memory_space=pl.ANY)
+    sums, weight_part = pl.pallas_call(
         own_kernel,
         out_shape=(
             jax.ShapeDtypeStruct((192, slot_total), jnp.float32),
-            jax.ShapeDtypeStruct((192, 2048), jnp.bfloat16),
+            jax.ShapeDtypeStruct(weight.shape, jnp.bfloat16),
         ),
-        in_specs=[smem] + [vmem] * 6,
-        out_specs=(vmem, vmem),
+        in_specs=[smem] + [vmem] * 7,
+        out_specs=(vmem, hbm),
+        scratch_shapes=[
+            pltpu.VMEM((20, 192, 128), jnp.bfloat16), pltpu.SemaphoreType.DMA((20,))
+        ],
         compiler_params=params,
         cost_estimate=small,
         name="own",
-    )(at, weight, saved, *own_rows)
-    from_z, sums, part = lax.optimization_barrier((from_z, sums, part))
+    )(at, weight, saved, *own_rows, other)
+    from_z, sums, weight_part = lax.optimization_barrier((from_z, sums, weight_part))
     hidden_out, weight_out = pl.pallas_call(
         other_kernel,
         out_shape=(
             jax.ShapeDtypeStruct(saved.shape, jnp.bfloat16),
             jax.ShapeDtypeStruct(weight.shape, jnp.bfloat16),
         ),
-        in_specs=[smem] + [vmem] * 8,
-        out_specs=(vmem, vmem),
+        in_specs=[smem] + [vmem] * 6 + [hbm],
+        out_specs=(vmem, hbm),
+        input_output_aliases={7: 1},
+        scratch_shapes=[
+            pltpu.VMEM((12, 192, 128), jnp.bfloat16), pltpu.SemaphoreType.DMA((12,))
+        ],
         compiler_params=params,
         cost_estimate=small,
         name="other",
-    )(at, weight, saved, sums, part, *other_rows)
+    )(at, weight, saved, sums, *other_rows[1:], weight_part)
     grad_gate = pl.pallas_call(
         gate_kernel,
         out_shape=jax.ShapeDtypeStruct((1, 256), jnp.float32),
         in_specs=[vmem] * 3,
         out_specs=vmem,
         compiler_params=params,
-        cost_estimate=pl.CostEstimate(flops=int(5.5e+09), bytes_accessed=1000, transcendentals=0),
+        cost_estimate=pl.CostEstimate(flops=int(5e+09), bytes_accessed=1000, transcendentals=0),
         name="gate",
     )(from_z, target, gate_row)
     return (hidden_out.reshape(hidden_saved.shape), weight_out[None], grad_gate.reshape(256))

time: 158 us -> 158 us (level)
  starting transfers between devices: 60.4 us -> 62.5 us
  waiting for transfers between devices: 18 us -> 16.2 us
    ppermute x3, waiting for transfers between devices: 6.13 us -> 2.29 us  [per_device(): lax.ppermute(going, 'replica', [(i, i // 8 * 8 + (i % 8 // 2 + k) % 4 * 2...]
    all_to_all x1, waiting for transfers between devices: 2.74 us -> 5.88 us  [per_device(): lax.all_to_all(to_z, BOTH, 0, 0, tiled=True, axis_index_groups=groups('hi...]
    unnamed x20 -> x16, local copies, waits for them, and re-layouts: 5.88 us -> 4.78 us
  transfers between devices with their start and end apart: 11 -> 11, of which waited for: 5 -> 4; matrix products, arithmetic and copies ran while one was open for 0% -> 0% of each run, Pallas kernels for 4% -> 5%
where the time goes in v8:
time: 158 us; the launch traced here: 156 us
  starting transfers between devices  62.5 us (40%)
  blocking collectives  56 us (35%)
  waiting for transfers between devices  16.2 us (10%)
  Pallas kernels  15.1 us (10%)
  local copies, waits for them, and re-layouts  5.44 us (3%)
    all_gather x1, blocking collectives, per_device(): lax.all_gather(arrived, BOTH, axis=0, tiled=False, axis_index_groups=grou...  56 us
    all_to_all x1, starting transfers between devices, per_device(): lax.all_to_all(outgoing.reshape(experts, slot_count, -1), 'expert', 0, 0,...  16.1 us
    all_to_all x1, starting transfers between devices, per_device(): lax.all_to_all(to_z, BOTH, 0, 0, tiled=True, axis_index_groups=groups('hi...  11.6 us
    ppermute x3, starting transfers between devices, per_device(): lax.ppermute(going, 'replica', [(i, i // 8 * 8 + (i % 8 // 2 + k) % 4 * 2...  10.8 us
    ppermute x3, starting transfers between devices, per_device(): lax.ppermute(rows, 'replica', [(i, i ^ 1) for i in range(32)])  8.4 us
    all_to_all x1, waiting for transfers between devices, per_device(): lax.all_to_all(outgoing.reshape(experts, slot_count, -1), 'expert', 0, 0,...  7.75 us
    all_to_all x1, starting transfers between devices, per_device(): lax.all_to_all(plane_sums, BOTH, 0, 0, tiled=True, axis_index_groups=grou...  7.04 us
    all_to_all x1, waiting for transfers between devices, per_device(): lax.all_to_all(to_z, BOTH, 0, 0, tiled=True, axis_index_groups=groups('hi...  5.88 us
  transfers between devices with their start and end apart: 11, of which 4 were waited for; matrix products, arithmetic and copies ran while one was open for 0% of the time, Pallas kernels for 5%

profile of v8, /device:TPU:1, one launch (start us, length us, event | category | flops | bytes accessed | tf_op | source)
XLA Modules:
  0.0 156.0 jit_solution(7193744771983040015)
XLA Ops:
  0.6 0.7 reshape.29.gate_ref
  1.3 0.0 copy-start.6
  1.3 0.8 copy-done.6
  2.1 0.0 copy-start.7
  2.1 0.7 copy-done.7
  2.8 1.0 place.1
  3.9 16.1 %all-to-all-start = ((bf16[32,16,128]{2,1,0:T(8,128)(2,1)}), bf16[32,16,128]{2,1,0:T(8,128)(2,1)S(1)}, u32[]{:S(2)}, u32[]{:S(2)}) async-start(bf16[32,16,128]{2,1,0:T(8,128)(2,1)} %bitcast.5), calls=%async_computation | async-start | bytes 262144 | tf_op jit(solution)/shard_map/all_to_all | solution.py:193
  20.0 0.0 copy-start
  20.0 1.4 copy-done
  21.4 0.0 copy-start.2
  21.4 0.9 copy-done.2
  22.3 1.7 %pack.1 = bf16[4,192,1536]{2,1,0:T(8,128)(2,1)} custom-call(bf16[192,4096]{1,0:T(8,128)(2,1)S(1)} %bitcast.11, bf16[512,192]{1,0:T(8,128)(2,1)S(1)} %bitcast.14), custom_call_target="tpu_custom_call" | custom-call | bytes 4194304 | tf_op jit(solution)/shard_map/pack/pallas_call | solution.py:180
  24.0 7.7 %all-to-all-done = bf16[32,16,128]{2,1,0:T(8,128)(2,1)S(1)} async-done(((bf16[32,16,128]{2,1,0:T(8,128)(2,1)}), bf16[32,16,128]{2,1,0:T(8,128)(2,1)S(1)}, u32[]{:S(2)}, u32[]{:S(2)}) %all-to-all-start) | async-done | bytes 131104 | tf_op jit(solution)/shard_map/all_to_all | solution.py:193
  31.7 4.0 %all-to-all-start.1 = ((bf16[4,192,1536]{2,1,0:T(8,128)(2,1)}), bf16[4,192,1536]{2,1,0:T(8,128)(2,1)S(1)}, u32[]{:S(2)}, u32[]{:S(2)}) async-start(bf16[4,192,1536]{2,1,0:T(8,128)(2,1)} %pack.1), calls=%async_computation.1 | async-start | bytes 4718592 | tf_op jit(solution)/shard_map/all_to_all | solution.py:189
  35.7 56.0 %all_gather.3.rows_ref.r0 = bf16[4,512,128]{2,1,0:T(8,128)(2,1)S(1)} all-gather(bf16[1,512,128]{2,1,0:T(8,128)(2,1)S(1)} %bitcast.21), channel_id=1, replica_groups={{0,8,16,24},{1,9,17,25},{2,10,18,26},{3,11,19,27},{4,12,20,28},{5,13,21..., dimensions={0}, use_global_device_ids=true | all-gather | bytes 655360 | tf_op jit(solution)/shard_map/all_gather | solution.py:196
  91.8 4.5 %collective-permute-start = (bf16[4,512,128]{2,1,0:T(8,128)(2,1)S(1)}, bf16[4,512,128]{2,1,0:T(8,128)(2,1)S(1)}, u32[]{:S(2)}, u32[]{:S(2)}) collective-permute-start(bf16[4,512,128]{2,1,0:T(8,128)(2,1)S(1)} %all_gather.3.rows_ref.r0), channel_id=1, source_target_pairs={{0,1},{1,0},{2,3},{3,2},{4,5},{5,4},{6,7},{7,6},{8,9},{9,8},{10,11... | collective-permute-start | bytes 1572872 | tf_op jit(solution)/shard_map/ppermute | solution.py:197
  96.3 0.1 pad_add_fusion.at_ref
  96.4 0.0 all-to-all-done.1
  96.4 1.2 own_slots.1.own_ref
  97.5 0.2 collective-permute-done.rows_ref.o0
  97.8 1.8 %slots.1 = f32[32,1,128]{2,1,0:T(1,128)} custom-call(s32[2]{0:T(128)S(1)} %pad_add_fusion.at_ref, bf16[4,512,128]{2,1,0:T(8,128)(2,1)S(1)} %collective-permute-done.rows_ref.o0, bf16[768,1536]{1,0:T(8,128)(2,1)S(1)} %bitcast.18, f32[1,512]{1,0:T(1,128)S(1)} %own_slots.1.own_ref), custom_call_target="tpu_custom_call" | custom-call | flops 805306368 | bytes 6291456 | tf_op jit(solution)/shard_map/slots/pallas_call | solution.py:208
  99.6 7.0 %all-to-all-start.2 = ((f32[32,1,128]{2,1,0:T(1,128)}), f32[32,1,128]{2,1,0:T(1,128)S(1)}, u32[]{:S(2)}, u32[]{:S(2)}) async-start(f32[32,1,128]{2,1,0:T(1,128)} %slots.1), calls=%async_computation.2 | async-start | bytes 32768 | tf_op jit(solution)/shard_map/all_to_all | solution.py:217
  106.6 0.0 copy-start.1
  106.6 0.0 copy-start.3
  106.6 3.4 %collective-permute-start.1 = (bf16[4,512,128]{2,1,0:T(8,128)(2,1)S(1)}, bf16[4,512,128]{2,1,0:T(8,128)(2,1)S(1)}, u32[]{:S(2)}, u32[]{:S(2)}) collective-permute-start(bf16[4,512,128]{2,1,0:T(8,128)(2,1)S(1)} %all_gather.3.rows_ref.r0), channel_id=1, source_target_pairs={{0,2},{1,3},{2,4},{3,5},{4,6},{5,7},{6,0},{7,1},{8,10},{9,11},{10,... | collective-permute-start | bytes 1572872 | tf_op jit(solution)/shard_map/ppermute | solution.py:234
  110.1 4.3 %collective-permute-start.2 = (bf16[4,512,128]{2,1,0:T(8,128)(2,1)S(1)}, bf16[4,512,128]{2,1,0:T(8,128)(2,1)}, u32[]{:S(2)}, u32[]{:S(2)}) collective-permute-start(bf16[4,512,128]{2,1,0:T(8,128)(2,1)S(1)} %all_gather.3.rows_ref.r0), channel_id=1, source_target_pairs={{0,4},{1,5},{2,6},{3,7},{4,0},{5,1},{6,2},{7,3},{8,12},{9,13},{10,... | collective-permute-start | bytes 1572872 | tf_op jit(solution)/shard_map/ppermute | solution.py:234
  114.4 3.1 %collective-permute-start.3 = (bf16[4,512,128]{2,1,0:T(8,128)(2,1)S(1)}, bf16[4,512,128]{2,1,0:T(8,128)(2,1)}, u32[]{:S(2)}, u32[]{:S(2)}) collective-permute-start(bf16[4,512,128]{2,1,0:T(8,128)(2,1)S(1)} %all_gather.3.rows_ref.r0), channel_id=1, source_target_pairs={{0,6},{1,7},{2,0},{3,1},{4,2},{5,3},{6,4},{7,5},{8,14},{9,15},{10,... | collective-permute-start | bytes 1572872 | tf_op jit(solution)/shard_map/ppermute | solution.py:234
  117.5 0.0 all-to-all-done.2.sums_ref
  117.5 0.7 turn.1
  118.2 11.6 %all-to-all-start.3 = ((f32[32,1,64]{2,1,0:T(1,128)}), f32[32,1,64]{2,1,0:T(1,128)S(1)}, u32[]{:S(2)}, u32[]{:S(2)}) async-start(f32[32,1,64]{2,1,0:T(1,128)} %turn.1), calls=%async_computation.3 | async-start | bytes 32768 | tf_op jit(solution)/shard_map/all_to_all | solution.py:229
  129.8 0.0 collective-permute-done.1.r1
  129.8 3.4 %collective-permute-start.4 = (bf16[4,512,128]{2,1,0:T(8,128)(2,1)S(1)}, bf16[4,512,128]{2,1,0:T(8,128)(2,1)}, u32[]{:S(2)}, u32[]{:S(2)}) collective-permute-start(bf16[4,512,128]{2,1,0:T(8,128)(2,1)S(1)} %collective-permute-done.1.r1), channel_id=1, source_target_pairs={{0,1},{1,0},{2,3},{3,2},{4,5},{5,4},{6,7},{7,6},{8,9},{9,8},{10,11... | collective-permute-start | bytes 1572872 | tf_op jit(solution)/shard_map/ppermute | solution.py:242
  133.2 2.3 %collective-permute-done.2.r2 = bf16[4,512,128]{2,1,0:T(8,128)(2,1)} collective-permute-done((bf16[4,512,128]{2,1,0:T(8,128)(2,1)S(1)}, bf16[4,512,128]{2,1,0:T(8,128)(2,1)}, u32[]{:S(2)}, u32[]{:S(2)}) %collective-permute-start.2) | collective-permute-done | bytes 524320 | tf_op jit(solution)/shard_map/ppermute | solution.py:234
  135.5 3.1 %collective-permute-start.5 = (bf16[4,512,128]{2,1,0:T(8,128)(2,1)}, bf16[4,512,128]{2,1,0:T(8,128)(2,1)}, u32[]{:S(2)}, u32[]{:S(2)}) collective-permute-start(bf16[4,512,128]{2,1,0:T(8,128)(2,1)} %collective-permute-done.2.r2), channel_id=1, source_target_pairs={{0,1},{1,0},{2,3},{3,2},{4,5},{5,4},{6,7},{7,6},{8,9},{9,8},{10,11... | collective-permute-start | bytes 1572872 | tf_op jit(solution)/shard_map/ppermute | solution.py:242
  138.6 0.0 collective-permute-done.3.r3
  138.6 1.9 %collective-permute-start.6 = (bf16[4,512,128]{2,1,0:T(8,128)(2,1)}, bf16[4,512,128]{2,1,0:T(8,128)(2,1)}, u32[]{:S(2)}, u32[]{:S(2)}) collective-permute-start(bf16[4,512,128]{2,1,0:T(8,128)(2,1)} %collective-permute-done.3.r3), channel_id=1, source_target_pairs={{0,1},{1,0},{2,3},{3,2},{4,5},{5,4},{6,7},{7,6},{8,9},{9,8},{10,11... | collective-permute-start | bytes 1572872 | tf_op jit(solution)/shard_map/ppermute | solution.py:242
  140.5 0.0 copy-done.1
  140.5 0.0 copy-done.3
  140.5 3.8 %own.1 = (f32[192,512]{1,0:T(8,128)S(1)}, bf16[192,4096]{1,0:T(8,128)(2,1)}) custom-call(s32[2]{0:T(128)S(1)} %pad_add_fusion.at_ref, bf16[192,4096]{1,0:T(8,128)(2,1)S(1)} %bitcast.12, bf16[512,192]{1,0:T(8,128)(2,1)S(1)} %bitcast.15, bf16[4,512,128]{2,1,0:T(8,128)(2,1)S(1)} %all_gather.3.rows_ref.r0, bf16[4,512,128]{2,1,0:T(8,128)(2,1)S(1)} %collective-permute-done.1.r1, ...), custom_call_target="tpu_custom_call" | custom-call | flops 1000 | bytes 1000 | tf_op jit(solution)/shard_map/own/pallas_call | solution.py:246
  144.3 0.0 copy-start.4
  144.3 0.8 copy-done.4
  145.1 5.9 %all-to-all-done.3.sums_ref = f32[32,1,64]{2,1,0:T(1,128)S(1)} async-done(((f32[32,1,64]{2,1,0:T(1,128)}), f32[32,1,64]{2,1,0:T(1,128)S(1)}, u32[]{:S(2)}, u32[]{:S(2)}) %all-to-all-start.3) | async-done | bytes 8224 | tf_op jit(solution)/shard_map/all_to_all | solution.py:229
  150.9 0.8 gate.1
  151.8 0.0 collective-permute-done.4.o1
  151.8 0.0 collective-permute-done.5.o2
  151.8 0.0 collective-permute-done.6.o3
  151.8 0.1 copy-done.5
  151.9 4.1 %other.1 = (bf16[512,192]{1,0:T(8,128)(2,1)}, bf16[192,4096]{1,0:T(8,128)(2,1)}) custom-call(s32[2]{0:T(128)S(1)} %pad_add_fusion.at_ref, bf16[192,4096]{1,0:T(8,128)(2,1)S(1)} %bitcast.13, bf16[512,192]{1,0:T(8,128)(2,1)S(1)} %bitcast.16, f32[192,512]{1,0:T(8,128)S(1)} %copy-done.5, ...), custom_call_target="tpu_custom_call", output_to_operand_aliasing={{1}: (7, {})} | custom-call | flops 1000 | bytes 1000 | tf_op jit(solution)/shard_map/other/pallas_call | solution.py:262
  (1 shorter events, 0.0 us)
Async XLA Ops:
  1.3 0.8 copy-start.6
  2.1 0.7 copy-start.7
  3.9 27.9 %all-to-all-start = ((bf16[32,16,128]{2,1,0:T(8,128)(2,1)}), bf16[32,16,128]{2,1,0:T(8,128)(2,1)S(1)}, u32[]{:S(2)}, u32[]{:S(2)}) async-start(bf16[32,16,128]{2,1,0:T(8,128)(2,1)} %bitcast.5), calls=%async_computation | async-start | bytes 262144 | tf_op jit(solution)/shard_map/all_to_all | solution.py:193
  20.0 1.4 copy-start
  21.4 0.9 copy-start.2
  31.7 64.7 %all-to-all-start.1 = ((bf16[4,192,1536]{2,1,0:T(8,128)(2,1)}), bf16[4,192,1536]{2,1,0:T(8,128)(2,1)S(1)}, u32[]{:S(2)}, u32[]{:S(2)}) async-start(bf16[4,192,1536]{2,1,0:T(8,128)(2,1)} %pack.1), calls=%async_computation.1 | async-start | bytes 4718592 | tf_op jit(solution)/shard_map/all_to_all | solution.py:189
  91.8 6.0 %collective-permute-start = (bf16[4,512,128]{2,1,0:T(8,128)(2,1)S(1)}, bf16[4,512,128]{2,1,0:T(8,128)(2,1)S(1)}, u32[]{:S(2)}, u32[]{:S(2)}) collective-permute-start(bf16[4,512,128]{2,1,0:T(8,128)(2,1)S(1)} %all_gather.3.rows_ref.r0), channel_id=1, source_target_pairs={{0,1},{1,0},{2,3},{3,2},{4,5},{5,4},{6,7},{7,6},{8,9},{9,8},{10,11... | collective-permute-start | bytes 1572872 | tf_op jit(solution)/shard_map/ppermute | solution.py:197
  99.6 17.9 %all-to-all-start.2 = ((f32[32,1,128]{2,1,0:T(1,128)}), f32[32,1,128]{2,1,0:T(1,128)S(1)}, u32[]{:S(2)}, u32[]{:S(2)}) async-start(f32[32,1,128]{2,1,0:T(1,128)} %slots.1), calls=%async_computation.2 | async-start | bytes 32768 | tf_op jit(solution)/shard_map/all_to_all | solution.py:217
  106.6 33.9 %copy-start.1 = (bf16[1,192,4096]{2,1,0:T(8,128)(2,1)S(1)}, bf16[1,192,4096]{2,1,0:T(8,128)(2,1)}, u32[]{:S(2)}) copy-start(bf16[1,192,4096]{2,1,0:T(8,128)(2,1)} %param.9) | copy-start | bytes 4718596
  106.6 33.9 %copy-start.3 = (bf16[1,32,16,192]{3,2,1,0:T(8,128)(2,1)S(1)}, bf16[1,32,16,192]{3,2,1,0:T(8,128)(2,1)}, u32[]{:S(2)}) copy-start(bf16[1,32,16,192]{3,2,1,0:T(8,128)(2,1)} %param.8) | copy-start | bytes 589828
  106.6 23.1 %collective-permute-start.1 = (bf16[4,512,128]{2,1,0:T(8,128)(2,1)S(1)}, bf16[4,512,128]{2,1,0:T(8,128)(2,1)S(1)}, u32[]{:S(2)}, u32[]{:S(2)}) collective-permute-start(bf16[4,512,128]{2,1,0:T(8,128)(2,1)S(1)} %all_gather.3.rows_ref.r0), channel_id=1, source_target_pairs={{0,2},{1,3},{2,4},{3,5},{4,6},{5,7},{6,0},{7,1},{8,10},{9,11},{10,... | collective-permute-start | bytes 1572872 | tf_op jit(solution)/shard_map/ppermute | solution.py:234
  110.1 25.4 %collective-permute-start.2 = (bf16[4,512,128]{2,1,0:T(8,128)(2,1)S(1)}, bf16[4,512,128]{2,1,0:T(8,128)(2,1)}, u32[]{:S(2)}, u32[]{:S(2)}) collective-permute-start(bf16[4,512,128]{2,1,0:T(8,128)(2,1)S(1)} %all_gather.3.rows_ref.r0), channel_id=1, source_target_pairs={{0,4},{1,5},{2,6},{3,7},{4,0},{5,1},{6,2},{7,3},{8,12},{9,13},{10,... | collective-permute-start | bytes 1572872 | tf_op jit(solution)/shard_map/ppermute | solution.py:234
  114.4 24.2 %collective-permute-start.3 = (bf16[4,512,128]{2,1,0:T(8,128)(2,1)S(1)}, bf16[4,512,128]{2,1,0:T(8,128)(2,1)}, u32[]{:S(2)}, u32[]{:S(2)}) collective-permute-start(bf16[4,512,128]{2,1,0:T(8,128)(2,1)S(1)} %all_gather.3.rows_ref.r0), channel_id=1, source_target_pairs={{0,6},{1,7},{2,0},{3,1},{4,2},{5,3},{6,4},{7,5},{8,14},{9,15},{10,... | collective-permute-start | bytes 1572872 | tf_op jit(solution)/shard_map/ppermute | solution.py:234
  118.2 32.7 %all-to-all-start.3 = ((f32[32,1,64]{2,1,0:T(1,128)}), f32[32,1,64]{2,1,0:T(1,128)S(1)}, u32[]{:S(2)}, u32[]{:S(2)}) async-start(f32[32,1,64]{2,1,0:T(1,128)} %turn.1), calls=%async_computation.3 | async-start | bytes 32768 | tf_op jit(solution)/shard_map/all_to_all | solution.py:229
  129.8 22.0 %collective-permute-start.4 = (bf16[4,512,128]{2,1,0:T(8,128)(2,1)S(1)}, bf16[4,512,128]{2,1,0:T(8,128)(2,1)}, u32[]{:S(2)}, u32[]{:S(2)}) collective-permute-start(bf16[4,512,128]{2,1,0:T(8,128)(2,1)S(1)} %collective-permute-done.1.r1), channel_id=1, source_target_pairs={{0,1},{1,0},{2,3},{3,2},{4,5},{5,4},{6,7},{7,6},{8,9},{9,8},{10,11... | collective-permute-start | bytes 1572872 | tf_op jit(solution)/shard_map/ppermute | solution.py:242
  135.5 16.3 %collective-permute-start.5 = (bf16[4,512,128]{2,1,0:T(8,128)(2,1)}, bf16[4,512,128]{2,1,0:T(8,128)(2,1)}, u32[]{:S(2)}, u32[]{:S(2)}) collective-permute-start(bf16[4,512,128]{2,1,0:T(8,128)(2,1)} %collective-permute-done.2.r2), channel_id=1, source_target_pairs={{0,1},{1,0},{2,3},{3,2},{4,5},{5,4},{6,7},{7,6},{8,9},{9,8},{10,11... | collective-permute-start | bytes 1572872 | tf_op jit(solution)/shard_map/ppermute | solution.py:242
  138.6 13.2 %collective-permute-start.6 = (bf16[4,512,128]{2,1,0:T(8,128)(2,1)}, bf16[4,512,128]{2,1,0:T(8,128)(2,1)}, u32[]{:S(2)}, u32[]{:S(2)}) collective-permute-start(bf16[4,512,128]{2,1,0:T(8,128)(2,1)} %collective-permute-done.3.r3), channel_id=1, source_target_pairs={{0,1},{1,0},{2,3},{3,2},{4,5},{5,4},{6,7},{7,6},{8,9},{9,8},{10,11... | collective-permute-start | bytes 1572872 | tf_op jit(solution)/shard_map/ppermute | solution.py:242
  144.3 0.8 copy-start.4
  150.9 1.0 copy-start.5

commit v9 on v8

--- a/solution.py
+++ b/solution.py
@@ -105,17 +105,21 @@
     blocks, copies = [], []
     for row_ref, back, side in parts:
         source = lax.rem(at_ref[0] + 4 - back, 4)
-        for hi in range(4):
-            rows = row_ref[hi]
-            first = pl.multiple_of((hi * 4 + source) * 256 + side * 128, 128)
-            i = len(blocks)
-            held[i] = jnp.dot(left, rows, preferred_element_type=jnp.float32).astype(jnp.bfloat16)
-            copy = pltpu.make_async_copy(
-                held.at[i], weight_ref.at[:, pl.ds(first, 128)], sems.at[i]
-            )
-            copy.start()
-            blocks.append((rows, first))
-            copies.append(copy)
+        for hi in range(0, 4, 2):
+            pair = [row_ref[hi], row_ref[hi + 1]]
+            both = jnp.dot(
+                left, jnp.concatenate(pair, axis=1), preferred_element_type=jnp.float32
+            ).astype(jnp.bfloat16)
+            for more, rows in enumerate(pair):
+                first = pl.multiple_of(((hi + more) * 4 + source) * 256 + side * 128, 128)
+                i = len(blocks)
+                held[i] = both[:, more * 128 : more * 128 + 128]
+                copy = pltpu.make_async_copy(
+                    held.at[i], weight_ref.at[:, pl.ds(first, 128)], sems.at[i]
+                )
+                copy.start()
+                blocks.append((rows, first))
+                copies.append(copy)
     return product(w_ref, 0, 192, blocks), copies
 
 

time: 158 us -> 158 us (level)
  no operation moved by 1% of the time
where the time goes in v9:
time: 158 us; the launch traced here: 156 us
  starting transfers between devices  62.5 us (40%)
  blocking collectives  56 us (35%)
  waiting for transfers between devices  16.7 us (11%)
  Pallas kernels  14.3 us (9%)
  local copies, waits for them, and re-layouts  5.44 us (3%)
    all_gather x1, blocking collectives, per_device(): lax.all_gather(arrived, BOTH, axis=0, tiled=False, axis_index_groups=grou...  56 us
    all_to_all x1, starting transfers between devices, per_device(): lax.all_to_all(outgoing.reshape(experts, slot_count, -1), 'expert', 0, 0,...  16.1 us
    all_to_all x1, starting transfers between devices, per_device(): lax.all_to_all(to_z, BOTH, 0, 0, tiled=True, axis_index_groups=groups('hi...  11.6 us
    ppermute x3, starting transfers between devices, per_device(): lax.ppermute(going, 'replica', [(i, i // 8 * 8 + (i % 8 // 2 + k) % 4 * 2...  10.8 us
    ppermute x3, starting transfers between devices, per_device(): lax.ppermute(rows, 'replica', [(i, i ^ 1) for i in range(32)])  8.4 us
    all_to_all x1, waiting for transfers between devices, per_device(): lax.all_to_all(outgoing.reshape(experts, slot_count, -1), 'expert', 0, 0,...  7.75 us
    all_to_all x1, starting transfers between devices, per_device(): lax.all_to_all(plane_sums, BOTH, 0, 0, tiled=True, axis_index_groups=grou...  7.04 us
    all_to_all x1, waiting for transfers between devices, per_device(): lax.all_to_all(to_z, BOTH, 0, 0, tiled=True, axis_index_groups=groups('hi...  6.37 us
  transfers between devices with their start and end apart: 11, of which 4 were waited for; matrix products, arithmetic and copies ran while one was open for 0% of the time, Pallas kernels for 5%

profile of v9, /device:TPU:1, one launch (start us, length us, event | category | flops | bytes accessed | tf_op | source)
XLA Modules:
  0.0 155.8 jit_solution(10061609103919403637)
XLA Ops:
  0.6 0.7 reshape.29.gate_ref
  1.3 0.0 copy-start.6
  1.3 0.8 copy-done.6
  2.1 0.0 copy-start.7
  2.1 0.7 copy-done.7
  2.8 1.0 place.1
  3.9 16.1 %all-to-all-start = ((bf16[32,16,128]{2,1,0:T(8,128)(2,1)}), bf16[32,16,128]{2,1,0:T(8,128)(2,1)S(1)}, u32[]{:S(2)}, u32[]{:S(2)}) async-start(bf16[32,16,128]{2,1,0:T(8,128)(2,1)} %bitcast.5), calls=%async_computation | async-start | bytes 262144 | tf_op jit(solution)/shard_map/all_to_all | solution.py:197
  20.0 0.0 copy-start
  20.0 1.4 copy-done
  21.4 0.0 copy-start.2
  21.4 0.9 copy-done.2
  22.3 1.7 %pack.1 = bf16[4,192,1536]{2,1,0:T(8,128)(2,1)} custom-call(bf16[192,4096]{1,0:T(8,128)(2,1)S(1)} %bitcast.11, bf16[512,192]{1,0:T(8,128)(2,1)S(1)} %bitcast.14), custom_call_target="tpu_custom_call" | custom-call | bytes 4194304 | tf_op jit(solution)/shard_map/pack/pallas_call | solution.py:184
  24.0 7.7 %all-to-all-done = bf16[32,16,128]{2,1,0:T(8,128)(2,1)S(1)} async-done(((bf16[32,16,128]{2,1,0:T(8,128)(2,1)}), bf16[32,16,128]{2,1,0:T(8,128)(2,1)S(1)}, u32[]{:S(2)}, u32[]{:S(2)}) %all-to-all-start) | async-done | bytes 131104 | tf_op jit(solution)/shard_map/all_to_all | solution.py:197
  31.7 4.0 %all-to-all-start.1 = ((bf16[4,192,1536]{2,1,0:T(8,128)(2,1)}), bf16[4,192,1536]{2,1,0:T(8,128)(2,1)S(1)}, u32[]{:S(2)}, u32[]{:S(2)}) async-start(bf16[4,192,1536]{2,1,0:T(8,128)(2,1)} %pack.1), calls=%async_computation.1 | async-start | bytes 4718592 | tf_op jit(solution)/shard_map/all_to_all | solution.py:193
  35.7 56.0 %all_gather.3.rows_ref.r0 = bf16[4,512,128]{2,1,0:T(8,128)(2,1)S(1)} all-gather(bf16[1,512,128]{2,1,0:T(8,128)(2,1)S(1)} %bitcast.21), channel_id=1, replica_groups={{0,8,16,24},{1,9,17,25},{2,10,18,26},{3,11,19,27},{4,12,20,28},{5,13,21..., dimensions={0}, use_global_device_ids=true | all-gather | bytes 655360 | tf_op jit(solution)/shard_map/all_gather | solution.py:200
  91.8 4.5 %collective-permute-start = (bf16[4,512,128]{2,1,0:T(8,128)(2,1)S(1)}, bf16[4,512,128]{2,1,0:T(8,128)(2,1)S(1)}, u32[]{:S(2)}, u32[]{:S(2)}) collective-permute-start(bf16[4,512,128]{2,1,0:T(8,128)(2,1)S(1)} %all_gather.3.rows_ref.r0), channel_id=1, source_target_pairs={{0,1},{1,0},{2,3},{3,2},{4,5},{5,4},{6,7},{7,6},{8,9},{9,8},{10,11... | collective-permute-start | bytes 1572872 | tf_op jit(solution)/shard_map/ppermute | solution.py:201
  96.3 0.1 pad_add_fusion.at_ref
  96.4 0.0 all-to-all-done.1
  96.4 1.2 own_slots.1.own_ref
  97.5 0.2 collective-permute-done.rows_ref.o0
  97.8 1.8 %slots.1 = f32[32,1,128]{2,1,0:T(1,128)} custom-call(s32[2]{0:T(128)S(1)} %pad_add_fusion.at_ref, bf16[4,512,128]{2,1,0:T(8,128)(2,1)S(1)} %collective-permute-done.rows_ref.o0, bf16[768,1536]{1,0:T(8,128)(2,1)S(1)} %bitcast.18, f32[1,512]{1,0:T(1,128)S(1)} %own_slots.1.own_ref), custom_call_target="tpu_custom_call" | custom-call | flops 805306368 | bytes 6291456 | tf_op jit(solution)/shard_map/slots/pallas_call | solution.py:212
  99.6 7.0 %all-to-all-start.2 = ((f32[32,1,128]{2,1,0:T(1,128)}), f32[32,1,128]{2,1,0:T(1,128)S(1)}, u32[]{:S(2)}, u32[]{:S(2)}) async-start(f32[32,1,128]{2,1,0:T(1,128)} %slots.1), calls=%async_computation.2 | async-start | bytes 32768 | tf_op jit(solution)/shard_map/all_to_all | solution.py:221
  106.6 0.0 copy-start.1
  106.6 0.0 copy-start.3
  106.6 3.4 %collective-permute-start.1 = (bf16[4,512,128]{2,1,0:T(8,128)(2,1)S(1)}, bf16[4,512,128]{2,1,0:T(8,128)(2,1)S(1)}, u32[]{:S(2)}, u32[]{:S(2)}) collective-permute-start(bf16[4,512,128]{2,1,0:T(8,128)(2,1)S(1)} %all_gather.3.rows_ref.r0), channel_id=1, source_target_pairs={{0,2},{1,3},{2,4},{3,5},{4,6},{5,7},{6,0},{7,1},{8,10},{9,11},{10,... | collective-permute-start | bytes 1572872 | tf_op jit(solution)/shard_map/ppermute | solution.py:238
  110.1 4.3 %collective-permute-start.2 = (bf16[4,512,128]{2,1,0:T(8,128)(2,1)S(1)}, bf16[4,512,128]{2,1,0:T(8,128)(2,1)}, u32[]{:S(2)}, u32[]{:S(2)}) collective-permute-start(bf16[4,512,128]{2,1,0:T(8,128)(2,1)S(1)} %all_gather.3.rows_ref.r0), channel_id=1, source_target_pairs={{0,4},{1,5},{2,6},{3,7},{4,0},{5,1},{6,2},{7,3},{8,12},{9,13},{10,... | collective-permute-start | bytes 1572872 | tf_op jit(solution)/shard_map/ppermute | solution.py:238
  114.4 3.1 %collective-permute-start.3 = (bf16[4,512,128]{2,1,0:T(8,128)(2,1)S(1)}, bf16[4,512,128]{2,1,0:T(8,128)(2,1)}, u32[]{:S(2)}, u32[]{:S(2)}) collective-permute-start(bf16[4,512,128]{2,1,0:T(8,128)(2,1)S(1)} %all_gather.3.rows_ref.r0), channel_id=1, source_target_pairs={{0,6},{1,7},{2,0},{3,1},{4,2},{5,3},{6,4},{7,5},{8,14},{9,15},{10,... | collective-permute-start | bytes 1572872 | tf_op jit(solution)/shard_map/ppermute | solution.py:238
  117.5 0.0 all-to-all-done.2.sums_ref
  117.5 0.7 turn.1
  118.2 11.6 %all-to-all-start.3 = ((f32[32,1,64]{2,1,0:T(1,128)}), f32[32,1,64]{2,1,0:T(1,128)S(1)}, u32[]{:S(2)}, u32[]{:S(2)}) async-start(f32[32,1,64]{2,1,0:T(1,128)} %turn.1), calls=%async_computation.3 | async-start | bytes 32768 | tf_op jit(solution)/shard_map/all_to_all | solution.py:233
  129.8 0.0 collective-permute-done.1.r1
  129.8 3.4 %collective-permute-start.4 = (bf16[4,512,128]{2,1,0:T(8,128)(2,1)S(1)}, bf16[4,512,128]{2,1,0:T(8,128)(2,1)}, u32[]{:S(2)}, u32[]{:S(2)}) collective-permute-start(bf16[4,512,128]{2,1,0:T(8,128)(2,1)S(1)} %collective-permute-done.1.r1), channel_id=1, source_target_pairs={{0,1},{1,0},{2,3},{3,2},{4,5},{5,4},{6,7},{7,6},{8,9},{9,8},{10,11... | collective-permute-start | bytes 1572872 | tf_op jit(solution)/shard_map/ppermute | solution.py:246
  133.2 2.3 %collective-permute-done.2.r2 = bf16[4,512,128]{2,1,0:T(8,128)(2,1)} collective-permute-done((bf16[4,512,128]{2,1,0:T(8,128)(2,1)S(1)}, bf16[4,512,128]{2,1,0:T(8,128)(2,1)}, u32[]{:S(2)}, u32[]{:S(2)}) %collective-permute-start.2) | collective-permute-done | bytes 524320 | tf_op jit(solution)/shard_map/ppermute | solution.py:238
  135.5 3.1 %collective-permute-start.5 = (bf16[4,512,128]{2,1,0:T(8,128)(2,1)}, bf16[4,512,128]{2,1,0:T(8,128)(2,1)}, u32[]{:S(2)}, u32[]{:S(2)}) collective-permute-start(bf16[4,512,128]{2,1,0:T(8,128)(2,1)} %collective-permute-done.2.r2), channel_id=1, source_target_pairs={{0,1},{1,0},{2,3},{3,2},{4,5},{5,4},{6,7},{7,6},{8,9},{9,8},{10,11... | collective-permute-start | bytes 1572872 | tf_op jit(solution)/shard_map/ppermute | solution.py:246
  138.6 0.0 collective-permute-done.3.r3
  138.6 1.9 %collective-permute-start.6 = (bf16[4,512,128]{2,1,0:T(8,128)(2,1)}, bf16[4,512,128]{2,1,0:T(8,128)(2,1)}, u32[]{:S(2)}, u32[]{:S(2)}) collective-permute-start(bf16[4,512,128]{2,1,0:T(8,128)(2,1)} %collective-permute-done.3.r3), channel_id=1, source_target_pairs={{0,1},{1,0},{2,3},{3,2},{4,5},{5,4},{6,7},{7,6},{8,9},{9,8},{10,11... | collective-permute-start | bytes 1572872 | tf_op jit(solution)/shard_map/ppermute | solution.py:246
  140.5 0.0 copy-done.1
  140.5 0.0 copy-done.3
  140.5 3.3 %own.1 = (f32[192,512]{1,0:T(8,128)S(1)}, bf16[192,4096]{1,0:T(8,128)(2,1)}) custom-call(s32[2]{0:T(128)S(1)} %pad_add_fusion.at_ref, bf16[192,4096]{1,0:T(8,128)(2,1)S(1)} %bitcast.12, bf16[512,192]{1,0:T(8,128)(2,1)S(1)} %bitcast.15, bf16[4,512,128]{2,1,0:T(8,128)(2,1)S(1)} %all_gather.3.rows_ref.r0, bf16[4,512,128]{2,1,0:T(8,128)(2,1)S(1)} %collective-permute-done.1.r1, ...), custom_call_target="tpu_custom_call" | custom-call | flops 1000 | bytes 1000 | tf_op jit(solution)/shard_map/own/pallas_call | solution.py:250
  143.8 0.0 copy-start.4
  143.8 0.8 copy-done.4
  144.6 6.4 %all-to-all-done.3.sums_ref = f32[32,1,64]{2,1,0:T(1,128)S(1)} async-done(((f32[32,1,64]{2,1,0:T(1,128)}), f32[32,1,64]{2,1,0:T(1,128)S(1)}, u32[]{:S(2)}, u32[]{:S(2)}) %all-to-all-start.3) | async-done | bytes 8224 | tf_op jit(solution)/shard_map/all_to_all | solution.py:233
  150.9 0.8 gate.1
  151.8 0.0 collective-permute-done.4.o1
  151.8 0.0 collective-permute-done.5.o2
  151.8 0.0 collective-permute-done.6.o3
  151.8 0.1 copy-done.5
  151.9 3.8 %other.1 = (bf16[512,192]{1,0:T(8,128)(2,1)}, bf16[192,4096]{1,0:T(8,128)(2,1)}) custom-call(s32[2]{0:T(128)S(1)} %pad_add_fusion.at_ref, bf16[192,4096]{1,0:T(8,128)(2,1)S(1)} %bitcast.13, bf16[512,192]{1,0:T(8,128)(2,1)S(1)} %bitcast.16, f32[192,512]{1,0:T(8,128)S(1)} %copy-done.5, ...), custom_call_target="tpu_custom_call", output_to_operand_aliasing={{1}: (7, {})} | custom-call | flops 1000 | bytes 1000 | tf_op jit(solution)/shard_map/other/pallas_call | solution.py:266
  (1 shorter events, 0.0 us)
Async XLA Ops:
  1.3 0.8 copy-start.6
  2.1 0.7 copy-start.7
  3.9 27.9 %all-to-all-start = ((bf16[32,16,128]{2,1,0:T(8,128)(2,1)}), bf16[32,16,128]{2,1,0:T(8,128)(2,1)S(1)}, u32[]{:S(2)}, u32[]{:S(2)}) async-start(bf16[32,16,128]{2,1,0:T(8,128)(2,1)} %bitcast.5), calls=%async_computation | async-start | bytes 262144 | tf_op jit(solution)/shard_map/all_to_all | solution.py:197
  20.0 1.4 copy-start
  21.4 0.9 copy-start.2
  31.7 64.7 %all-to-all-start.1 = ((bf16[4,192,1536]{2,1,0:T(8,128)(2,1)}), bf16[4,192,1536]{2,1,0:T(8,128)(2,1)S(1)}, u32[]{:S(2)}, u32[]{:S(2)}) async-start(bf16[4,192,1536]{2,1,0:T(8,128)(2,1)} %pack.1), calls=%async_computation.1 | async-start | bytes 4718592 | tf_op jit(solution)/shard_map/all_to_all | solution.py:193
  91.8 6.0 %collective-permute-start = (bf16[4,512,128]{2,1,0:T(8,128)(2,1)S(1)}, bf16[4,512,128]{2,1,0:T(8,128)(2,1)S(1)}, u32[]{:S(2)}, u32[]{:S(2)}) collective-permute-start(bf16[4,512,128]{2,1,0:T(8,128)(2,1)S(1)} %all_gather.3.rows_ref.r0), channel_id=1, source_target_pairs={{0,1},{1,0},{2,3},{3,2},{4,5},{5,4},{6,7},{7,6},{8,9},{9,8},{10,11... | collective-permute-start | bytes 1572872 | tf_op jit(solution)/shard_map/ppermute | solution.py:201
  99.6 17.9 %all-to-all-start.2 = ((f32[32,1,128]{2,1,0:T(1,128)}), f32[32,1,128]{2,1,0:T(1,128)S(1)}, u32[]{:S(2)}, u32[]{:S(2)}) async-start(f32[32,1,128]{2,1,0:T(1,128)} %slots.1), calls=%async_computation.2 | async-start | bytes 32768 | tf_op jit(solution)/shard_map/all_to_all | solution.py:221
  106.6 33.9 %copy-start.1 = (bf16[1,192,4096]{2,1,0:T(8,128)(2,1)S(1)}, bf16[1,192,4096]{2,1,0:T(8,128)(2,1)}, u32[]{:S(2)}) copy-start(bf16[1,192,4096]{2,1,0:T(8,128)(2,1)} %param.9) | copy-start | bytes 4718596
  106.6 33.9 %copy-start.3 = (bf16[1,32,16,192]{3,2,1,0:T(8,128)(2,1)S(1)}, bf16[1,32,16,192]{3,2,1,0:T(8,128)(2,1)}, u32[]{:S(2)}) copy-start(bf16[1,32,16,192]{3,2,1,0:T(8,128)(2,1)} %param.8) | copy-start | bytes 589828
  106.6 23.1 %collective-permute-start.1 = (bf16[4,512,128]{2,1,0:T(8,128)(2,1)S(1)}, bf16[4,512,128]{2,1,0:T(8,128)(2,1)S(1)}, u32[]{:S(2)}, u32[]{:S(2)}) collective-permute-start(bf16[4,512,128]{2,1,0:T(8,128)(2,1)S(1)} %all_gather.3.rows_ref.r0), channel_id=1, source_target_pairs={{0,2},{1,3},{2,4},{3,5},{4,6},{5,7},{6,0},{7,1},{8,10},{9,11},{10,... | collective-permute-start | bytes 1572872 | tf_op jit(solution)/shard_map/ppermute | solution.py:238
  110.1 25.4 %collective-permute-start.2 = (bf16[4,512,128]{2,1,0:T(8,128)(2,1)S(1)}, bf16[4,512,128]{2,1,0:T(8,128)(2,1)}, u32[]{:S(2)}, u32[]{:S(2)}) collective-permute-start(bf16[4,512,128]{2,1,0:T(8,128)(2,1)S(1)} %all_gather.3.rows_ref.r0), channel_id=1, source_target_pairs={{0,4},{1,5},{2,6},{3,7},{4,0},{5,1},{6,2},{7,3},{8,12},{9,13},{10,... | collective-permute-start | bytes 1572872 | tf_op jit(solution)/shard_map/ppermute | solution.py:238
  114.4 24.2 %collective-permute-start.3 = (bf16[4,512,128]{2,1,0:T(8,128)(2,1)S(1)}, bf16[4,512,128]{2,1,0:T(8,128)(2,1)}, u32[]{:S(2)}, u32[]{:S(2)}) collective-permute-start(bf16[4,512,128]{2,1,0:T(8,128)(2,1)S(1)} %all_gather.3.rows_ref.r0), channel_id=1, source_target_pairs={{0,6},{1,7},{2,0},{3,1},{4,2},{5,3},{6,4},{7,5},{8,14},{9,15},{10,... | collective-permute-start | bytes 1572872 | tf_op jit(solution)/shard_map/ppermute | solution.py:238
  118.2 32.7 %all-to-all-start.3 = ((f32[32,1,64]{2,1,0:T(1,128)}), f32[32,1,64]{2,1,0:T(1,128)S(1)}, u32[]{:S(2)}, u32[]{:S(2)}) async-start(f32[32,1,64]{2,1,0:T(1,128)} %turn.1), calls=%async_computation.3 | async-start | bytes 32768 | tf_op jit(solution)/shard_map/all_to_all | solution.py:233
  129.8 22.0 %collective-permute-start.4 = (bf16[4,512,128]{2,1,0:T(8,128)(2,1)S(1)}, bf16[4,512,128]{2,1,0:T(8,128)(2,1)}, u32[]{:S(2)}, u32[]{:S(2)}) collective-permute-start(bf16[4,512,128]{2,1,0:T(8,128)(2,1)S(1)} %collective-permute-done.1.r1), channel_id=1, source_target_pairs={{0,1},{1,0},{2,3},{3,2},{4,5},{5,4},{6,7},{7,6},{8,9},{9,8},{10,11... | collective-permute-start | bytes 1572872 | tf_op jit(solution)/shard_map/ppermute | solution.py:246
  135.5 16.3 %collective-permute-start.5 = (bf16[4,512,128]{2,1,0:T(8,128)(2,1)}, bf16[4,512,128]{2,1,0:T(8,128)(2,1)}, u32[]{:S(2)}, u32[]{:S(2)}) collective-permute-start(bf16[4,512,128]{2,1,0:T(8,128)(2,1)} %collective-permute-done.2.r2), channel_id=1, source_target_pairs={{0,1},{1,0},{2,3},{3,2},{4,5},{5,4},{6,7},{7,6},{8,9},{9,8},{10,11... | collective-permute-start | bytes 1572872 | tf_op jit(solution)/shard_map/ppermute | solution.py:246
  138.6 13.2 %collective-permute-start.6 = (bf16[4,512,128]{2,1,0:T(8,128)(2,1)}, bf16[4,512,128]{2,1,0:T(8,128)(2,1)}, u32[]{:S(2)}, u32[]{:S(2)}) collective-permute-start(bf16[4,512,128]{2,1,0:T(8,128)(2,1)} %collective-permute-done.3.r3), channel_id=1, source_target_pairs={{0,1},{1,0},{2,3},{3,2},{4,5},{5,4},{6,7},{7,6},{8,9},{9,8},{10,11... | collective-permute-start | bytes 1572872 | tf_op jit(solution)/shard_map/ppermute | solution.py:246
  143.8 0.8 copy-start.4
  150.9 1.0 copy-start.5

commit v10 on v9

--- a/solution.py
+++ b/solution.py
@@ -100,8 +100,7 @@
             out_ref[hi * 8 + lo] = line
 
 
-def some_results(at_ref, w_ref, saved_ref, parts, weight_ref, held, sems):
-    left = saved_ref[...].T
+def some_results(at_ref, w_ref, left, parts, weight_ref, held, sems):
     blocks, copies = [], []
     for row_ref, back, side in parts:
         source = lax.rem(at_ref[0] + 4 - back, 4)
@@ -126,18 +125,33 @@
 def own_kernel(at_ref, w_ref, saved_ref, r0, r1, r2, r3, o0, sums_ref, weight_ref, held, sems):
     core = at_ref[1]
     parts = [(r0, 0, core), (o0, 0, 1 - core), (r1, 1, core), (r2, 2, core), (r3, 3, core)]
-    sums_ref[...], copies = some_results(at_ref, w_ref, saved_ref, parts, weight_ref, held, sems)
+    left = saved_ref[...].T
+    sums_ref[...], copies = some_results(at_ref, w_ref, left, parts, weight_ref, held, sems)
     for copy in copies:
         copy.wait()
 
 
 def other_kernel(
-    at_ref, w_ref, saved_ref, sums_ref, o1, o2, o3, started_ref, hidden_ref, weight_ref, held, sems
+    at_ref, w_ref, saved_ref, sums_ref, o1, o2, o3, started_ref, hidden_ref, weight_ref,
+    held, sems, rows_in, sums_in, in_sems,
 ):
-    side = 1 - at_ref[1]
-    parts = [(o1, 1, side), (o2, 2, side), (o3, 3, side)]
-    total, copies = some_results(at_ref, w_ref, saved_ref, parts, weight_ref, held, sems)
-    hidden_ref[...] = (sums_ref[...] + total).T.astype(jnp.bfloat16)
+    arriving = [
+        pltpu.make_async_copy(ref, rows_in.at[n], in_sems.at[n]) for n, ref in enumerate((o1, o2, o3))
+    ] + [pltpu.make_async_copy(sums_ref, sums_in, in_sems.at[3])]
+    for copy in arriving:
+        copy.start()
+    side, left = 1 - at_ref[1], saved_ref[...].T
+    total, copies = None, []
+    for n in range(3):
+        arriving[n].wait()
+        here = [(rows_in.at[n], n + 1, side)]
+        term, more = some_results(
+            at_ref, w_ref, left, here, weight_ref, held.at[pl.ds(n * 4, 4)], sems.at[pl.ds(n * 4, 4)]
+        )
+        total = term if total is None else total + term
+        copies += more
+    arriving[3].wait()
+    hidden_ref[...] = (sums_in[...] + total).T.astype(jnp.bfloat16)
     for copy in copies:
         copy.wait()
 
@@ -269,11 +283,15 @@
             jax.ShapeDtypeStruct(saved.shape, jnp.bfloat16),
             jax.ShapeDtypeStruct(weight.shape, jnp.bfloat16),
         ),
-        in_specs=[smem] + [vmem] * 6 + [hbm],
+        in_specs=[smem] + [vmem] * 2 + [hbm] * 5,
         out_specs=(vmem, hbm),
         input_output_aliases={7: 1},
         scratch_shapes=[
-            pltpu.VMEM((12, 192, 128), jnp.bfloat16), pltpu.SemaphoreType.DMA((12,))
+            pltpu.VMEM((12, 192, 128), jnp.bfloat16),
+            pltpu.SemaphoreType.DMA((12,)),
+            pltpu.VMEM((3, 4, 512, 128), jnp.bfloat16),
+            pltpu.VMEM((192, 512), jnp.float32),
+            pltpu.SemaphoreType.DMA((4,)),
         ],
         compiler_params=params,
         cost_estimate=small,

time: 158 us -> 158 us (level)
  no operation moved by 1% of the time
where the time goes in v10:
time: 158 us; the launch traced here: 156 us
  starting transfers between devices  62.5 us (40%)
  blocking collectives  56 us (35%)
  waiting for transfers between devices  16.7 us (11%)
  Pallas kernels  14.6 us (9%)
  local copies, waits for them, and re-layouts  5.44 us (3%)
    all_gather x1, blocking collectives, per_device(): lax.all_gather(arrived, BOTH, axis=0, tiled=False, axis_index_groups=grou...  56 us
    all_to_all x1, starting transfers between devices, per_device(): lax.all_to_all(outgoing.reshape(experts, slot_count, -1), 'expert', 0, 0,...  16.1 us
    all_to_all x1, starting transfers between devices, per_device(): lax.all_to_all(to_z, BOTH, 0, 0, tiled=True, axis_index_groups=groups('hi...  11.6 us
    ppermute x3, starting transfers between devices, per_device(): lax.ppermute(going, 'replica', [(i, i // 8 * 8 + (i % 8 // 2 + k) % 4 * 2...  10.8 us
    ppermute x3, starting transfers between devices, per_device(): lax.ppermute(rows, 'replica', [(i, i ^ 1) for i in range(32)])  8.4 us
    all_to_all x1, waiting for transfers between devices, per_device(): lax.all_to_all(outgoing.reshape(experts, slot_count, -1), 'expert', 0, 0,...  7.75 us
    all_to_all x1, starting transfers between devices, per_device(): lax.all_to_all(plane_sums, BOTH, 0, 0, tiled=True, axis_index_groups=grou...  7.04 us
    all_to_all x1, waiting for transfers between devices, per_device(): lax.all_to_all(to_z, BOTH, 0, 0, tiled=True, axis_index_groups=groups('hi...  6.37 us
  transfers between devices with their start and end apart: 11, of which 4 were waited for; matrix products, arithmetic and copies ran while one was open for 0% of the time, Pallas kernels for 5%

profile of v10, /device:TPU:1, one launch (start us, length us, event | category | flops | bytes accessed | tf_op | source)
XLA Modules:
  0.0 156.1 jit_solution(10567375462078836434)
XLA Ops:
  0.6 0.7 reshape.29.gate_ref
  1.3 0.0 copy-start.6
  1.3 0.8 copy-done.6
  2.1 0.0 copy-start.7
  2.1 0.7 copy-done.7
  2.8 1.0 place.1
  3.9 16.1 %all-to-all-start = ((bf16[32,16,128]{2,1,0:T(8,128)(2,1)}), bf16[32,16,128]{2,1,0:T(8,128)(2,1)S(1)}, u32[]{:S(2)}, u32[]{:S(2)}) async-start(bf16[32,16,128]{2,1,0:T(8,128)(2,1)} %bitcast.5), calls=%async_computation | async-start | bytes 262144 | tf_op jit(solution)/shard_map/all_to_all | solution.py:211
  20.0 0.0 copy-start
  20.0 1.4 copy-done
  21.4 0.0 copy-start.2
  21.4 0.9 copy-done.2
  22.3 1.7 %pack.1 = bf16[4,192,1536]{2,1,0:T(8,128)(2,1)} custom-call(bf16[192,4096]{1,0:T(8,128)(2,1)S(1)} %bitcast.11, bf16[512,192]{1,0:T(8,128)(2,1)S(1)} %bitcast.14), custom_call_target="tpu_custom_call" | custom-call | bytes 4194304 | tf_op jit(solution)/shard_map/pack/pallas_call | solution.py:198
  24.0 7.7 %all-to-all-done = bf16[32,16,128]{2,1,0:T(8,128)(2,1)S(1)} async-done(((bf16[32,16,128]{2,1,0:T(8,128)(2,1)}), bf16[32,16,128]{2,1,0:T(8,128)(2,1)S(1)}, u32[]{:S(2)}, u32[]{:S(2)}) %all-to-all-start) | async-done | bytes 131104 | tf_op jit(solution)/shard_map/all_to_all | solution.py:211
  31.7 4.0 %all-to-all-start.1 = ((bf16[4,192,1536]{2,1,0:T(8,128)(2,1)}), bf16[4,192,1536]{2,1,0:T(8,128)(2,1)S(1)}, u32[]{:S(2)}, u32[]{:S(2)}) async-start(bf16[4,192,1536]{2,1,0:T(8,128)(2,1)} %pack.1), calls=%async_computation.1 | async-start | bytes 4718592 | tf_op jit(solution)/shard_map/all_to_all | solution.py:207
  35.7 56.0 %all_gather.3.rows_ref.r0 = bf16[4,512,128]{2,1,0:T(8,128)(2,1)S(1)} all-gather(bf16[1,512,128]{2,1,0:T(8,128)(2,1)S(1)} %bitcast.21), channel_id=1, replica_groups={{0,8,16,24},{1,9,17,25},{2,10,18,26},{3,11,19,27},{4,12,20,28},{5,13,21..., dimensions={0}, use_global_device_ids=true | all-gather | bytes 655360 | tf_op jit(solution)/shard_map/all_gather | solution.py:214
  91.8 4.5 %collective-permute-start = (bf16[4,512,128]{2,1,0:T(8,128)(2,1)S(1)}, bf16[4,512,128]{2,1,0:T(8,128)(2,1)S(1)}, u32[]{:S(2)}, u32[]{:S(2)}) collective-permute-start(bf16[4,512,128]{2,1,0:T(8,128)(2,1)S(1)} %all_gather.3.rows_ref.r0), channel_id=1, source_target_pairs={{0,1},{1,0},{2,3},{3,2},{4,5},{5,4},{6,7},{7,6},{8,9},{9,8},{10,11... | collective-permute-start | bytes 1572872 | tf_op jit(solution)/shard_map/ppermute | solution.py:215
  96.3 0.1 pad_add_fusion.at_ref
  96.4 0.0 all-to-all-done.1
  96.4 1.2 own_slots.1.own_ref
  97.5 0.2 collective-permute-done.rows_ref.o0
  97.8 1.8 %slots.1 = f32[32,1,128]{2,1,0:T(1,128)} custom-call(s32[2]{0:T(128)S(1)} %pad_add_fusion.at_ref, bf16[4,512,128]{2,1,0:T(8,128)(2,1)S(1)} %collective-permute-done.rows_ref.o0, bf16[768,1536]{1,0:T(8,128)(2,1)S(1)} %bitcast.18, f32[1,512]{1,0:T(1,128)S(1)} %own_slots.1.own_ref), custom_call_target="tpu_custom_call" | custom-call | flops 805306368 | bytes 6291456 | tf_op jit(solution)/shard_map/slots/pallas_call | solution.py:226
  99.6 7.0 %all-to-all-start.2 = ((f32[32,1,128]{2,1,0:T(1,128)}), f32[32,1,128]{2,1,0:T(1,128)S(1)}, u32[]{:S(2)}, u32[]{:S(2)}) async-start(f32[32,1,128]{2,1,0:T(1,128)} %slots.1), calls=%async_computation.2 | async-start | bytes 32768 | tf_op jit(solution)/shard_map/all_to_all | solution.py:235
  106.6 0.0 copy-start.1
  106.6 0.0 copy-start.3
  106.6 3.4 %collective-permute-start.1 = (bf16[4,512,128]{2,1,0:T(8,128)(2,1)S(1)}, bf16[4,512,128]{2,1,0:T(8,128)(2,1)S(1)}, u32[]{:S(2)}, u32[]{:S(2)}) collective-permute-start(bf16[4,512,128]{2,1,0:T(8,128)(2,1)S(1)} %all_gather.3.rows_ref.r0), channel_id=1, source_target_pairs={{0,2},{1,3},{2,4},{3,5},{4,6},{5,7},{6,0},{7,1},{8,10},{9,11},{10,... | collective-permute-start | bytes 1572872 | tf_op jit(solution)/shard_map/ppermute | solution.py:252
  110.1 4.3 %collective-permute-start.2 = (bf16[4,512,128]{2,1,0:T(8,128)(2,1)S(1)}, bf16[4,512,128]{2,1,0:T(8,128)(2,1)}, u32[]{:S(2)}, u32[]{:S(2)}) collective-permute-start(bf16[4,512,128]{2,1,0:T(8,128)(2,1)S(1)} %all_gather.3.rows_ref.r0), channel_id=1, source_target_pairs={{0,4},{1,5},{2,6},{3,7},{4,0},{5,1},{6,2},{7,3},{8,12},{9,13},{10,... | collective-permute-start | bytes 1572872 | tf_op jit(solution)/shard_map/ppermute | solution.py:252
  114.4 3.1 %collective-permute-start.3 = (bf16[4,512,128]{2,1,0:T(8,128)(2,1)S(1)}, bf16[4,512,128]{2,1,0:T(8,128)(2,1)}, u32[]{:S(2)}, u32[]{:S(2)}) collective-permute-start(bf16[4,512,128]{2,1,0:T(8,128)(2,1)S(1)} %all_gather.3.rows_ref.r0), channel_id=1, source_target_pairs={{0,6},{1,7},{2,0},{3,1},{4,2},{5,3},{6,4},{7,5},{8,14},{9,15},{10,... | collective-permute-start | bytes 1572872 | tf_op jit(solution)/shard_map/ppermute | solution.py:252
  117.5 0.0 all-to-all-done.2.sums_ref
  117.5 0.7 turn.1
  118.2 11.6 %all-to-all-start.3 = ((f32[32,1,64]{2,1,0:T(1,128)}), f32[32,1,64]{2,1,0:T(1,128)S(1)}, u32[]{:S(2)}, u32[]{:S(2)}) async-start(f32[32,1,64]{2,1,0:T(1,128)} %turn.1), calls=%async_computation.3 | async-start | bytes 32768 | tf_op jit(solution)/shard_map/all_to_all | solution.py:247
  129.8 0.0 collective-permute-done.1.r1
  129.8 3.4 %collective-permute-start.4 = (bf16[4,512,128]{2,1,0:T(8,128)(2,1)S(1)}, bf16[4,512,128]{2,1,0:T(8,128)(2,1)}, u32[]{:S(2)}, u32[]{:S(2)}) collective-permute-start(bf16[4,512,128]{2,1,0:T(8,128)(2,1)S(1)} %collective-permute-done.1.r1), channel_id=1, source_target_pairs={{0,1},{1,0},{2,3},{3,2},{4,5},{5,4},{6,7},{7,6},{8,9},{9,8},{10,11... | collective-permute-start | bytes 1572872 | tf_op jit(solution)/shard_map/ppermute | solution.py:260
  133.2 2.3 %collective-permute-done.2.r2 = bf16[4,512,128]{2,1,0:T(8,128)(2,1)} collective-permute-done((bf16[4,512,128]{2,1,0:T(8,128)(2,1)S(1)}, bf16[4,512,128]{2,1,0:T(8,128)(2,1)}, u32[]{:S(2)}, u32[]{:S(2)}) %collective-permute-start.2) | collective-permute-done | bytes 524320 | tf_op jit(solution)/shard_map/ppermute | solution.py:252
  135.5 3.1 %collective-permute-start.5 = (bf16[4,512,128]{2,1,0:T(8,128)(2,1)}, bf16[4,512,128]{2,1,0:T(8,128)(2,1)}, u32[]{:S(2)}, u32[]{:S(2)}) collective-permute-start(bf16[4,512,128]{2,1,0:T(8,128)(2,1)} %collective-permute-done.2.r2), channel_id=1, source_target_pairs={{0,1},{1,0},{2,3},{3,2},{4,5},{5,4},{6,7},{7,6},{8,9},{9,8},{10,11... | collective-permute-start | bytes 1572872 | tf_op jit(solution)/shard_map/ppermute | solution.py:260
  138.6 0.0 collective-permute-done.3.r3
  138.6 1.9 %collective-permute-start.6 = (bf16[4,512,128]{2,1,0:T(8,128)(2,1)}, bf16[4,512,128]{2,1,0:T(8,128)(2,1)}, u32[]{:S(2)}, u32[]{:S(2)}) collective-permute-start(bf16[4,512,128]{2,1,0:T(8,128)(2,1)} %collective-permute-done.3.r3), channel_id=1, source_target_pairs={{0,1},{1,0},{2,3},{3,2},{4,5},{5,4},{6,7},{7,6},{8,9},{9,8},{10,11... | collective-permute-start | bytes 1572872 | tf_op jit(solution)/shard_map/ppermute | solution.py:260
  140.5 0.0 copy-done.1
  140.5 0.0 copy-done.3
  140.5 3.3 %own.1 = (f32[192,512]{1,0:T(8,128)S(1)}, bf16[192,4096]{1,0:T(8,128)(2,1)}) custom-call(s32[2]{0:T(128)S(1)} %pad_add_fusion.at_ref, bf16[192,4096]{1,0:T(8,128)(2,1)S(1)} %bitcast.12, bf16[512,192]{1,0:T(8,128)(2,1)S(1)} %bitcast.15, bf16[4,512,128]{2,1,0:T(8,128)(2,1)S(1)} %all_gather.3.rows_ref.r0, bf16[4,512,128]{2,1,0:T(8,128)(2,1)S(1)} %collective-permute-done.1.r1, ...), custom_call_target="tpu_custom_call" | custom-call | flops 1000 | bytes 1000 | tf_op jit(solution)/shard_map/own/pallas_call | solution.py:264
  143.8 0.0 copy-start.4
  143.8 0.8 copy-done.4
  144.6 6.4 %all-to-all-done.3.sums_ref = f32[32,1,64]{2,1,0:T(1,128)S(1)} async-done(((f32[32,1,64]{2,1,0:T(1,128)}), f32[32,1,64]{2,1,0:T(1,128)S(1)}, u32[]{:S(2)}, u32[]{:S(2)}) %all-to-all-start.3) | async-done | bytes 8224 | tf_op jit(solution)/shard_map/all_to_all | solution.py:247
  150.9 0.8 gate.1
  151.8 0.0 collective-permute-done.4.o1
  151.8 0.0 collective-permute-done.5.o2
  151.8 0.0 collective-permute-done.6.o3
  151.8 0.1 copy-done.5
  151.9 4.2 %other.1 = (bf16[512,192]{1,0:T(8,128)(2,1)}, bf16[192,4096]{1,0:T(8,128)(2,1)}) custom-call(s32[2]{0:T(128)S(1)} %pad_add_fusion.at_ref, bf16[192,4096]{1,0:T(8,128)(2,1)S(1)} %bitcast.13, bf16[512,192]{1,0:T(8,128)(2,1)S(1)} %bitcast.16, f32[192,512]{1,0:T(8,128)S(1)} %copy-done.5, ...), custom_call_target="tpu_custom_call", output_to_operand_aliasing={{1}: (7, {})} | custom-call | flops 1000 | bytes 1000 | tf_op jit(solution)/shard_map/other/pallas_call | solution.py:280
  (1 shorter events, 0.0 us)
Async XLA Ops:
  1.3 0.8 copy-start.6
  2.1 0.7 copy-start.7
  3.9 27.9 %all-to-all-start = ((bf16[32,16,128]{2,1,0:T(8,128)(2,1)}), bf16[32,16,128]{2,1,0:T(8,128)(2,1)S(1)}, u32[]{:S(2)}, u32[]{:S(2)}) async-start(bf16[32,16,128]{2,1,0:T(8,128)(2,1)} %bitcast.5), calls=%async_computation | async-start | bytes 262144 | tf_op jit(solution)/shard_map/all_to_all | solution.py:211
  20.0 1.4 copy-start
  21.4 0.9 copy-start.2
  31.7 64.7 %all-to-all-start.1 = ((bf16[4,192,1536]{2,1,0:T(8,128)(2,1)}), bf16[4,192,1536]{2,1,0:T(8,128)(2,1)S(1)}, u32[]{:S(2)}, u32[]{:S(2)}) async-start(bf16[4,192,1536]{2,1,0:T(8,128)(2,1)} %pack.1), calls=%async_computation.1 | async-start | bytes 4718592 | tf_op jit(solution)/shard_map/all_to_all | solution.py:207
  91.8 6.0 %collective-permute-start = (bf16[4,512,128]{2,1,0:T(8,128)(2,1)S(1)}, bf16[4,512,128]{2,1,0:T(8,128)(2,1)S(1)}, u32[]{:S(2)}, u32[]{:S(2)}) collective-permute-start(bf16[4,512,128]{2,1,0:T(8,128)(2,1)S(1)} %all_gather.3.rows_ref.r0), channel_id=1, source_target_pairs={{0,1},{1,0},{2,3},{3,2},{4,5},{5,4},{6,7},{7,6},{8,9},{9,8},{10,11... | collective-permute-start | bytes 1572872 | tf_op jit(solution)/shard_map/ppermute | solution.py:215
  99.6 17.9 %all-to-all-start.2 = ((f32[32,1,128]{2,1,0:T(1,128)}), f32[32,1,128]{2,1,0:T(1,128)S(1)}, u32[]{:S(2)}, u32[]{:S(2)}) async-start(f32[32,1,128]{2,1,0:T(1,128)} %slots.1), calls=%async_computation.2 | async-start | bytes 32768 | tf_op jit(solution)/shard_map/all_to_all | solution.py:235
  106.6 33.9 %copy-start.1 = (bf16[1,192,4096]{2,1,0:T(8,128)(2,1)S(1)}, bf16[1,192,4096]{2,1,0:T(8,128)(2,1)}, u32[]{:S(2)}) copy-start(bf16[1,192,4096]{2,1,0:T(8,128)(2,1)} %param.9) | copy-start | bytes 4718596
  106.6 33.9 %copy-start.3 = (bf16[1,32,16,192]{3,2,1,0:T(8,128)(2,1)S(1)}, bf16[1,32,16,192]{3,2,1,0:T(8,128)(2,1)}, u32[]{:S(2)}) copy-start(bf16[1,32,16,192]{3,2,1,0:T(8,128)(2,1)} %param.8) | copy-start | bytes 589828
  106.6 23.1 %collective-permute-start.1 = (bf16[4,512,128]{2,1,0:T(8,128)(2,1)S(1)}, bf16[4,512,128]{2,1,0:T(8,128)(2,1)S(1)}, u32[]{:S(2)}, u32[]{:S(2)}) collective-permute-start(bf16[4,512,128]{2,1,0:T(8,128)(2,1)S(1)} %all_gather.3.rows_ref.r0), channel_id=1, source_target_pairs={{0,2},{1,3},{2,4},{3,5},{4,6},{5,7},{6,0},{7,1},{8,10},{9,11},{10,... | collective-permute-start | bytes 1572872 | tf_op jit(solution)/shard_map/ppermute | solution.py:252
  110.1 25.4 %collective-permute-start.2 = (bf16[4,512,128]{2,1,0:T(8,128)(2,1)S(1)}, bf16[4,512,128]{2,1,0:T(8,128)(2,1)}, u32[]{:S(2)}, u32[]{:S(2)}) collective-permute-start(bf16[4,512,128]{2,1,0:T(8,128)(2,1)S(1)} %all_gather.3.rows_ref.r0), channel_id=1, source_target_pairs={{0,4},{1,5},{2,6},{3,7},{4,0},{5,1},{6,2},{7,3},{8,12},{9,13},{10,... | collective-permute-start | bytes 1572872 | tf_op jit(solution)/shard_map/ppermute | solution.py:252
  114.4 24.2 %collective-permute-start.3 = (bf16[4,512,128]{2,1,0:T(8,128)(2,1)S(1)}, bf16[4,512,128]{2,1,0:T(8,128)(2,1)}, u32[]{:S(2)}, u32[]{:S(2)}) collective-permute-start(bf16[4,512,128]{2,1,0:T(8,128)(2,1)S(1)} %all_gather.3.rows_ref.r0), channel_id=1, source_target_pairs={{0,6},{1,7},{2,0},{3,1},{4,2},{5,3},{6,4},{7,5},{8,14},{9,15},{10,... | collective-permute-start | bytes 1572872 | tf_op jit(solution)/shard_map/ppermute | solution.py:252
  118.2 32.7 %all-to-all-start.3 = ((f32[32,1,64]{2,1,0:T(1,128)}), f32[32,1,64]{2,1,0:T(1,128)S(1)}, u32[]{:S(2)}, u32[]{:S(2)}) async-start(f32[32,1,64]{2,1,0:T(1,128)} %turn.1), calls=%async_computation.3 | async-start | bytes 32768 | tf_op jit(solution)/shard_map/all_to_all | solution.py:247
  129.8 22.0 %collective-permute-start.4 = (bf16[4,512,128]{2,1,0:T(8,128)(2,1)S(1)}, bf16[4,512,128]{2,1,0:T(8,128)(2,1)}, u32[]{:S(2)}, u32[]{:S(2)}) collective-permute-start(bf16[4,512,128]{2,1,0:T(8,128)(2,1)S(1)} %collective-permute-done.1.r1), channel_id=1, source_target_pairs={{0,1},{1,0},{2,3},{3,2},{4,5},{5,4},{6,7},{7,6},{8,9},{9,8},{10,11... | collective-permute-start | bytes 1572872 | tf_op jit(solution)/shard_map/ppermute | solution.py:260
  135.5 16.3 %collective-permute-start.5 = (bf16[4,512,128]{2,1,0:T(8,128)(2,1)}, bf16[4,512,128]{2,1,0:T(8,128)(2,1)}, u32[]{:S(2)}, u32[]{:S(2)}) collective-permute-start(bf16[4,512,128]{2,1,0:T(8,128)(2,1)} %collective-permute-done.2.r2), channel_id=1, source_target_pairs={{0,1},{1,0},{2,3},{3,2},{4,5},{5,4},{6,7},{7,6},{8,9},{9,8},{10,11... | collective-permute-start | bytes 1572872 | tf_op jit(solution)/shard_map/ppermute | solution.py:260
  138.6 13.2 %collective-permute-start.6 = (bf16[4,512,128]{2,1,0:T(8,128)(2,1)}, bf16[4,512,128]{2,1,0:T(8,128)(2,1)}, u32[]{:S(2)}, u32[]{:S(2)}) collective-permute-start(bf16[4,512,128]{2,1,0:T(8,128)(2,1)} %collective-permute-done.3.r3), channel_id=1, source_target_pairs={{0,1},{1,0},{2,3},{3,2},{4,5},{5,4},{6,7},{7,6},{8,9},{9,8},{10,11... | collective-permute-start | bytes 1572872 | tf_op jit(solution)/shard_map/ppermute | solution.py:260
  143.8 0.8 copy-start.4
  150.9 1.0 copy-start.5

commit v11 on v9

--- a/solution.py
+++ b/solution.py
@@ -123,7 +123,7 @@
     return product(w_ref, 0, 192, blocks), copies
 
 
-def own_kernel(at_ref, w_ref, saved_ref, r0, r1, r2, r3, o0, sums_ref, weight_ref, held, sems):
+def own_kernel(at_ref, w_ref, saved_ref, r3, r2, r1, r0, o0, sums_ref, weight_ref, held, sems):
     core = at_ref[1]
     parts = [(r0, 0, core), (o0, 0, 1 - core), (r1, 1, core), (r2, 2, core), (r3, 3, core)]
     sums_ref[...], copies = some_results(at_ref, w_ref, saved_ref, parts, weight_ref, held, sems)
@@ -261,7 +261,7 @@
         compiler_params=params,
         cost_estimate=small,
         name="own",
-    )(at, weight, saved, *own_rows, other)
+    )(at, weight, saved, *own_rows[::-1], other)
     from_z, sums, weight_part = lax.optimization_barrier((from_z, sums, weight_part))
     hidden_out, weight_out = pl.pallas_call(
         other_kernel,

time: 158 us -> 157 us (level)
  starting transfers between devices: 62.5 us -> 59.6 us
  waiting for transfers between devices: 16.7 us -> 19.3 us
    ppermute x3, waiting for transfers between devices: 2.29 us -> 11.3 us  [per_device(): lax.ppermute(going, 'replica', [(i, i // 8 * 8 + (i % 8 // 2 + k) % 4 * 2...]
    all_to_all x1, waiting for transfers between devices: 6.37 us -> 0.01 us  [per_device(): lax.all_to_all(to_z, BOTH, 0, 0, tiled=True, axis_index_groups=groups('hi...]
    ppermute x3, starting transfers between devices: 8.4 us -> 6.72 us  [per_device(): lax.ppermute(rows, 'replica', [(i, i ^ 1) for i in range(32)])]
  transfers between devices with their start and end apart: 11 -> 11, of which waited for: 4 -> 3; matrix products, arithmetic and copies ran while one was open for 0% -> 0% of each run, Pallas kernels for 5% -> 5%
where the time goes in v11:
time: 157 us; the launch traced here: 156 us
  starting transfers between devices  59.6 us (38%)
  blocking collectives  56 us (36%)
  waiting for transfers between devices  19.3 us (12%)
  Pallas kernels  14.4 us (9%)
  local copies, waits for them, and re-layouts  5.44 us (3%)
    all_gather x1, blocking collectives, per_device(): lax.all_gather(arrived, BOTH, axis=0, tiled=False, axis_index_groups=grou...  56 us
    all_to_all x1, starting transfers between devices, per_device(): lax.all_to_all(outgoing.reshape(experts, slot_count, -1), 'expert', 0, 0,...  16.1 us
    all_to_all x1, starting transfers between devices, per_device(): lax.all_to_all(to_z, BOTH, 0, 0, tiled=True, axis_index_groups=groups('hi...  11.6 us
    ppermute x3, waiting for transfers between devices, per_device(): lax.ppermute(going, 'replica', [(i, i // 8 * 8 + (i % 8 // 2 + k) % 4 * 2...  11.3 us
    ppermute x3, starting transfers between devices, per_device(): lax.ppermute(going, 'replica', [(i, i // 8 * 8 + (i % 8 // 2 + k) % 4 * 2...  9.61 us
    all_to_all x1, waiting for transfers between devices, per_device(): lax.all_to_all(outgoing.reshape(experts, slot_count, -1), 'expert', 0, 0,...  7.75 us
    all_to_all x1, starting transfers between devices, per_device(): lax.all_to_all(plane_sums, BOTH, 0, 0, tiled=True, axis_index_groups=grou...  7.04 us
    ppermute x3, starting transfers between devices, per_device(): lax.ppermute(rows, 'replica', [(i, i ^ 1) for i in range(32)])  6.72 us
  transfers between devices with their start and end apart: 11, of which 3 were waited for; matrix products, arithmetic and copies ran while one was open for 0% of the time, Pallas kernels for 5%

profile of v11, /device:TPU:1, one launch (start us, length us, event | category | flops | bytes accessed | tf_op | source)
XLA Modules:
  0.0 155.6 jit_solution(14068384832405584626)
XLA Ops:
  0.6 0.7 reshape.29.gate_ref
  1.3 0.0 copy-start.6
  1.3 0.8 copy-done.6
  2.1 0.0 copy-start.7
  2.1 0.7 copy-done.7
  2.8 1.0 place.1
  3.9 16.1 %all-to-all-start = ((bf16[32,16,128]{2,1,0:T(8,128)(2,1)}), bf16[32,16,128]{2,1,0:T(8,128)(2,1)S(1)}, u32[]{:S(2)}, u32[]{:S(2)}) async-start(bf16[32,16,128]{2,1,0:T(8,128)(2,1)} %bitcast.5), calls=%async_computation | async-start | bytes 262144 | tf_op jit(solution)/shard_map/all_to_all | solution.py:197
  20.0 0.0 copy-start
  20.0 1.4 copy-done
  21.4 0.0 copy-start.2
  21.4 0.9 copy-done.2
  22.3 1.7 %pack.1 = bf16[4,192,1536]{2,1,0:T(8,128)(2,1)} custom-call(bf16[192,4096]{1,0:T(8,128)(2,1)S(1)} %bitcast.11, bf16[512,192]{1,0:T(8,128)(2,1)S(1)} %bitcast.14), custom_call_target="tpu_custom_call" | custom-call | bytes 4194304 | tf_op jit(solution)/shard_map/pack/pallas_call | solution.py:184
  24.0 7.7 %all-to-all-done = bf16[32,16,128]{2,1,0:T(8,128)(2,1)S(1)} async-done(((bf16[32,16,128]{2,1,0:T(8,128)(2,1)}), bf16[32,16,128]{2,1,0:T(8,128)(2,1)S(1)}, u32[]{:S(2)}, u32[]{:S(2)}) %all-to-all-start) | async-done | bytes 131104 | tf_op jit(solution)/shard_map/all_to_all | solution.py:197
  31.7 4.0 %all-to-all-start.1 = ((bf16[4,192,1536]{2,1,0:T(8,128)(2,1)}), bf16[4,192,1536]{2,1,0:T(8,128)(2,1)S(1)}, u32[]{:S(2)}, u32[]{:S(2)}) async-start(bf16[4,192,1536]{2,1,0:T(8,128)(2,1)} %pack.1), calls=%async_computation.1 | async-start | bytes 4718592 | tf_op jit(solution)/shard_map/all_to_all | solution.py:193
  35.7 56.0 %all_gather.3.rows_ref.r0 = bf16[4,512,128]{2,1,0:T(8,128)(2,1)S(1)} all-gather(bf16[1,512,128]{2,1,0:T(8,128)(2,1)S(1)} %bitcast.21), channel_id=1, replica_groups={{0,8,16,24},{1,9,17,25},{2,10,18,26},{3,11,19,27},{4,12,20,28},{5,13,21..., dimensions={0}, use_global_device_ids=true | all-gather | bytes 655360 | tf_op jit(solution)/shard_map/all_gather | solution.py:200
  91.8 4.5 %collective-permute-start = (bf16[4,512,128]{2,1,0:T(8,128)(2,1)S(1)}, bf16[4,512,128]{2,1,0:T(8,128)(2,1)S(1)}, u32[]{:S(2)}, u32[]{:S(2)}) collective-permute-start(bf16[4,512,128]{2,1,0:T(8,128)(2,1)S(1)} %all_gather.3.rows_ref.r0), channel_id=1, source_target_pairs={{0,1},{1,0},{2,3},{3,2},{4,5},{5,4},{6,7},{7,6},{8,9},{9,8},{10,11... | collective-permute-start | bytes 1572872 | tf_op jit(solution)/shard_map/ppermute | solution.py:201
  96.3 0.1 pad_add_fusion.at_ref
  96.4 0.0 all-to-all-done.1
  96.4 1.2 own_slots.1.own_ref
  97.5 0.2 collective-permute-done.rows_ref.o0
  97.8 1.8 %slots.1 = f32[32,1,128]{2,1,0:T(1,128)} custom-call(s32[2]{0:T(128)S(1)} %pad_add_fusion.at_ref, bf16[4,512,128]{2,1,0:T(8,128)(2,1)S(1)} %collective-permute-done.rows_ref.o0, bf16[768,1536]{1,0:T(8,128)(2,1)S(1)} %bitcast.18, f32[1,512]{1,0:T(1,128)S(1)} %own_slots.1.own_ref), custom_call_target="tpu_custom_call" | custom-call | flops 805306368 | bytes 6291456 | tf_op jit(solution)/shard_map/slots/pallas_call | solution.py:212
  99.6 7.0 %all-to-all-start.2 = ((f32[32,1,128]{2,1,0:T(1,128)}), f32[32,1,128]{2,1,0:T(1,128)S(1)}, u32[]{:S(2)}, u32[]{:S(2)}) async-start(f32[32,1,128]{2,1,0:T(1,128)} %slots.1), calls=%async_computation.2 | async-start | bytes 32768 | tf_op jit(solution)/shard_map/all_to_all | solution.py:221
  106.6 0.0 copy-start.1
  106.6 0.0 copy-start.3
  106.6 4.6 %collective-permute-start.1 = (bf16[4,512,128]{2,1,0:T(8,128)(2,1)S(1)}, bf16[4,512,128]{2,1,0:T(8,128)(2,1)S(1)}, u32[]{:S(2)}, u32[]{:S(2)}) collective-permute-start(bf16[4,512,128]{2,1,0:T(8,128)(2,1)S(1)} %all_gather.3.rows_ref.r0), channel_id=1, source_target_pairs={{0,6},{1,7},{2,0},{3,1},{4,2},{5,3},{6,4},{7,5},{8,14},{9,15},{10,... | collective-permute-start | bytes 1572872 | tf_op jit(solution)/shard_map/ppermute | solution.py:238
  111.3 2.5 %collective-permute-start.2 = (bf16[4,512,128]{2,1,0:T(8,128)(2,1)S(1)}, bf16[4,512,128]{2,1,0:T(8,128)(2,1)}, u32[]{:S(2)}, u32[]{:S(2)}) collective-permute-start(bf16[4,512,128]{2,1,0:T(8,128)(2,1)S(1)} %all_gather.3.rows_ref.r0), channel_id=1, source_target_pairs={{0,4},{1,5},{2,6},{3,7},{4,0},{5,1},{6,2},{7,3},{8,12},{9,13},{10,... | collective-permute-start | bytes 1572872 | tf_op jit(solution)/shard_map/ppermute | solution.py:238
  113.8 2.5 %collective-permute-start.3 = (bf16[4,512,128]{2,1,0:T(8,128)(2,1)S(1)}, bf16[4,512,128]{2,1,0:T(8,128)(2,1)}, u32[]{:S(2)}, u32[]{:S(2)}) collective-permute-start(bf16[4,512,128]{2,1,0:T(8,128)(2,1)S(1)} %all_gather.3.rows_ref.r0), channel_id=1, source_target_pairs={{0,2},{1,3},{2,4},{3,5},{4,6},{5,7},{6,0},{7,1},{8,10},{9,11},{10,... | collective-permute-start | bytes 1572872 | tf_op jit(solution)/shard_map/ppermute | solution.py:238
  116.3 0.0 all-to-all-done.2.sums_ref
  116.3 0.7 turn.1
  117.0 11.6 %all-to-all-start.3 = ((f32[32,1,64]{2,1,0:T(1,128)}), f32[32,1,64]{2,1,0:T(1,128)S(1)}, u32[]{:S(2)}, u32[]{:S(2)}) async-start(f32[32,1,64]{2,1,0:T(1,128)} %turn.1), calls=%async_computation.3 | async-start | bytes 32768 | tf_op jit(solution)/shard_map/all_to_all | solution.py:233
  128.6 11.3 %collective-permute-done.3.r1 = bf16[4,512,128]{2,1,0:T(8,128)(2,1)} collective-permute-done((bf16[4,512,128]{2,1,0:T(8,128)(2,1)S(1)}, bf16[4,512,128]{2,1,0:T(8,128)(2,1)}, u32[]{:S(2)}, u32[]{:S(2)}) %collective-permute-start.3) | collective-permute-done | bytes 524320 | tf_op jit(solution)/shard_map/ppermute | solution.py:238
  139.9 2.4 %collective-permute-start.4 = (bf16[4,512,128]{2,1,0:T(8,128)(2,1)}, bf16[4,512,128]{2,1,0:T(8,128)(2,1)}, u32[]{:S(2)}, u32[]{:S(2)}) collective-permute-start(bf16[4,512,128]{2,1,0:T(8,128)(2,1)} %collective-permute-done.3.r1), channel_id=1, source_target_pairs={{0,1},{1,0},{2,3},{3,2},{4,5},{5,4},{6,7},{7,6},{8,9},{9,8},{10,11... | collective-permute-start | bytes 1572872 | tf_op jit(solution)/shard_map/ppermute | solution.py:246
  142.3 0.0 collective-permute-done.2.r2
  142.3 1.9 %collective-permute-start.5 = (bf16[4,512,128]{2,1,0:T(8,128)(2,1)}, bf16[4,512,128]{2,1,0:T(8,128)(2,1)}, u32[]{:S(2)}, u32[]{:S(2)}) collective-permute-start(bf16[4,512,128]{2,1,0:T(8,128)(2,1)} %collective-permute-done.2.r2), channel_id=1, source_target_pairs={{0,1},{1,0},{2,3},{3,2},{4,5},{5,4},{6,7},{7,6},{8,9},{9,8},{10,11... | collective-permute-start | bytes 1572872 | tf_op jit(solution)/shard_map/ppermute | solution.py:246
  144.2 0.0 collective-permute-done.1.r3
  144.2 2.4 %collective-permute-start.6 = (bf16[4,512,128]{2,1,0:T(8,128)(2,1)S(1)}, bf16[4,512,128]{2,1,0:T(8,128)(2,1)}, u32[]{:S(2)}, u32[]{:S(2)}) collective-permute-start(bf16[4,512,128]{2,1,0:T(8,128)(2,1)S(1)} %collective-permute-done.1.r3), channel_id=1, source_target_pairs={{0,1},{1,0},{2,3},{3,2},{4,5},{5,4},{6,7},{7,6},{8,9},{9,8},{10,11... | collective-permute-start | bytes 1572872 | tf_op jit(solution)/shard_map/ppermute | solution.py:246
  146.6 0.0 copy-done.1
  146.7 0.0 copy-done.3
  146.7 3.4 %own.1 = (f32[192,512]{1,0:T(8,128)S(1)}, bf16[192,4096]{1,0:T(8,128)(2,1)}) custom-call(s32[2]{0:T(128)S(1)} %pad_add_fusion.at_ref, bf16[192,4096]{1,0:T(8,128)(2,1)S(1)} %bitcast.12, bf16[512,192]{1,0:T(8,128)(2,1)S(1)} %bitcast.15, bf16[4,512,128]{2,1,0:T(8,128)(2,1)S(1)} %collective-permute-done.1.r3, bf16[4,512,128]{2,1,0:T(8,128)(2,1)} %collective-permute-done.2.r2, ...), custom_call_target="tpu_custom_call" | custom-call | flops 1000 | bytes 1000 | tf_op jit(solution)/shard_map/own/pallas_call | solution.py:250
  150.0 0.0 copy-start.4
  150.0 0.8 copy-done.4
  150.8 0.0 all-to-all-done.3.sums_ref
  150.8 0.8 gate.1
  151.6 0.0 collective-permute-done.4.o1
  151.6 0.0 collective-permute-done.5.o2
  151.7 0.0 collective-permute-done.6.o3
  151.7 0.1 copy-done.5
  151.8 3.8 %other.1 = (bf16[512,192]{1,0:T(8,128)(2,1)}, bf16[192,4096]{1,0:T(8,128)(2,1)}) custom-call(s32[2]{0:T(128)S(1)} %pad_add_fusion.at_ref, bf16[192,4096]{1,0:T(8,128)(2,1)S(1)} %bitcast.13, bf16[512,192]{1,0:T(8,128)(2,1)S(1)} %bitcast.16, f32[192,512]{1,0:T(8,128)S(1)} %copy-done.5, ...), custom_call_target="tpu_custom_call", output_to_operand_aliasing={{1}: (7, {})} | custom-call | flops 1000 | bytes 1000 | tf_op jit(solution)/shard_map/other/pallas_call | solution.py:266
  (1 shorter events, 0.0 us)
Async XLA Ops:
  1.3 0.8 copy-start.6
  2.1 0.7 copy-start.7
  3.9 27.9 %all-to-all-start = ((bf16[32,16,128]{2,1,0:T(8,128)(2,1)}), bf16[32,16,128]{2,1,0:T(8,128)(2,1)S(1)}, u32[]{:S(2)}, u32[]{:S(2)}) async-start(bf16[32,16,128]{2,1,0:T(8,128)(2,1)} %bitcast.5), calls=%async_computation | async-start | bytes 262144 | tf_op jit(solution)/shard_map/all_to_all | solution.py:197
  20.0 1.4 copy-start
  21.4 0.9 copy-start.2
  31.7 64.7 %all-to-all-start.1 = ((bf16[4,192,1536]{2,1,0:T(8,128)(2,1)}), bf16[4,192,1536]{2,1,0:T(8,128)(2,1)S(1)}, u32[]{:S(2)}, u32[]{:S(2)}) async-start(bf16[4,192,1536]{2,1,0:T(8,128)(2,1)} %pack.1), calls=%async_computation.1 | async-start | bytes 4718592 | tf_op jit(solution)/shard_map/all_to_all | solution.py:193
  91.8 6.0 %collective-permute-start = (bf16[4,512,128]{2,1,0:T(8,128)(2,1)S(1)}, bf16[4,512,128]{2,1,0:T(8,128)(2,1)S(1)}, u32[]{:S(2)}, u32[]{:S(2)}) collective-permute-start(bf16[4,512,128]{2,1,0:T(8,128)(2,1)S(1)} %all_gather.3.rows_ref.r0), channel_id=1, source_target_pairs={{0,1},{1,0},{2,3},{3,2},{4,5},{5,4},{6,7},{7,6},{8,9},{9,8},{10,11... | collective-permute-start | bytes 1572872 | tf_op jit(solution)/shard_map/ppermute | solution.py:201
  99.6 16.7 %all-to-all-start.2 = ((f32[32,1,128]{2,1,0:T(1,128)}), f32[32,1,128]{2,1,0:T(1,128)S(1)}, u32[]{:S(2)}, u32[]{:S(2)}) async-start(f32[32,1,128]{2,1,0:T(1,128)} %slots.1), calls=%async_computation.2 | async-start | bytes 32768 | tf_op jit(solution)/shard_map/all_to_all | solution.py:221
  106.6 40.0 %copy-start.1 = (bf16[1,192,4096]{2,1,0:T(8,128)(2,1)S(1)}, bf16[1,192,4096]{2,1,0:T(8,128)(2,1)}, u32[]{:S(2)}) copy-start(bf16[1,192,4096]{2,1,0:T(8,128)(2,1)} %param.9) | copy-start | bytes 4718596
  106.6 40.0 %copy-start.3 = (bf16[1,32,16,192]{3,2,1,0:T(8,128)(2,1)S(1)}, bf16[1,32,16,192]{3,2,1,0:T(8,128)(2,1)}, u32[]{:S(2)}) copy-start(bf16[1,32,16,192]{3,2,1,0:T(8,128)(2,1)} %param.8) | copy-start | bytes 589828
  106.6 37.6 %collective-permute-start.1 = (bf16[4,512,128]{2,1,0:T(8,128)(2,1)S(1)}, bf16[4,512,128]{2,1,0:T(8,128)(2,1)S(1)}, u32[]{:S(2)}, u32[]{:S(2)}) collective-permute-start(bf16[4,512,128]{2,1,0:T(8,128)(2,1)S(1)} %all_gather.3.rows_ref.r0), channel_id=1, source_target_pairs={{0,6},{1,7},{2,0},{3,1},{4,2},{5,3},{6,4},{7,5},{8,14},{9,15},{10,... | collective-permute-start | bytes 1572872 | tf_op jit(solution)/shard_map/ppermute | solution.py:238
  111.3 31.0 %collective-permute-start.2 = (bf16[4,512,128]{2,1,0:T(8,128)(2,1)S(1)}, bf16[4,512,128]{2,1,0:T(8,128)(2,1)}, u32[]{:S(2)}, u32[]{:S(2)}) collective-permute-start(bf16[4,512,128]{2,1,0:T(8,128)(2,1)S(1)} %all_gather.3.rows_ref.r0), channel_id=1, source_target_pairs={{0,4},{1,5},{2,6},{3,7},{4,0},{5,1},{6,2},{7,3},{8,12},{9,13},{10,... | collective-permute-start | bytes 1572872 | tf_op jit(solution)/shard_map/ppermute | solution.py:238
  113.8 26.1 %collective-permute-start.3 = (bf16[4,512,128]{2,1,0:T(8,128)(2,1)S(1)}, bf16[4,512,128]{2,1,0:T(8,128)(2,1)}, u32[]{:S(2)}, u32[]{:S(2)}) collective-permute-start(bf16[4,512,128]{2,1,0:T(8,128)(2,1)S(1)} %all_gather.3.rows_ref.r0), channel_id=1, source_target_pairs={{0,2},{1,3},{2,4},{3,5},{4,6},{5,7},{6,0},{7,1},{8,10},{9,11},{10,... | collective-permute-start | bytes 1572872 | tf_op jit(solution)/shard_map/ppermute | solution.py:238
  117.0 33.8 %all-to-all-start.3 = ((f32[32,1,64]{2,1,0:T(1,128)}), f32[32,1,64]{2,1,0:T(1,128)S(1)}, u32[]{:S(2)}, u32[]{:S(2)}) async-start(f32[32,1,64]{2,1,0:T(1,128)} %turn.1), calls=%async_computation.3 | async-start | bytes 32768 | tf_op jit(solution)/shard_map/all_to_all | solution.py:233
  139.9 11.8 %collective-permute-start.4 = (bf16[4,512,128]{2,1,0:T(8,128)(2,1)}, bf16[4,512,128]{2,1,0:T(8,128)(2,1)}, u32[]{:S(2)}, u32[]{:S(2)}) collective-permute-start(bf16[4,512,128]{2,1,0:T(8,128)(2,1)} %collective-permute-done.3.r1), channel_id=1, source_target_pairs={{0,1},{1,0},{2,3},{3,2},{4,5},{5,4},{6,7},{7,6},{8,9},{9,8},{10,11... | collective-permute-start | bytes 1572872 | tf_op jit(solution)/shard_map/ppermute | solution.py:246
  142.3 9.4 %collective-permute-start.5 = (bf16[4,512,128]{2,1,0:T(8,128)(2,1)}, bf16[4,512,128]{2,1,0:T(8,128)(2,1)}, u32[]{:S(2)}, u32[]{:S(2)}) collective-permute-start(bf16[4,512,128]{2,1,0:T(8,128)(2,1)} %collective-permute-done.2.r2), channel_id=1, source_target_pairs={{0,1},{1,0},{2,3},{3,2},{4,5},{5,4},{6,7},{7,6},{8,9},{9,8},{10,11... | collective-permute-start | bytes 1572872 | tf_op jit(solution)/shard_map/ppermute | solution.py:246
  144.2 7.4 %collective-permute-start.6 = (bf16[4,512,128]{2,1,0:T(8,128)(2,1)S(1)}, bf16[4,512,128]{2,1,0:T(8,128)(2,1)}, u32[]{:S(2)}, u32[]{:S(2)}) collective-permute-start(bf16[4,512,128]{2,1,0:T(8,128)(2,1)S(1)} %collective-permute-done.1.r3), channel_id=1, source_target_pairs={{0,1},{1,0},{2,3},{3,2},{4,5},{5,4},{6,7},{7,6},{8,9},{9,8},{10,11... | collective-permute-start | bytes 1572872 | tf_op jit(solution)/shard_map/ppermute | solution.py:246
  150.0 0.8 copy-start.4
  150.8 1.0 copy-start.5
